TPU v7x, 256 devices: a whole 4x4x8 slice. The times are simulated.
256 devices in a mesh: dp: 64 (over z, x_lo, y), mp: 4 (over x_hi, core).
Axes of the slice: x: 4 (x_hi: 2, x_lo: 2; x = x_hi * 2 + x_lo), y: 4, z: 8, core: 2. Of those that a mesh axis runs over, the one named last changes fastest.
Arguments:
- image_features: bfloat16 [10240, 1152], P('dp'), may hold values from -36 to 36
- text_features: bfloat16 [10240, 1152], P('dp'), may hold values from -36 to 36
- image_proj: bfloat16 [1152, 1152], P(None, 'mp'), may hold values from -0.75 to 0.75
- text_proj: bfloat16 [1152, 1152], P(None, 'mp'), may hold values from -0.75 to 0.75
- log_scale: float32 [1], replicated, may hold values from 4.3 to 4.7
- bias: float32 [1], replicated, may hold values from -11 to -9
Outputs:
- grad_image_features: float32 [10240, 1152], P('dp', 'mp')
- grad_text_features: float32 [10240, 1152], P('dp', 'mp')
- grad_image_proj: float32 [1152, 1152], P('dp', 'mp')
- grad_text_proj: float32 [1152, 1152], P('dp', 'mp')
All inputs are finite; a program needn't handle non-finite values.
Results may differ from a plain program's by a relative error of at most 0.0075.
Values may be sent and summed in bfloat16 or wider, within the bound.
No kernel may reach another device: no remote copies, remote signals or barrier semaphores. Data moves between devices by JAX's collectives and lax.ppermute only.
A program may use at most 128 MiB of HBM per device.

v0:
```python
import jax
import jax.numpy as jnp
from jax import lax
from jax.sharding import Mesh, PartitionSpec as P

AXES = ("z", "xl", "y", "xh", "c")
SIZES = (8, 2, 4, 2, 2)
DP = ("z", "xl", "y")
MP = ("xh", "c")
PLANE = ("xl", "y", "xh")
BF = jnp.bfloat16
F32 = jnp.float32


def a2a(x, axes):
    return lax.all_to_all(x, axes, 0, 0, tiled=True)


def swap_core(x):
    return lax.ppermute(x, "c", [(0, 1), (1, 0)])


def shift(x, axis, size, step):
    return lax.ppermute(x, axis, [(i, (i + step) % size) for i in range(size)])


def mp_shift(x, dx, dc):
    pairs = [(a * 2 + b, (a ^ dx) * 2 + (b ^ dc)) for a in range(2) for b in range(2)]
    return lax.ppermute(x, MP, pairs)


def rows_from_slices(pair, xh, c):
    quarters = pair.reshape(2, 2, 2, 40, 288)
    got = {}
    for dx in range(2):
        for dc in range(2):
            to = lax.dynamic_index_in_dim(quarters, xh ^ dx, 1, keepdims=False)
            to = lax.dynamic_index_in_dim(to, c ^ dc, 1, keepdims=False)
            got[dx, dc] = mp_shift(to, dx, dc) if dx or dc else to
    parts = []
    for a in range(2):
        for b in range(2):
            near = jnp.where(c == b, got[0, 0], got[0, 1])
            far = jnp.where(c == b, got[1, 0], got[1, 1])
            parts.append(jnp.where(xh == a, near, far))
    return jnp.concatenate(parts, axis=2)


def shards(image_features, text_features, image_proj, text_proj, log_scale, bias):
    xl, y, xh, c = (lax.axis_index(a) for a in AXES[1:])
    p_img = jnp.dot(image_features, image_proj, preferred_element_type=F32)
    p_txt = jnp.dot(text_features, text_proj, preferred_element_type=F32)
    own = rows_from_slices(jnp.stack([p_img, p_txt]), xh, c)
    r = lax.rsqrt(jnp.sum(own * own, axis=2, keepdims=True) + 1e-06)
    z = (own * r).astype(BF)
    z_img, z_txt = z[0], z[1]
    r_img, r_txt = r[0], r[1]

    img = jnp.broadcast_to(z_img[None], (16, 40, 1152))
    img, z_near = lax.optimization_barrier((img, z_txt))
    img = a2a(img, PLANE).reshape(640, 1152)
    up, down = [z_near], [z_near]
    for d in range(3):
        up.append(shift(up[-1], "z", 8, 1))
        down.append(shift(down[-1], "z", 8, -1))
    up.append(shift(up[-1], "z", 8, 1))
    txt_own = jnp.concatenate(up + down[:0:-1])

    stacked = jnp.concatenate(lax.optimization_barrier((image_features, text_features, down[2]))[:2])
    col = jnp.arange(576, dtype=jnp.int32)
    source = (col % 144) // 18 * 144 + col // 144 * 18 + col % 18

    def pick(half):
        chosen = jnp.arange(1152, dtype=jnp.int32)[:, None] == (source + 72 * half)[None, :]
        return jnp.dot(stacked, chosen.astype(BF), preferred_element_type=F32).astype(BF)

    keep = pick(xl)
    come = lax.ppermute(pick(1 - xl), "xl", [(0, 1), (1, 0)])
    keep, come, img = lax.optimization_barrier((keep, come, img))
    first, second = jnp.where(xl == 0, keep, come), jnp.where(xl == 0, come, keep)
    fi = jnp.concatenate([first[:160], second[:160]])
    ft = jnp.concatenate([first[160:], second[160:]])

    txt_oth = swap_core(txt_own)

    scale = jnp.exp(log_scale[0])
    offset = bias[0]
    place = (xl * 4 + y) * 2 + xh
    row_ids = jnp.arange(640, dtype=jnp.int32)[:, None] - place * 40
    col_ids = jnp.arange(320, dtype=jnp.int32)[None, :]
    diag = (row_ids == col_ids) & (row_ids >= 0) & (row_ids < 40)

    def coefs(txt, mask):
        d = jnp.einsum("re,ce->rc", img, txt, preferred_element_type=F32)
        logits = scale * d + offset
        if mask is None:
            return (scale * jax.nn.sigmoid(logits)).astype(BF)
        sign = jnp.where(mask, F32(1.0), F32(-1.0))
        return (-sign * jax.nn.sigmoid(-sign * logits) * scale).astype(BF)

    coef_oth = coefs(txt_oth, None)
    coef_own = coefs(txt_own, diag)
    t_oth = jnp.einsum("rc,re->ce", coef_oth, img, preferred_element_type=F32).astype(BF)
    t_got = swap_core(t_oth)
    t_own = jnp.einsum("rc,re->ce", coef_own, img, preferred_element_type=F32)
    t_sum = t_own + t_got.astype(F32)
    blocks = [t_sum[40 * d : 40 * d + 40] for d in range(8)]
    up, down = blocks[4], blocks[3]
    for d in range(1, 5):
        up = shift(up.astype(BF), "z", 8, 1).astype(F32) + blocks[(4 + d) % 8]
        if d < 3:
            down = shift(down.astype(BF), "z", 8, -1).astype(F32) + blocks[3 - d]
    gz_txt = up + shift(down.astype(BF), "z", 8, -1).astype(F32)
    g_img = (
        jnp.dot(coef_own, txt_own, preferred_element_type=F32)
        + jnp.dot(coef_oth, txt_oth, preferred_element_type=F32)
    ).astype(BF).reshape(16, 40, 1152)
    gz_img = jnp.sum(a2a(g_img, PLANE).astype(F32), axis=0)

    gz = jnp.stack([gz_img, gz_txt])
    values = z.astype(F32)
    inner = jnp.sum(values * gz, axis=2, keepdims=True)
    gp_rows = (r * (gz - values * inner)).astype(BF)
    cut = gp_rows.reshape(2, 40, 4, 288).transpose(2, 0, 1, 3)
    rest = jnp.concatenate([cut[:, 0, :, 256:], cut[:, 1, :, 256:], jnp.zeros((4, 40, 64), BF)], axis=2)
    piece = jnp.concatenate(
        [cut[:, :, :, :128].reshape(4, 80, 128), cut[:, :, :, 128:256].reshape(4, 80, 128), rest], axis=1
    )
    got = a2a(jnp.broadcast_to(piece[None], (2, 4, 200, 128)).reshape(8, 200, 128), ("xl", "xh", "c"))
    a_img, a_txt, b_img, b_txt, rest = (got[:, 40 * i : 40 * i + 40].reshape(320, 128) for i in range(5))

    def rows_dot(x, g):
        return jnp.einsum("rd,re->de", x, g, preferred_element_type=F32)

    lane = jnp.arange(128, dtype=jnp.int32)[None, :]
    rest_img = jnp.where(lane < 32, rest, jnp.zeros_like(rest))
    rest_txt = jnp.where(lane < 32, jnp.zeros_like(rest), rest)
    w = jnp.concatenate(
        [
            rows_dot(fi, jnp.concatenate([a_img, b_img], axis=1)),
            rows_dot(ft, jnp.concatenate([a_txt, b_txt], axis=1)),
            rows_dot(fi, rest_img) + rows_dot(ft, rest_txt),
        ],
        axis=1,
    ).reshape(4, 144, 640)
    up = lax.dynamic_index_in_dim(w, (y + 2) % 4, 0, keepdims=False).astype(BF)
    down = lax.dynamic_index_in_dim(w, (y + 3) % 4, 0, keepdims=False).astype(BF)
    up, got = lax.optimization_barrier((shift(up, "y", 4, 1), got))
    up = up.astype(F32) + lax.dynamic_index_in_dim(w, (y + 1) % 4, 0, keepdims=False)
    w = lax.dynamic_index_in_dim(w, y, 0, keepdims=False) + shift(down, "y", 4, -1).astype(F32)
    w = w + shift(up.astype(BF), "y", 4, 1).astype(F32)
    w = jnp.sum(a2a(w.astype(BF).reshape(8, 18, 640), ("z",)).astype(F32), axis=0)
    w_img = jnp.concatenate([w[:, :256], w[:, 512:544]], axis=1)
    w_txt = jnp.concatenate([w[:, 256:512], w[:, 544:576]], axis=1)

    mine = lax.dynamic_slice_in_dim(got, xl * 4, 4, 0)
    mine = [mine[:, 40 * i : 40 * i + 40].reshape(160, 128) for i in range(5)]
    gp_img = jnp.concatenate([mine[0], mine[2], mine[4][:, :32]], axis=1)
    gp_txt = jnp.concatenate([mine[1], mine[3], mine[4][:, 32:64]], axis=1)

    def feature_part(to):
        out = [
            jnp.einsum("re,de->rd", g, lax.dynamic_slice_in_dim(p, to * 288, 288, 0), preferred_element_type=F32)
            for g, p in ((gp_img, image_proj), (gp_txt, text_proj))
        ]
        return jnp.stack(out)

    f = feature_part(xh * 2 + c)
    for dx, dc in ((0, 1), (1, 0), (1, 1)):
        other = feature_part((xh ^ dx) * 2 + (c ^ dc)).astype(BF)
        f = f + mp_shift(other, dx, dc).astype(F32)
    return f[0], f[1], w_img, w_txt


def solution(mesh):
    fine = Mesh(mesh.devices.reshape(SIZES), AXES)
    in_specs = (P(DP, None), P(DP, None), P(None, MP), P(None, MP), P(), P())
    out_specs = (P(DP, MP), P(DP, MP), P(DP, MP), P(DP, MP))
    return jax.shard_map(shards, mesh=fine, in_specs=in_specs, out_specs=out_specs, check_vma=False)
```

profile of v0, /device:TPU:2, one launch (start us, length us, event | category | flops | bytes accessed | tf_op | source)
XLA Modules:
  0.0 167.0 jit_solution(12667338157587178156)
XLA Ops:
  0.7 1.7 %fusion.120 = f32[160,288]{1,0:T(8,128)S(1)} fusion(bf16[160,1152]{1,0:T(8,128)(2,1)} %param.6, bf16[1152,288]{0,1:T(8,128)(2,1)} %param.8), kind=kOutput, calls=%fused_computation.217 | convolution fusion | flops 106168320 | bytes 1216512 | tf_op jit(solution)/shard_map/dot_general | solution.py:51
  3.0 2.2 %collective-permute-start.1 = (f32[2,40,288]{2,1,0:T(8,128)S(1)}, f32[2,40,288]{2,1,0:T(8,128)S(1)}, u32[]{:S(2)}, u32[]{:S(2)}) collective-permute-start(f32[2,40,288]{2,1,0:T(8,128)S(1)} %get-tuple-element.41), channel_id=1, source_target_pairs={{0,2},{1,3},{2,0},{3,1},{4,6},{5,7},{6,4},{7,5},{8,10},{9,11},{10,... | collective-permute-start | bytes 276488 | tf_op jit(solution)/shard_map/ppermute | solution.py:29
  6.4 4.3 %collective-permute-done.1 = f32[2,40,288]{2,1,0:T(8,128)S(1)} collective-permute-done((f32[2,40,288]{2,1,0:T(8,128)S(1)}, f32[2,40,288]{2,1,0:T(8,128)S(1)}, u32[]{:S(2)}, u32[]{:S(2)}) %collective-permute-start.1) | collective-permute-done | bytes 92192 | tf_op jit(solution)/shard_map/ppermute | solution.py:29
  10.7 1.7 %collective-permute-done.2 = f32[2,40,288]{2,1,0:T(8,128)S(1)} collective-permute-done((f32[2,40,288]{2,1,0:T(8,128)S(1)}, f32[2,40,288]{2,1,0:T(8,128)S(1)}, u32[]{:S(2)}, u32[]{:S(2)}) %collective-permute-start.2) | collective-permute-done | bytes 92192 | tf_op jit(solution)/shard_map/ppermute | solution.py:29
  14.8 5.9 %collective-permute-start.3 = (bf16[40,1152]{1,0:T(8,128)(2,1)}, bf16[40,1152]{1,0:T(8,128)(2,1)}, u32[]{:S(2)}, u32[]{:S(2)}) collective-permute-start(bf16[40,1152]{1,0:T(8,128)(2,1)} %get-tuple-element.13), channel_id=1, source_target_pairs={{0,224},{32,0},{64,32},{96,64},{128,96},{160,128},{192,160},{224,1... | collective-permute-start | bytes 276488 | tf_op jit(solution)/shard_map/ppermute | solution.py:24
  22.3 7.6 %all-to-all-start = ((bf16[16,40,1152]{2,1,0:T(8,128)(2,1)}), bf16[16,40,1152]{2,1,0:T(8,128)(2,1)S(1)}, u32[]{:S(2)}, u32[]{:S(2)}) async-start(bf16[16,40,1152]{2,1,0:T(8,128)(2,1)} %broadcast_in_dim.47), calls=%async_computation | async-start | bytes 2949120 | tf_op jit(solution)/shard_map/all_to_all | solution.py:16
  29.9 3.3 %collective-permute-start.4 = (bf16[40,1152]{1,0:T(8,128)(2,1)}, bf16[40,1152]{1,0:T(8,128)(2,1)S(1)}, u32[]{:S(2)}, u32[]{:S(2)}) collective-permute-start(bf16[40,1152]{1,0:T(8,128)(2,1)} %collective-permute-done.3), channel_id=1, source_target_pairs={{0,224},{32,0},{64,32},{96,64},{128,96},{160,128},{192,160},{224,1... | collective-permute-start | bytes 276488 | tf_op jit(solution)/shard_map/ppermute | solution.py:24
  35.7 3.6 %collective-permute-start.10 = (bf16[40,1152]{1,0:T(8,128)(2,1)S(1)}, bf16[40,1152]{1,0:T(8,128)(2,1)S(1)}, u32[]{:S(2)}, u32[]{:S(2)}) collective-permute-start(bf16[40,1152]{1,0:T(8,128)(2,1)S(1)} %collective-permute-done.4), channel_id=1, source_target_pairs={{0,224},{32,0},{64,32},{96,64},{128,96},{160,128},{192,160},{224,1... | collective-permute-start | bytes 276488 | tf_op jit(solution)/shard_map/ppermute | solution.py:24
  39.9 5.1 %collective-permute-done.8 = bf16[40,1152]{1,0:T(8,128)(2,1)S(1)} collective-permute-done((bf16[40,1152]{1,0:T(8,128)(2,1)S(1)}, bf16[40,1152]{1,0:T(8,128)(2,1)S(1)}, u32[]{:S(2)}, u32[]{:S(2)}) %collective-permute-start.8) | collective-permute-done | bytes 92192 | tf_op jit(solution)/shard_map/ppermute | solution.py:24
  45.7 5.1 %collective-permute-done.9 = bf16[40,1152]{1,0:T(8,128)(2,1)S(1)} collective-permute-done((bf16[40,1152]{1,0:T(8,128)(2,1)S(1)}, bf16[40,1152]{1,0:T(8,128)(2,1)S(1)}, u32[]{:S(2)}, u32[]{:S(2)}) %collective-permute-start.9) | collective-permute-done | bytes 92192 | tf_op jit(solution)/shard_map/ppermute | solution.py:24
  57.4 2.8 %fusion.22 = bf16[320,576]{1,0:T(8,128)(2,1)} fusion(bf16[320,1152]{1,0:T(8,128)(2,1)} %copy-done.16, s32[576]{0:T(1024)S(1)} %broadcast_add_fusion.1), kind=kOutput, calls=%fused_computation.31 | convolution fusion | flops 425521152 | bytes 1108224 | tf_op jit(solution)/shard_map/dot_general | solution.py:75
  60.2 7.9 %collective-permute-done.5 = bf16[320,576]{1,0:T(8,128)(2,1)S(1)} collective-permute-done((bf16[320,576]{1,0:T(8,128)(2,1)}, bf16[320,576]{1,0:T(8,128)(2,1)S(1)}, u32[]{:S(2)}, u32[]{:S(2)}) %collective-permute-start.5) | collective-permute-done | bytes 368672 | tf_op jit(solution)/shard_map/ppermute | solution.py:78
  68.0 2.1 %fusion.19 = bf16[640,320]{0,1:T(8,128)(2,1)S(1)} fusion(bf16[640,1152]{1,0:T(8,128)(2,1)S(1)} %bitcast.103, bf16[320,1152]{1,0:T(8,128)(2,1)} %collective-permute-done.11, f32[]{:T(128)} %bitcast.102, f32[]{:T(128)} %bitcast.9), kind=kOutput, calls=%fused_computation.28 | convolution fusion | flops 473292800 | bytes 2621448 | tf_op jit(solution)/shard_map/re,ce->rc/dot_general | solution.py:94
  71.9 2.0 %fusion.20 = bf16[640,320]{0,1:T(8,128)(2,1)S(1)} fusion(bf16[640,1152]{1,0:T(8,128)(2,1)S(1)} %bitcast.105, bf16[320,1152]{1,0:T(8,128)(2,1)} %constant_dynamic-update-slice_fusion.2, f32[]{:T(128)} %bitcast.101, f32[]{:T(128)} %bitcast.9, s32[640]{0:T(1024)S(1)} %iota_subtract_fusion, pred[640]{0:T(1024)(128)(4,1)S(1)} %get-tuple-element.72, ...), kind=kOutput, calls=%fused_computation.29 | convolution fusion | flops 474726400 | bytes 2625288 | tf_op jit(solution)/shard_map/re,ce->rc/dot_general | solution.py:94
  74.4 2.0 %fusion.119 = (bf16[320,1152]{1,0:T(8,128)(2,1)S(1)}, f32[320,1152]{1,0:T(8,128)S(1)}) fusion(bf16[320,1152]{1,0:T(8,128)(2,1)} %collective-permute-done.12, bf16[640,320]{0,1:T(8,128)(2,1)S(1)} %fusion.20, bf16[640,1152]{1,0:T(8,128)(2,1)S(1)} %bitcast.106), kind=kOutput, calls=%fused_computation.216 | convolution fusion | flops 472965120 | bytes 4833280 | tf_op jit(solution)/shard_map/rc,re->ce/dot_general | solution.py:105
  76.5 2.7 %fusion.122 = f32[640,1152]{1,0:T(8,128)S(1)} fusion(bf16[640,320]{0,1:T(8,128)(2,1)S(1)} %copy-done.15, bf16[320,1152]{1,0:T(8,128)(2,1)} %collective-permute-done.11), kind=kOutput, calls=%fused_computation.219 | convolution fusion | flops 471859200 | bytes 4096000 | tf_op jit(solution)/shard_map/dot_general | solution.py:116
  79.2 2.7 %collective-permute-start.17 = (bf16[40,1152]{1,0:T(8,128)(2,1)S(1)}, bf16[40,1152]{1,0:T(8,128)(2,1)S(1)}, u32[]{:S(2)}, u32[]{:S(2)}) collective-permute-start(bf16[40,1152]{1,0:T(8,128)(2,1)S(1)} %get-tuple-element.33), channel_id=1, source_target_pairs={{0,224},{32,0},{64,32},{96,64},{128,96},{160,128},{192,160},{224,1... | collective-permute-start | bytes 276488 | tf_op jit(solution)/shard_map/ppermute | solution.py:24
  82.6 2.2 %fusion = bf16[640,1152]{1,0:T(8,128)(2,1)} fusion(f32[640,1152]{1,0:T(8,128)S(1)} %fusion.122, bf16[640,320]{0,1:T(8,128)(2,1)S(1)} %fusion.20, bf16[320,1152]{1,0:T(8,128)(2,1)S(1)} %copy-done.10), kind=kOutput, calls=%fused_computation.1 | convolution fusion | flops 473333760 | bytes 5570560 | tf_op jit(solution)/shard_map/dot_general | solution.py:115
  84.8 7.2 %all-to-all-start.1 = ((bf16[16,40,1152]{2,1,0:T(8,128)(2,1)}), bf16[16,40,1152]{2,1,0:T(8,128)(2,1)S(1)}, u32[]{:S(2)}, u32[]{:S(2)}) async-start(bf16[16,40,1152]{2,1,0:T(8,128)(2,1)} %bitcast.107), calls=%async_computation.1 | async-start | bytes 2949120 | tf_op jit(solution)/shard_map/all_to_all | solution.py:16
  93.1 3.3 %collective-permute-start.18 = (bf16[40,1152]{1,0:T(8,128)(2,1)S(1)}, bf16[40,1152]{1,0:T(8,128)(2,1)S(1)}, u32[]{:S(2)}, u32[]{:S(2)}) collective-permute-start(bf16[40,1152]{1,0:T(8,128)(2,1)S(1)} %get-tuple-element.29), channel_id=1, source_target_pairs={{0,224},{32,0},{64,32},{96,64},{128,96},{160,128},{192,160},{224,1... | collective-permute-start | bytes 276488 | tf_op jit(solution)/shard_map/ppermute | solution.py:24
  96.5 2.4 %collective-permute-done.15 = bf16[40,1152]{1,0:T(8,128)(2,1)S(1)} collective-permute-done((bf16[40,1152]{1,0:T(8,128)(2,1)S(1)}, bf16[40,1152]{1,0:T(8,128)(2,1)S(1)}, u32[]{:S(2)}, u32[]{:S(2)}) %collective-permute-start.15) | collective-permute-done | bytes 92192 | tf_op jit(solution)/shard_map/ppermute | solution.py:24
  99.9 3.4 %collective-permute-start.19 = (bf16[40,1152]{1,0:T(8,128)(2,1)S(1)}, bf16[40,1152]{1,0:T(8,128)(2,1)S(1)}, u32[]{:S(2)}, u32[]{:S(2)}) collective-permute-start(bf16[40,1152]{1,0:T(8,128)(2,1)S(1)} %get-tuple-element.27), channel_id=1, source_target_pairs={{0,224},{32,0},{64,32},{96,64},{128,96},{160,128},{192,160},{224,1... | collective-permute-start | bytes 276488 | tf_op jit(solution)/shard_map/ppermute | solution.py:24
  103.3 2.1 %collective-permute-done.19 = bf16[40,1152]{1,0:T(8,128)(2,1)S(1)} collective-permute-done((bf16[40,1152]{1,0:T(8,128)(2,1)S(1)}, bf16[40,1152]{1,0:T(8,128)(2,1)S(1)}, u32[]{:S(2)}, u32[]{:S(2)}) %collective-permute-start.19) | collective-permute-done | bytes 92192 | tf_op jit(solution)/shard_map/ppermute | solution.py:24
  105.4 3.6 %collective-permute-done.16 = bf16[40,1152]{1,0:T(8,128)(2,1)S(1)} collective-permute-done((bf16[40,1152]{1,0:T(8,128)(2,1)S(1)}, bf16[40,1152]{1,0:T(8,128)(2,1)S(1)}, u32[]{:S(2)}, u32[]{:S(2)}) %collective-permute-start.16) | collective-permute-done | bytes 92192 | tf_op jit(solution)/shard_map/ppermute | solution.py:24
  114.4 5.6 %all-to-all-start.2 = ((bf16[8,200,128]{2,1,0:T(8,128)(2,1)}), bf16[8,200,128]{2,1,0:T(8,128)(2,1)S(1)}, u32[]{:S(2)}, u32[]{:S(2)}) async-start(bf16[8,200,128]{2,1,0:T(8,128)(2,1)} %bitcast.23), calls=%async_computation.2 | async-start | bytes 819200 | tf_op jit(solution)/shard_map/all_to_all | solution.py:16
  120.2 6.9 %all-to-all-done.2 = bf16[8,200,128]{2,1,0:T(8,128)(2,1)S(1)} async-done(((bf16[8,200,128]{2,1,0:T(8,128)(2,1)}), bf16[8,200,128]{2,1,0:T(8,128)(2,1)S(1)}, u32[]{:S(2)}, u32[]{:S(2)}) %all-to-all-start.2) | async-done | bytes 409632 | tf_op jit(solution)/shard_map/all_to_all | solution.py:16
  129.5 3.2 %collective-permute-start.24 = (bf16[144,640]{1,0:T(8,128)(2,1)}, bf16[144,640]{1,0:T(8,128)(2,1)S(1)}, u32[]{:S(2)}, u32[]{:S(2)}) collective-permute-start(bf16[144,640]{1,0:T(8,128)(2,1)} %get-tuple-element.24), channel_id=1, source_target_pairs={{0,12},{4,0},{8,4},{12,8},{1,13},{5,1},{9,5},{13,9},{2,14},{6,2},{... | collective-permute-start | bytes 552968 | tf_op jit(solution)/shard_map/ppermute | solution.py:24
  132.7 4.2 %collective-permute-done.20 = bf16[144,640]{1,0:T(8,128)(2,1)S(1)} collective-permute-done((bf16[144,640]{1,0:T(8,128)(2,1)}, bf16[144,640]{1,0:T(8,128)(2,1)S(1)}, u32[]{:S(2)}, u32[]{:S(2)}) %collective-permute-start.20) | collective-permute-done | bytes 184352 | tf_op jit(solution)/shard_map/ppermute | solution.py:24
  140.9 1.7 %collective-permute-start.22 = (bf16[2,160,288]{2,1,0:T(8,128)(2,1)}, bf16[2,160,288]{2,1,0:T(8,128)(2,1)}, u32[]{:S(2)}, u32[]{:S(2)}) collective-permute-start(bf16[2,160,288]{2,1,0:T(8,128)(2,1)} %pad_maximum_fusion.8), channel_id=1, source_target_pairs={{0,2},{1,3},{2,0},{3,1},{4,6},{5,7},{6,4},{7,5},{8,10},{9,11},{10,... | collective-permute-start | bytes 552968 | tf_op jit(solution)/shard_map/ppermute | solution.py:29
  146.4 1.8 %collective-permute-done.25 = bf16[144,640]{1,0:T(8,128)(2,1)S(1)} collective-permute-done((bf16[144,640]{1,0:T(8,128)(2,1)S(1)}, bf16[144,640]{1,0:T(8,128)(2,1)S(1)}, u32[]{:S(2)}, u32[]{:S(2)}) %collective-permute-start.25) | collective-permute-done | bytes 184352 | tf_op jit(solution)/shard_map/ppermute | solution.py:24
  149.0 4.1 %all-to-all-start.3 = ((bf16[8,18,640]{2,1,0:T(8,128)(2,1)}), bf16[8,18,640]{2,1,0:T(8,128)(2,1)S(1)}, u32[]{:S(2)}, u32[]{:S(2)}) async-start(bf16[8,18,640]{2,1,0:T(8,128)(2,1)} %reshape.164), calls=%async_computation.3 | async-start | bytes 491520 | tf_op jit(solution)/shard_map/all_to_all | solution.py:16
  155.1 10.5 %all-to-all-done.3 = bf16[8,18,640]{2,1,0:T(8,128)(2,1)S(1)} async-done(((bf16[8,18,640]{2,1,0:T(8,128)(2,1)}), bf16[8,18,640]{2,1,0:T(8,128)(2,1)S(1)}, u32[]{:S(2)}, u32[]{:S(2)}) %all-to-all-start.3) | async-done | bytes 184352 | tf_op jit(solution)/shard_map/all_to_all | solution.py:16
  (149 shorter events, 39.5 us)
Async XLA Ops:
  2.9 3.5 %collective-permute-start = (f32[2,40,288]{2,1,0:T(8,128)S(1)}, f32[2,40,288]{2,1,0:T(8,128)S(1)}, u32[]{:S(2)}, u32[]{:S(2)}) collective-permute-start(f32[2,40,288]{2,1,0:T(8,128)S(1)} %get-tuple-element.40), channel_id=1, source_target_pairs={{0,1},{1,0},{2,3},{3,2},{4,5},{5,4},{6,7},{7,6},{8,9},{9,8},{10,11... | collective-permute-start | bytes 276488 | tf_op jit(solution)/shard_map/ppermute | solution.py:29
  3.0 7.7 %collective-permute-start.1 = (f32[2,40,288]{2,1,0:T(8,128)S(1)}, f32[2,40,288]{2,1,0:T(8,128)S(1)}, u32[]{:S(2)}, u32[]{:S(2)}) collective-permute-start(f32[2,40,288]{2,1,0:T(8,128)S(1)} %get-tuple-element.41), channel_id=1, source_target_pairs={{0,2},{1,3},{2,0},{3,1},{4,6},{5,7},{6,4},{7,5},{8,10},{9,11},{10,... | collective-permute-start | bytes 276488 | tf_op jit(solution)/shard_map/ppermute | solution.py:29
  5.2 7.2 %collective-permute-start.2 = (f32[2,40,288]{2,1,0:T(8,128)S(1)}, f32[2,40,288]{2,1,0:T(8,128)S(1)}, u32[]{:S(2)}, u32[]{:S(2)}) collective-permute-start(f32[2,40,288]{2,1,0:T(8,128)S(1)} %get-tuple-element.39), channel_id=1, source_target_pairs={{0,3},{1,2},{2,1},{3,0},{4,7},{5,6},{6,5},{7,4},{8,11},{9,10},{10,... | collective-permute-start | bytes 276488 | tf_op jit(solution)/shard_map/ppermute | solution.py:29
  14.8 15.1 %collective-permute-start.3 = (bf16[40,1152]{1,0:T(8,128)(2,1)}, bf16[40,1152]{1,0:T(8,128)(2,1)}, u32[]{:S(2)}, u32[]{:S(2)}) collective-permute-start(bf16[40,1152]{1,0:T(8,128)(2,1)} %get-tuple-element.13), channel_id=1, source_target_pairs={{0,224},{32,0},{64,32},{96,64},{128,96},{160,128},{192,160},{224,1... | collective-permute-start | bytes 276488 | tf_op jit(solution)/shard_map/ppermute | solution.py:24
  20.7 12.5 %collective-permute-start.6 = (bf16[40,1152]{1,0:T(8,128)(2,1)}, bf16[40,1152]{1,0:T(8,128)(2,1)}, u32[]{:S(2)}, u32[]{:S(2)}) collective-permute-start(bf16[40,1152]{1,0:T(8,128)(2,1)} %get-tuple-element.13), channel_id=1, source_target_pairs={{0,32},{32,64},{64,96},{96,128},{128,160},{160,192},{192,224},{224... | collective-permute-start | bytes 276488 | tf_op jit(solution)/shard_map/ppermute | solution.py:24
  22.3 13.4 %copy-start.2 = (bf16[160,1152]{1,0:T(8,128)(2,1)S(1)}, bf16[160,1152]{1,0:T(8,128)(2,1)}, u32[]{:S(2)}) copy-start(bf16[160,1152]{1,0:T(8,128)(2,1)} %param.6) | copy-start | bytes 1105924
  22.3 45.7 %all-to-all-start = ((bf16[16,40,1152]{2,1,0:T(8,128)(2,1)}), bf16[16,40,1152]{2,1,0:T(8,128)(2,1)S(1)}, u32[]{:S(2)}, u32[]{:S(2)}) async-start(bf16[16,40,1152]{2,1,0:T(8,128)(2,1)} %broadcast_in_dim.47), calls=%async_computation | async-start | bytes 2949120 | tf_op jit(solution)/shard_map/all_to_all | solution.py:16
  29.9 5.8 %collective-permute-start.4 = (bf16[40,1152]{1,0:T(8,128)(2,1)}, bf16[40,1152]{1,0:T(8,128)(2,1)S(1)}, u32[]{:S(2)}, u32[]{:S(2)}) collective-permute-start(bf16[40,1152]{1,0:T(8,128)(2,1)} %collective-permute-done.3), channel_id=1, source_target_pairs={{0,224},{32,0},{64,32},{96,64},{128,96},{160,128},{192,160},{224,1... | collective-permute-start | bytes 276488 | tf_op jit(solution)/shard_map/ppermute | solution.py:24
  33.2 6.1 %collective-permute-start.7 = (bf16[40,1152]{1,0:T(8,128)(2,1)}, bf16[40,1152]{1,0:T(8,128)(2,1)S(1)}, u32[]{:S(2)}, u32[]{:S(2)}) collective-permute-start(bf16[40,1152]{1,0:T(8,128)(2,1)} %collective-permute-done.6), channel_id=1, source_target_pairs={{0,32},{32,64},{64,96},{96,128},{128,160},{160,192},{192,224},{224... | collective-permute-start | bytes 276488 | tf_op jit(solution)/shard_map/ppermute | solution.py:24
  35.7 15.7 %collective-permute-start.10 = (bf16[40,1152]{1,0:T(8,128)(2,1)S(1)}, bf16[40,1152]{1,0:T(8,128)(2,1)S(1)}, u32[]{:S(2)}, u32[]{:S(2)}) collective-permute-start(bf16[40,1152]{1,0:T(8,128)(2,1)S(1)} %collective-permute-done.4), channel_id=1, source_target_pairs={{0,224},{32,0},{64,32},{96,64},{128,96},{160,128},{192,160},{224,1... | collective-permute-start | bytes 276488 | tf_op jit(solution)/shard_map/ppermute | solution.py:24
  39.3 5.8 %collective-permute-start.8 = (bf16[40,1152]{1,0:T(8,128)(2,1)S(1)}, bf16[40,1152]{1,0:T(8,128)(2,1)S(1)}, u32[]{:S(2)}, u32[]{:S(2)}) collective-permute-start(bf16[40,1152]{1,0:T(8,128)(2,1)S(1)} %collective-permute-done.7), channel_id=1, source_target_pairs={{0,32},{32,64},{64,96},{96,128},{128,160},{160,192},{192,224},{224... | collective-permute-start | bytes 276488 | tf_op jit(solution)/shard_map/ppermute | solution.py:24
  45.0 5.8 %collective-permute-start.9 = (bf16[40,1152]{1,0:T(8,128)(2,1)S(1)}, bf16[40,1152]{1,0:T(8,128)(2,1)S(1)}, u32[]{:S(2)}, u32[]{:S(2)}) collective-permute-start(bf16[40,1152]{1,0:T(8,128)(2,1)S(1)} %collective-permute-done.8), channel_id=1, source_target_pairs={{0,32},{32,64},{64,96},{96,128},{128,160},{160,192},{192,224},{224... | collective-permute-start | bytes 276488 | tf_op jit(solution)/shard_map/ppermute | solution.py:24
  54.3 13.8 %collective-permute-start.11 = (bf16[320,1152]{1,0:T(8,128)(2,1)}, bf16[320,1152]{1,0:T(8,128)(2,1)}, u32[]{:S(2)}, u32[]{:S(2)}) collective-permute-start(bf16[320,1152]{1,0:T(8,128)(2,1)} %constant_dynamic-update-slice_fusion.2), channel_id=1, source_target_pairs={{0,1},{1,0},{2,3},{3,2},{4,5},{5,4},{6,7},{7,6},{8,9},{9,8},{10,11... | collective-permute-start | bytes 2211848 | tf_op jit(solution)/shard_map/ppermute | solution.py:20
  55.9 12.1 %collective-permute-start.5 = (bf16[320,576]{1,0:T(8,128)(2,1)}, bf16[320,576]{1,0:T(8,128)(2,1)S(1)}, u32[]{:S(2)}, u32[]{:S(2)}) collective-permute-start(bf16[320,576]{1,0:T(8,128)(2,1)} %fusion.21), channel_id=1, source_target_pairs={{0,16},{16,0},{1,17},{17,1},{2,18},{18,2},{3,19},{19,3},{4,20},{20... | collective-permute-start | bytes 1105928 | tf_op jit(solution)/shard_map/ppermute | solution.py:78
  71.8 2.6 %collective-permute-start.12 = (bf16[320,1152]{1,0:T(8,128)(2,1)}, bf16[320,1152]{1,0:T(8,128)(2,1)}, u32[]{:S(2)}, u32[]{:S(2)}) collective-permute-start(bf16[320,1152]{1,0:T(8,128)(2,1)} %convolution_convert_fusion), channel_id=1, source_target_pairs={{0,1},{1,0},{2,3},{3,2},{4,5},{5,4},{6,7},{7,6},{8,9},{9,8},{10,11... | collective-permute-start | bytes 2211848 | tf_op jit(solution)/shard_map/ppermute | solution.py:20
  76.4 6.0 %collective-permute-start.13 = (bf16[40,1152]{1,0:T(8,128)(2,1)S(1)}, bf16[40,1152]{1,0:T(8,128)(2,1)S(1)}, u32[]{:S(2)}, u32[]{:S(2)}) collective-permute-start(bf16[40,1152]{1,0:T(8,128)(2,1)S(1)} %get-tuple-element.32), channel_id=1, source_target_pairs={{0,32},{32,64},{64,96},{96,128},{128,160},{160,192},{192,224},{224... | collective-permute-start | bytes 276488 | tf_op jit(solution)/shard_map/ppermute | solution.py:24
  79.2 12.7 %collective-permute-start.17 = (bf16[40,1152]{1,0:T(8,128)(2,1)S(1)}, bf16[40,1152]{1,0:T(8,128)(2,1)S(1)}, u32[]{:S(2)}, u32[]{:S(2)}) collective-permute-start(bf16[40,1152]{1,0:T(8,128)(2,1)S(1)} %get-tuple-element.33), channel_id=1, source_target_pairs={{0,224},{32,0},{64,32},{96,64},{128,96},{160,128},{192,160},{224,1... | collective-permute-start | bytes 276488 | tf_op jit(solution)/shard_map/ppermute | solution.py:24
  82.5 9.5 %collective-permute-start.14 = (bf16[40,1152]{1,0:T(8,128)(2,1)S(1)}, bf16[40,1152]{1,0:T(8,128)(2,1)S(1)}, u32[]{:S(2)}, u32[]{:S(2)}) collective-permute-start(bf16[40,1152]{1,0:T(8,128)(2,1)S(1)} %fusion.59), channel_id=1, source_target_pairs={{0,32},{32,64},{64,96},{96,128},{128,160},{160,192},{192,224},{224... | collective-permute-start | bytes 276488 | tf_op jit(solution)/shard_map/ppermute | solution.py:24
  84.8 27.4 %all-to-all-start.1 = ((bf16[16,40,1152]{2,1,0:T(8,128)(2,1)}), bf16[16,40,1152]{2,1,0:T(8,128)(2,1)S(1)}, u32[]{:S(2)}, u32[]{:S(2)}) async-start(bf16[16,40,1152]{2,1,0:T(8,128)(2,1)} %bitcast.107), calls=%async_computation.1 | async-start | bytes 2949120 | tf_op jit(solution)/shard_map/all_to_all | solution.py:16
  93.0 5.8 %collective-permute-start.15 = (bf16[40,1152]{1,0:T(8,128)(2,1)S(1)}, bf16[40,1152]{1,0:T(8,128)(2,1)S(1)}, u32[]{:S(2)}, u32[]{:S(2)}) collective-permute-start(bf16[40,1152]{1,0:T(8,128)(2,1)S(1)} %get-tuple-element.28), channel_id=1, source_target_pairs={{0,32},{32,64},{64,96},{96,128},{128,160},{160,192},{192,224},{224... | collective-permute-start | bytes 276488 | tf_op jit(solution)/shard_map/ppermute | solution.py:24
  93.1 5.8 %collective-permute-start.18 = (bf16[40,1152]{1,0:T(8,128)(2,1)S(1)}, bf16[40,1152]{1,0:T(8,128)(2,1)S(1)}, u32[]{:S(2)}, u32[]{:S(2)}) collective-permute-start(bf16[40,1152]{1,0:T(8,128)(2,1)S(1)} %get-tuple-element.29), channel_id=1, source_target_pairs={{0,224},{32,0},{64,32},{96,64},{128,96},{160,128},{192,160},{224,1... | collective-permute-start | bytes 276488 | tf_op jit(solution)/shard_map/ppermute | solution.py:24
  99.9 5.5 %collective-permute-start.19 = (bf16[40,1152]{1,0:T(8,128)(2,1)S(1)}, bf16[40,1152]{1,0:T(8,128)(2,1)S(1)}, u32[]{:S(2)}, u32[]{:S(2)}) collective-permute-start(bf16[40,1152]{1,0:T(8,128)(2,1)S(1)} %get-tuple-element.27), channel_id=1, source_target_pairs={{0,224},{32,0},{64,32},{96,64},{128,96},{160,128},{192,160},{224,1... | collective-permute-start | bytes 276488 | tf_op jit(solution)/shard_map/ppermute | solution.py:24
  103.3 5.8 %collective-permute-start.16 = (bf16[40,1152]{1,0:T(8,128)(2,1)S(1)}, bf16[40,1152]{1,0:T(8,128)(2,1)S(1)}, u32[]{:S(2)}, u32[]{:S(2)}) collective-permute-start(bf16[40,1152]{1,0:T(8,128)(2,1)S(1)} %get-tuple-element.26), channel_id=1, source_target_pairs={{0,32},{32,64},{64,96},{96,128},{128,160},{160,192},{192,224},{224... | collective-permute-start | bytes 276488 | tf_op jit(solution)/shard_map/ppermute | solution.py:24
  114.4 12.7 %all-to-all-start.2 = ((bf16[8,200,128]{2,1,0:T(8,128)(2,1)}), bf16[8,200,128]{2,1,0:T(8,128)(2,1)S(1)}, u32[]{:S(2)}, u32[]{:S(2)}) async-start(bf16[8,200,128]{2,1,0:T(8,128)(2,1)} %bitcast.23), calls=%async_computation.2 | async-start | bytes 819200 | tf_op jit(solution)/shard_map/all_to_all | solution.py:16
  128.7 9.0 %copy-start.4 = (bf16[1152,288]{0,1:T(8,128)(2,1)S(1)}, bf16[1152,288]{0,1:T(8,128)(2,1)}, u32[]{:S(2)}) copy-start(bf16[1152,288]{0,1:T(8,128)(2,1)} %param.8) | copy-start | bytes 1990660
  129.5 7.5 %collective-permute-start.20 = (bf16[144,640]{1,0:T(8,128)(2,1)}, bf16[144,640]{1,0:T(8,128)(2,1)S(1)}, u32[]{:S(2)}, u32[]{:S(2)}) collective-permute-start(bf16[144,640]{1,0:T(8,128)(2,1)} %get-tuple-element.25), channel_id=1, source_target_pairs={{0,4},{4,8},{8,12},{12,0},{1,5},{5,9},{9,13},{13,1},{2,6},{6,10},{... | collective-permute-start | bytes 552968 | tf_op jit(solution)/shard_map/ppermute | solution.py:24
  129.5 16.9 %collective-permute-start.24 = (bf16[144,640]{1,0:T(8,128)(2,1)}, bf16[144,640]{1,0:T(8,128)(2,1)S(1)}, u32[]{:S(2)}, u32[]{:S(2)}) collective-permute-start(bf16[144,640]{1,0:T(8,128)(2,1)} %get-tuple-element.24), channel_id=1, source_target_pairs={{0,12},{4,0},{8,4},{12,8},{1,13},{5,1},{9,5},{13,9},{2,14},{6,2},{... | collective-permute-start | bytes 552968 | tf_op jit(solution)/shard_map/ppermute | solution.py:24
  139.1 13.9 %collective-permute-start.23 = (bf16[2,160,288]{2,1,0:T(8,128)(2,1)}, bf16[2,160,288]{2,1,0:T(8,128)(2,1)S(1)}, u32[]{:S(2)}, u32[]{:S(2)}) collective-permute-start(bf16[2,160,288]{2,1,0:T(8,128)(2,1)} %pad_maximum_fusion.9), channel_id=1, source_target_pairs={{0,3},{1,2},{2,1},{3,0},{4,7},{5,6},{6,5},{7,4},{8,11},{9,10},{10,... | collective-permute-start | bytes 552968 | tf_op jit(solution)/shard_map/ppermute | solution.py:29
  140.1 8.0 %collective-permute-start.25 = (bf16[144,640]{1,0:T(8,128)(2,1)S(1)}, bf16[144,640]{1,0:T(8,128)(2,1)S(1)}, u32[]{:S(2)}, u32[]{:S(2)}) collective-permute-start(bf16[144,640]{1,0:T(8,128)(2,1)S(1)} %fusion.37), channel_id=1, source_target_pairs={{0,4},{4,8},{8,12},{12,0},{1,5},{5,9},{9,13},{13,1},{2,6},{6,10},{... | collective-permute-start | bytes 552968 | tf_op jit(solution)/shard_map/ppermute | solution.py:24
  140.9 12.2 %collective-permute-start.22 = (bf16[2,160,288]{2,1,0:T(8,128)(2,1)}, bf16[2,160,288]{2,1,0:T(8,128)(2,1)}, u32[]{:S(2)}, u32[]{:S(2)}) collective-permute-start(bf16[2,160,288]{2,1,0:T(8,128)(2,1)} %pad_maximum_fusion.8), channel_id=1, source_target_pairs={{0,2},{1,3},{2,0},{3,1},{4,6},{5,7},{6,4},{7,5},{8,10},{9,11},{10,... | collective-permute-start | bytes 552968 | tf_op jit(solution)/shard_map/ppermute | solution.py:29
  144.0 9.1 %collective-permute-start.21 = (bf16[2,160,288]{2,1,0:T(8,128)(2,1)}, bf16[2,160,288]{2,1,0:T(8,128)(2,1)}, u32[]{:S(2)}, u32[]{:S(2)}) collective-permute-start(bf16[2,160,288]{2,1,0:T(8,128)(2,1)} %pad_maximum_fusion.7), channel_id=1, source_target_pairs={{0,1},{1,0},{2,3},{3,2},{4,5},{5,4},{6,7},{7,6},{8,9},{9,8},{10,11... | collective-permute-start | bytes 552968 | tf_op jit(solution)/shard_map/ppermute | solution.py:29
  149.0 16.6 %all-to-all-start.3 = ((bf16[8,18,640]{2,1,0:T(8,128)(2,1)}), bf16[8,18,640]{2,1,0:T(8,128)(2,1)S(1)}, u32[]{:S(2)}, u32[]{:S(2)}) async-start(bf16[8,18,640]{2,1,0:T(8,128)(2,1)} %reshape.164), calls=%async_computation.3 | async-start | bytes 491520 | tf_op jit(solution)/shard_map/all_to_all | solution.py:16
  (16 other events, 47.8 us)
where the time goes:
time: 170 us; the launch traced here: 167 us
  waiting for transfers between devices  58.7 us (35%)
  starting transfers between devices  57.2 us (34%)
  matrix products  23.2 us (14%)
  local copies, waits for them, and re-layouts  15.4 us (9%)
  other arithmetic  10.1 us (6%)
  between operations  2.59 us (2%)
    ppermute x17, waiting for transfers between devices, shift(): return lax.ppermute(x, axis, [(i, (i + step) % size) for i in range(size)])  25.7 us
    ppermute x17, starting transfers between devices, shift(): return lax.ppermute(x, axis, [(i, (i + step) % size) for i in range(size)])  25.7 us
    all_to_all x4, starting transfers between devices, a2a(): return lax.all_to_all(x, axes, 0, 0, tiled=True)  24.6 us
    all_to_all x4, waiting for transfers between devices, a2a(): return lax.all_to_all(x, axes, 0, 0, tiled=True)  18.6 us
    ppermute x1, waiting for transfers between devices, shards(): come = lax.ppermute(pick(1 - xl), 'xl', [(0, 1), (1, 0)])  7.87 us
    unnamed x44, local copies, waits for them, and re-layouts  6.97 us
    ppermute x6, starting transfers between devices, mp_shift(): return lax.ppermute(x, MP, pairs)  6.83 us
    ppermute x6, waiting for transfers between devices, mp_shift(): return lax.ppermute(x, MP, pairs)  6.01 us
  transfers between devices with their start and end apart: 30, of which 16 were waited for; matrix products, arithmetic and copies ran while one was open for 19% of the time, Pallas kernels for 0%

commit v1 on v0

--- a/solution.py
+++ b/solution.py
@@ -1,6 +1,8 @@
 import jax
 import jax.numpy as jnp
 from jax import lax
+from jax.experimental import pallas as pl
+from jax.experimental.pallas import tpu as pltpu
 from jax.sharding import Mesh, PartitionSpec as P
 
 AXES = ("z", "xl", "y", "xh", "c")
@@ -46,13 +48,96 @@
     return jnp.concatenate(parts, axis=2)
 
 
+def block_kernel(scalars, place, img_in, *refs):
+    pieces, (t_oth, t_own, g_img, img, parts, texts, coef_t, img_sem, sems) = refs[:16], refs[16:]
+    scale, offset = scalars[0], scalars[1]
+    img_copy = pltpu.make_async_copy(img_in, img, img_sem)
+    copies = [pltpu.make_async_copy(pieces[d], parts.at[d], sems.at[d]) for d in range(16)]
+    for copy in copies:
+        copy.start()
+    img_copy.start()
+    for d in range(8):
+        copies[2 * d].wait()
+        copies[2 * d + 1].wait()
+        texts[80 * d : 80 * d + 80, :] = jnp.concatenate([parts[2 * d], parts[2 * d + 1]])
+    img_copy.wait()
+    first = place[0] * 40
+
+    def images(i, _):
+        at = pl.multiple_of(i * 128, 128)
+        block = img[pl.ds(at, 128), :]
+        dots = lax.dot_general(block, texts[...], (((1,), (1,)), ((), ())), preferred_element_type=F32)
+        rows = lax.broadcasted_iota(jnp.int32, (128, 640), 0) + at - first
+        cols = lax.broadcasted_iota(jnp.int32, (128, 640), 1) - 320
+        sign = jnp.where((rows == cols) & (cols >= 0) & (cols < 40), F32(1.0), F32(-1.0))
+        value = -sign * scale * jax.nn.sigmoid(-sign * (scale * dots + offset))
+        coef_t[:, pl.ds(at, 128)] = value.T.astype(BF)
+        value = value.astype(BF)
+        g_img[pl.ds(at, 128), :] = jnp.dot(value, texts[...], preferred_element_type=F32).astype(BF)
+        return 0
+
+    lax.fori_loop(0, 5, images, 0)
+
+    def others(j, _):
+        at = pl.multiple_of(j * 160, 32)
+        t_oth[pl.ds(at, 160), :] = jnp.dot(
+            coef_t[pl.ds(at, 160), :], img[...], preferred_element_type=F32
+        ).astype(BF)
+        return 0
+
+    lax.fori_loop(0, 2, others, 0)
+
+    def owns(j, _):
+        at = pl.multiple_of(j * 160, 32)
+        t_own[pl.ds(at, 160), :] = jnp.dot(coef_t[pl.ds(320 + at, 160), :], img[...], preferred_element_type=F32)
+        return 0
+
+    lax.fori_loop(0, 2, owns, 0)
+
+
+def block_grads(scalars, place, img, pieces):
+    small = pl.BlockSpec(memory_space=pltpu.SMEM)
+    large = pl.BlockSpec(memory_space=pl.ANY)
+    vmem = pl.BlockSpec(memory_space=pltpu.VMEM)
+    return pl.pallas_call(
+        block_kernel,
+        out_shape=[
+            jax.ShapeDtypeStruct((320, 1152), BF),
+            jax.ShapeDtypeStruct((320, 1152), F32),
+            jax.ShapeDtypeStruct((640, 1152), BF),
+        ],
+        in_specs=[small, small] + [large] * 17,
+        out_specs=[vmem] * 3,
+        scratch_shapes=[
+            pltpu.VMEM((640, 1152), BF),
+            pltpu.VMEM((16, 40, 1152), BF),
+            pltpu.VMEM((640, 1152), BF),
+            pltpu.VMEM((640, 640), BF),
+            pltpu.SemaphoreType.DMA,
+            pltpu.SemaphoreType.DMA((16,)),
+        ],
+        compiler_params=pltpu.CompilerParams(vmem_limit_bytes=24 * 2**20),
+        cost_estimate=pl.CostEstimate(flops=2900000000, bytes_accessed=8000000, transcendentals=400000),
+    )(scalars, place, img, *pieces)
+
+
 def shards(image_features, text_features, image_proj, text_proj, log_scale, bias):
     xl, y, xh, c = (lax.axis_index(a) for a in AXES[1:])
     p_img = jnp.dot(image_features, image_proj, preferred_element_type=F32)
     p_txt = jnp.dot(text_features, text_proj, preferred_element_type=F32)
+    stacked = jnp.concatenate(lax.optimization_barrier((image_features, text_features, p_img, p_txt))[:2])
+    col = jnp.arange(576, dtype=jnp.int32)
+    source = (col % 144) // 18 * 144 + col // 144 * 18 + col % 18
+
+    def pick(half):
+        chosen = jnp.arange(1152, dtype=jnp.int32)[:, None] == (source + 72 * half)[None, :]
+        return jnp.dot(stacked, chosen.astype(BF), preferred_element_type=F32).astype(BF)
+
+    keep, give = pick(xl), pick(1 - xl)
     own = rows_from_slices(jnp.stack([p_img, p_txt]), xh, c)
     r = lax.rsqrt(jnp.sum(own * own, axis=2, keepdims=True) + 1e-06)
     z = (own * r).astype(BF)
+    z, keep, give = lax.optimization_barrier((z, keep, give))
     z_img, z_txt = z[0], z[1]
     r_img, r_txt = r[0], r[1]
 
@@ -64,57 +149,24 @@
         up.append(shift(up[-1], "z", 8, 1))
         down.append(shift(down[-1], "z", 8, -1))
     up.append(shift(up[-1], "z", 8, 1))
-    txt_own = jnp.concatenate(up + down[:0:-1])
-
-    stacked = jnp.concatenate(lax.optimization_barrier((image_features, text_features, down[2]))[:2])
-    col = jnp.arange(576, dtype=jnp.int32)
-    source = (col % 144) // 18 * 144 + col // 144 * 18 + col % 18
-
-    def pick(half):
-        chosen = jnp.arange(1152, dtype=jnp.int32)[:, None] == (source + 72 * half)[None, :]
-        return jnp.dot(stacked, chosen.astype(BF), preferred_element_type=F32).astype(BF)
-
-    keep = pick(xl)
-    come = lax.ppermute(pick(1 - xl), "xl", [(0, 1), (1, 0)])
-    keep, come, img = lax.optimization_barrier((keep, come, img))
+    txt_own = up + down[:0:-1]
+    txt_oth = [swap_core(piece) for piece in txt_own]
+    give, img = lax.optimization_barrier((give, img))
+    come = lax.ppermute(give, "xl", [(0, 1), (1, 0)])
     first, second = jnp.where(xl == 0, keep, come), jnp.where(xl == 0, come, keep)
     fi = jnp.concatenate([first[:160], second[:160]])
     ft = jnp.concatenate([first[160:], second[160:]])
 
-    txt_oth = swap_core(txt_own)
-
-    scale = jnp.exp(log_scale[0])
-    offset = bias[0]
     place = (xl * 4 + y) * 2 + xh
-    row_ids = jnp.arange(640, dtype=jnp.int32)[:, None] - place * 40
-    col_ids = jnp.arange(320, dtype=jnp.int32)[None, :]
-    diag = (row_ids == col_ids) & (row_ids >= 0) & (row_ids < 40)
-
-    def coefs(txt, mask):
-        d = jnp.einsum("re,ce->rc", img, txt, preferred_element_type=F32)
-        logits = scale * d + offset
-        if mask is None:
-            return (scale * jax.nn.sigmoid(logits)).astype(BF)
-        sign = jnp.where(mask, F32(1.0), F32(-1.0))
-        return (-sign * jax.nn.sigmoid(-sign * logits) * scale).astype(BF)
-
-    coef_oth = coefs(txt_oth, None)
-    coef_own = coefs(txt_own, diag)
-    t_oth = jnp.einsum("rc,re->ce", coef_oth, img, preferred_element_type=F32).astype(BF)
+    scalars = jnp.concatenate([jnp.exp(log_scale), bias])
+    t_oth, t_own, g_img = block_grads(scalars, place.astype(jnp.int32).reshape(1), img, txt_oth + txt_own)
     t_got = swap_core(t_oth)
-    t_own = jnp.einsum("rc,re->ce", coef_own, img, preferred_element_type=F32)
     t_sum = t_own + t_got.astype(F32)
-    blocks = [t_sum[40 * d : 40 * d + 40] for d in range(8)]
-    up, down = blocks[4], blocks[3]
-    for d in range(1, 5):
-        up = shift(up.astype(BF), "z", 8, 1).astype(F32) + blocks[(4 + d) % 8]
-        if d < 3:
-            down = shift(down.astype(BF), "z", 8, -1).astype(F32) + blocks[3 - d]
-    gz_txt = up + shift(down.astype(BF), "z", 8, -1).astype(F32)
-    g_img = (
-        jnp.dot(coef_own, txt_own, preferred_element_type=F32)
-        + jnp.dot(coef_oth, txt_oth, preferred_element_type=F32)
-    ).astype(BF).reshape(16, 40, 1152)
+    t_out = t_sum[40:].astype(BF)
+    gz_txt = t_sum[:40]
+    for d in range(1, 8):
+        gz_txt = gz_txt + shift(t_out[40 * d - 40 : 40 * d], "z", 8, -d).astype(F32)
+    g_img = g_img.reshape(16, 40, 1152)
     gz_img = jnp.sum(a2a(g_img, PLANE).astype(F32), axis=0)
 
     gz = jnp.stack([gz_img, gz_txt])
@@ -145,8 +197,7 @@
     ).reshape(4, 144, 640)
     up = lax.dynamic_index_in_dim(w, (y + 2) % 4, 0, keepdims=False).astype(BF)
     down = lax.dynamic_index_in_dim(w, (y + 3) % 4, 0, keepdims=False).astype(BF)
-    up, got = lax.optimization_barrier((shift(up, "y", 4, 1), got))
-    up = up.astype(F32) + lax.dynamic_index_in_dim(w, (y + 1) % 4, 0, keepdims=False)
+    up = shift(up, "y", 4, 1).astype(F32) + lax.dynamic_index_in_dim(w, (y + 1) % 4, 0, keepdims=False)
     w = lax.dynamic_index_in_dim(w, y, 0, keepdims=False) + shift(down, "y", 4, -1).astype(F32)
     w = w + shift(up.astype(BF), "y", 4, 1).astype(F32)
     w = jnp.sum(a2a(w.astype(BF).reshape(8, 18, 640), ("z",)).astype(F32), axis=0)

time: 170 us -> 176 us (1.035)
  matrix products: 23.2 us -> 9.16 us
  Pallas kernels: 0 us -> 10.8 us
  starting transfers between devices: 57.2 us -> 64.4 us
  local copies, waits for them, and re-layouts: 15.4 us -> 22 us
  other arithmetic: 10.1 us -> 5.68 us
    dot_general x6 -> x0, matrix products: 12.7 us -> none  [the longest x2 4.16 us: coefs(): d = jnp.einsum('re,ce->rc', img, txt, preferred_element_type=F32)]
    pallas_call x0 -> x1, Pallas kernels: none -> 10.8 us  [block_grads(): pl.pallas_call(block_kernel, out_shape=[jax.ShapeDtypeStruct((320, 1152),...]
    unnamed x44 -> x59, local copies, waits for them, and re-layouts: 6.97 us -> 17.3 us
    ppermute x1, waiting for transfers between devices: 7.87 us -> 17.2 us  [shards(): come = lax.ppermute(give, 'xl', [(0, 1), (1, 0)])]
    ppermute x17, starting transfers between devices: 25.7 us -> 29.5 us  [shift(): return lax.ppermute(x, axis, [(i, (i + step) % size) for i in range(size)])]
    ppermute x6, waiting for transfers between devices: 6.01 us -> 2.67 us  [mp_shift(): return lax.ppermute(x, MP, pairs)]
    all_to_all x4, starting transfers between devices: 24.6 us -> 26.9 us  [a2a(): return lax.all_to_all(x, axes, 0, 0, tiled=True)]
    ppermute x2 -> x9, starting transfers between devices: 0.01 us -> 2.39 us  [swap_core(): return lax.ppermute(x, 'c', [(0, 1), (1, 0)])]
  transfers between devices with their start and end apart: 30 -> 37, of which waited for: 16 -> 14; matrix products, arithmetic and copies ran while one was open for 19% -> 6% of each run, Pallas kernels for 0% -> 0%
where the time goes in v1:
time: 176 us; the launch traced here: 174 us
  starting transfers between devices  64.4 us (37%)
  waiting for transfers between devices  59.6 us (34%)
  local copies, waits for them, and re-layouts  22 us (12%)
  Pallas kernels  10.8 us (6%)
  matrix products  9.16 us (5%)
  other arithmetic  5.68 us (3%)
  between operations  2.57 us (1%)
    ppermute x17, starting transfers between devices, shift(): return lax.ppermute(x, axis, [(i, (i + step) % size) for i in range(size)])  29.5 us
    all_to_all x4, starting transfers between devices, a2a(): return lax.all_to_all(x, axes, 0, 0, tiled=True)  26.9 us
    ppermute x17, waiting for transfers between devices, shift(): return lax.ppermute(x, axis, [(i, (i + step) % size) for i in range(size)])  23.4 us
    unnamed x59, local copies, waits for them, and re-layouts  17.3 us
    ppermute x1, waiting for transfers between devices, shards(): come = lax.ppermute(give, 'xl', [(0, 1), (1, 0)])  17.2 us
    all_to_all x4, waiting for transfers between devices, a2a(): return lax.all_to_all(x, axes, 0, 0, tiled=True)  16.3 us
    pallas_call x1, Pallas kernels, block_grads(): pl.pallas_call(block_kernel, out_shape=[jax.ShapeDtypeStruct((320, 1152),...  10.8 us
    ppermute x6, starting transfers between devices, mp_shift(): return lax.ppermute(x, MP, pairs)  5.38 us
  transfers between devices with their start and end apart: 37, of which 14 were waited for; matrix products, arithmetic and copies ran while one was open for 6% of the time, Pallas kernels for 0%

profile of v1, /device:TPU:2, one launch (start us, length us, event | category | flops | bytes accessed | tf_op | source)
XLA Modules:
  0.0 174.3 jit_solution(8843125632346169180)
XLA Ops:
  1.7 1.5 fusion.102
  3.8 2.2 %collective-permute-start.1 = (f32[2,40,288]{2,1,0:T(8,128)S(1)}, f32[2,40,288]{2,1,0:T(8,128)S(1)}, u32[]{:S(2)}, u32[]{:S(2)}) collective-permute-start(f32[2,40,288]{2,1,0:T(8,128)S(1)} %get-tuple-element.50), channel_id=1, source_target_pairs={{0,2},{1,3},{2,0},{3,1},{4,6},{5,7},{6,4},{7,5},{8,10},{9,11},{10,... | collective-permute-start | bytes 276488 | tf_op jit(solution)/shard_map/ppermute | solution.py:31
  7.3 1.6 fusion.10
  8.9 1.6 fusion.9
  11.5 1.7 collective-permute-done.2
  15.0 7.5 %all-to-all-start = ((bf16[16,40,1152]{2,1,0:T(8,128)(2,1)}), bf16[16,40,1152]{2,1,0:T(8,128)(2,1)S(1)}, u32[]{:S(2)}, u32[]{:S(2)}) async-start(bf16[16,40,1152]{2,1,0:T(8,128)(2,1)} %broadcast_in_dim.37), calls=%async_computation | async-start | bytes 2949120 | tf_op jit(solution)/shard_map/all_to_all | solution.py:18
  22.5 1.9 %collective-permute-start.4 = (bf16[40,1152]{1,0:T(8,128)(2,1)S(1)}, bf16[40,1152]{1,0:T(8,128)(2,1)S(1)}, u32[]{:S(2)}, u32[]{:S(2)}) collective-permute-start(bf16[40,1152]{1,0:T(8,128)(2,1)S(1)} %get-tuple-element.22.refs_8_), channel_id=1, source_target_pairs={{0,32},{32,64},{64,96},{96,128},{128,160},{160,192},{192,224},{224... | collective-permute-start | bytes 276488 | tf_op jit(solution)/shard_map/ppermute | solution.py:26
  24.4 4.0 %collective-permute-start.12 = (bf16[40,1152]{1,0:T(8,128)(2,1)S(1)}, bf16[40,1152]{1,0:T(8,128)(2,1)S(1)}, u32[]{:S(2)}, u32[]{:S(2)}) collective-permute-start(bf16[40,1152]{1,0:T(8,128)(2,1)S(1)} %get-tuple-element.22.refs_8_), channel_id=1, source_target_pairs={{0,224},{32,0},{64,32},{96,64},{128,96},{160,128},{192,160},{224,1... | collective-permute-start | bytes 276488 | tf_op jit(solution)/shard_map/ppermute | solution.py:26
  28.4 2.5 %collective-permute-done.4.refs_9_ = bf16[40,1152]{1,0:T(8,128)(2,1)S(1)} collective-permute-done((bf16[40,1152]{1,0:T(8,128)(2,1)S(1)}, bf16[40,1152]{1,0:T(8,128)(2,1)S(1)}, u32[]{:S(2)}, u32[]{:S(2)}) %collective-permute-start.4) | collective-permute-done | bytes 92192 | tf_op jit(solution)/shard_map/ppermute | solution.py:26
  30.9 3.3 %collective-permute-start.13 = (bf16[40,1152]{1,0:T(8,128)(2,1)S(1)}, bf16[40,1152]{1,0:T(8,128)(2,1)S(1)}, u32[]{:S(2)}, u32[]{:S(2)}) collective-permute-start(bf16[40,1152]{1,0:T(8,128)(2,1)S(1)} %collective-permute-done.12.refs_15_), channel_id=1, source_target_pairs={{0,224},{32,0},{64,32},{96,64},{128,96},{160,128},{192,160},{224,1... | collective-permute-start | bytes 276488 | tf_op jit(solution)/shard_map/ppermute | solution.py:26
  34.2 2.5 %collective-permute-done.6.refs_10_ = bf16[40,1152]{1,0:T(8,128)(2,1)S(1)} collective-permute-done((bf16[40,1152]{1,0:T(8,128)(2,1)S(1)}, bf16[40,1152]{1,0:T(8,128)(2,1)S(1)}, u32[]{:S(2)}, u32[]{:S(2)}) %collective-permute-start.6) | collective-permute-done | bytes 92192 | tf_op jit(solution)/shard_map/ppermute | solution.py:26
  37.2 3.2 %collective-permute-start.14 = (bf16[40,1152]{1,0:T(8,128)(2,1)S(1)}, bf16[40,1152]{1,0:T(8,128)(2,1)S(1)}, u32[]{:S(2)}, u32[]{:S(2)}) collective-permute-start(bf16[40,1152]{1,0:T(8,128)(2,1)S(1)} %collective-permute-done.13.refs_14_), channel_id=1, source_target_pairs={{0,224},{32,0},{64,32},{96,64},{128,96},{160,128},{192,160},{224,1... | collective-permute-start | bytes 276488 | tf_op jit(solution)/shard_map/ppermute | solution.py:26
  40.4 2.0 %collective-permute-done.8.refs_11_ = bf16[40,1152]{1,0:T(8,128)(2,1)S(1)} collective-permute-done((bf16[40,1152]{1,0:T(8,128)(2,1)S(1)}, bf16[40,1152]{1,0:T(8,128)(2,1)S(1)}, u32[]{:S(2)}, u32[]{:S(2)}) %collective-permute-start.8) | collective-permute-done | bytes 92192 | tf_op jit(solution)/shard_map/ppermute | solution.py:26
  62.6 10.8 %shard_map.93 = (bf16[320,1152]{1,0:T(8,128)(2,1)S(1)}, f32[320,1152]{1,0:T(8,128)S(1)}, bf16[640,1152]{1,0:T(8,128)(2,1)}) custom-call(f32[2]{0:T(128)S(1)} %pad_maximum_fusion.16.scalars, s32[1]{0:T(128)} %bitcast.8.place, bf16[640,1152]{1,0:T(8,128)(2,1)S(1)} %bitcast.88, bf16[40,1152]{1,0:T(8,128)(2,1)S(1)} %collective-permute-done.3.refs_0_, ...), custom_call_target="tpu_custom_call" | custom-call | flops 2900000000 | bytes 8000000 | tf_op jit(solution)/shard_map/pallas_call | solution.py:102
  74.1 7.4 %all-to-all-start.1 = ((bf16[16,40,1152]{2,1,0:T(8,128)(2,1)}), bf16[16,40,1152]{2,1,0:T(8,128)(2,1)}, u32[]{:S(2)}, u32[]{:S(2)}) async-start(bf16[16,40,1152]{2,1,0:T(8,128)(2,1)} %bitcast.12), calls=%async_computation.1 | async-start | bytes 2949120 | tf_op jit(solution)/shard_map/all_to_all | solution.py:18
  83.1 2.1 %collective-permute-start.19 = (bf16[40,1152]{1,0:T(8,128)(2,1)S(1)}, bf16[40,1152]{1,0:T(8,128)(2,1)S(1)}, u32[]{:S(2)}, u32[]{:S(2)}) collective-permute-start(bf16[40,1152]{1,0:T(8,128)(2,1)S(1)} %get-tuple-element.36), channel_id=1, source_target_pairs={{0,224},{32,0},{64,32},{96,64},{128,96},{160,128},{192,160},{224,1... | collective-permute-start | bytes 276488 | tf_op jit(solution)/shard_map/ppermute | solution.py:26
  85.6 4.3 %collective-permute-start.21 = (bf16[40,1152]{1,0:T(8,128)(2,1)S(1)}, bf16[40,1152]{1,0:T(8,128)(2,1)S(1)}, u32[]{:S(2)}, u32[]{:S(2)}) collective-permute-start(bf16[40,1152]{1,0:T(8,128)(2,1)S(1)} %get-tuple-element.41), channel_id=1, source_target_pairs={{0,160},{32,192},{64,224},{96,0},{128,32},{160,64},{192,96},{224,1... | collective-permute-start | bytes 276488 | tf_op jit(solution)/shard_map/ppermute | solution.py:26
  91.2 17.2 %collective-permute-done.29 = bf16[320,576]{1,0:T(8,128)(2,1)S(1)} collective-permute-done((bf16[320,576]{1,0:T(8,128)(2,1)S(1)}, bf16[320,576]{1,0:T(8,128)(2,1)S(1)}, u32[]{:S(2)}, u32[]{:S(2)}) %collective-permute-start.29) | collective-permute-done | bytes 368672 | tf_op jit(solution)/shard_map/ppermute | solution.py:155
  108.4 3.9 %collective-permute-start.23 = (bf16[40,1152]{1,0:T(8,128)(2,1)S(1)}, bf16[40,1152]{1,0:T(8,128)(2,1)S(1)}, u32[]{:S(2)}, u32[]{:S(2)}) collective-permute-start(bf16[40,1152]{1,0:T(8,128)(2,1)S(1)} %get-tuple-element.39), channel_id=1, source_target_pairs={{0,96},{32,128},{64,160},{96,192},{128,224},{160,0},{192,32},{224,... | collective-permute-start | bytes 276488 | tf_op jit(solution)/shard_map/ppermute | solution.py:26
  112.4 1.6 collective-permute-start.25
  114.1 6.4 %collective-permute-done.23 = bf16[40,1152]{1,0:T(8,128)(2,1)S(1)} collective-permute-done((bf16[40,1152]{1,0:T(8,128)(2,1)S(1)}, bf16[40,1152]{1,0:T(8,128)(2,1)S(1)}, u32[]{:S(2)}, u32[]{:S(2)}) %collective-permute-start.23) | collective-permute-done | bytes 92192 | tf_op jit(solution)/shard_map/ppermute | solution.py:26
  120.5 1.4 collective-permute-done.24
  121.9 1.5 collective-permute-done.25
  123.6 1.6 convert_reduce_fusion
  126.8 7.0 %all-to-all-start.2 = ((bf16[8,200,128]{2,1,0:T(8,128)(2,1)}), bf16[8,200,128]{2,1,0:T(8,128)(2,1)S(1)}, u32[]{:S(2)}, u32[]{:S(2)}) async-start(bf16[8,200,128]{2,1,0:T(8,128)(2,1)} %bitcast.20), calls=%async_computation.2 | async-start | bytes 819200 | tf_op jit(solution)/shard_map/all_to_all | solution.py:18
  133.8 7.0 %all-to-all-done.2 = bf16[8,200,128]{2,1,0:T(8,128)(2,1)S(1)} async-done(((bf16[8,200,128]{2,1,0:T(8,128)(2,1)}), bf16[8,200,128]{2,1,0:T(8,128)(2,1)S(1)}, u32[]{:S(2)}, u32[]{:S(2)}) %all-to-all-start.2) | async-done | bytes 409632 | tf_op jit(solution)/shard_map/all_to_all | solution.py:18
  142.5 3.2 %collective-permute-start.30 = (bf16[144,640]{1,0:T(8,128)(2,1)S(1)}, bf16[144,640]{1,0:T(8,128)(2,1)S(1)}, u32[]{:S(2)}, u32[]{:S(2)}) collective-permute-start(bf16[144,640]{1,0:T(8,128)(2,1)S(1)} %get-tuple-element.32), channel_id=1, source_target_pairs={{0,12},{4,0},{8,4},{12,8},{1,13},{5,1},{9,5},{13,9},{2,14},{6,2},{... | collective-permute-start | bytes 552968 | tf_op jit(solution)/shard_map/ppermute | solution.py:26
  147.3 2.4 %collective-permute-done.31 = bf16[144,640]{1,0:T(8,128)(2,1)S(1)} collective-permute-done((bf16[144,640]{1,0:T(8,128)(2,1)S(1)}, bf16[144,640]{1,0:T(8,128)(2,1)S(1)}, u32[]{:S(2)}, u32[]{:S(2)}) %collective-permute-start.31) | collective-permute-done | bytes 184352 | tf_op jit(solution)/shard_map/ppermute | solution.py:26
  149.9 1.7 collective-permute-start.27
  153.2 3.4 %collective-permute-done.32 = bf16[144,640]{1,0:T(8,128)(2,1)S(1)} collective-permute-done((bf16[144,640]{1,0:T(8,128)(2,1)S(1)}, bf16[144,640]{1,0:T(8,128)(2,1)S(1)}, u32[]{:S(2)}, u32[]{:S(2)}) %collective-permute-start.32) | collective-permute-done | bytes 184352 | tf_op jit(solution)/shard_map/ppermute | solution.py:26
  157.4 5.1 %all-to-all-start.3 = ((bf16[8,18,640]{2,1,0:T(8,128)(2,1)}), bf16[8,18,640]{2,1,0:T(8,128)(2,1)S(1)}, u32[]{:S(2)}, u32[]{:S(2)}) async-start(bf16[8,18,640]{2,1,0:T(8,128)(2,1)} %reshape.151), calls=%async_computation.3 | async-start | bytes 491520 | tf_op jit(solution)/shard_map/all_to_all | solution.py:18
  163.5 9.4 %all-to-all-done.3 = bf16[8,18,640]{2,1,0:T(8,128)(2,1)S(1)} async-done(((bf16[8,18,640]{2,1,0:T(8,128)(2,1)}), bf16[8,18,640]{2,1,0:T(8,128)(2,1)S(1)}, u32[]{:S(2)}, u32[]{:S(2)}) %all-to-all-start.3) | async-done | bytes 184352 | tf_op jit(solution)/shard_map/all_to_all | solution.py:18
  (166 shorter events, 38.8 us)
Async XLA Ops:
  3.7 6.8 %collective-permute-start = (f32[2,40,288]{2,1,0:T(8,128)S(1)}, f32[2,40,288]{2,1,0:T(8,128)S(1)}, u32[]{:S(2)}, u32[]{:S(2)}) collective-permute-start(f32[2,40,288]{2,1,0:T(8,128)S(1)} %get-tuple-element.49), channel_id=1, source_target_pairs={{0,1},{1,0},{2,3},{3,2},{4,5},{5,4},{6,7},{7,6},{8,9},{9,8},{10,11... | collective-permute-start | bytes 276488 | tf_op jit(solution)/shard_map/ppermute | solution.py:31
  3.8 7.7 %collective-permute-start.1 = (f32[2,40,288]{2,1,0:T(8,128)S(1)}, f32[2,40,288]{2,1,0:T(8,128)S(1)}, u32[]{:S(2)}, u32[]{:S(2)}) collective-permute-start(f32[2,40,288]{2,1,0:T(8,128)S(1)} %get-tuple-element.50), channel_id=1, source_target_pairs={{0,2},{1,3},{2,0},{3,1},{4,6},{5,7},{6,4},{7,5},{8,10},{9,11},{10,... | collective-permute-start | bytes 276488 | tf_op jit(solution)/shard_map/ppermute | solution.py:31
  6.0 7.2 %collective-permute-start.2 = (f32[2,40,288]{2,1,0:T(8,128)S(1)}, f32[2,40,288]{2,1,0:T(8,128)S(1)}, u32[]{:S(2)}, u32[]{:S(2)}) collective-permute-start(f32[2,40,288]{2,1,0:T(8,128)S(1)} %get-tuple-element.48), channel_id=1, source_target_pairs={{0,3},{1,2},{2,1},{3,0},{4,7},{5,6},{6,5},{7,4},{8,11},{9,10},{10,... | collective-permute-start | bytes 276488 | tf_op jit(solution)/shard_map/ppermute | solution.py:31
  15.0 33.9 %all-to-all-start = ((bf16[16,40,1152]{2,1,0:T(8,128)(2,1)}), bf16[16,40,1152]{2,1,0:T(8,128)(2,1)S(1)}, u32[]{:S(2)}, u32[]{:S(2)}) async-start(bf16[16,40,1152]{2,1,0:T(8,128)(2,1)} %broadcast_in_dim.37), calls=%async_computation | async-start | bytes 2949120 | tf_op jit(solution)/shard_map/all_to_all | solution.py:18
  22.5 8.4 %collective-permute-start.4 = (bf16[40,1152]{1,0:T(8,128)(2,1)S(1)}, bf16[40,1152]{1,0:T(8,128)(2,1)S(1)}, u32[]{:S(2)}, u32[]{:S(2)}) collective-permute-start(bf16[40,1152]{1,0:T(8,128)(2,1)S(1)} %get-tuple-element.22.refs_8_), channel_id=1, source_target_pairs={{0,32},{32,64},{64,96},{96,128},{128,160},{160,192},{192,224},{224... | collective-permute-start | bytes 276488 | tf_op jit(solution)/shard_map/ppermute | solution.py:26
  24.4 6.5 %collective-permute-start.12 = (bf16[40,1152]{1,0:T(8,128)(2,1)S(1)}, bf16[40,1152]{1,0:T(8,128)(2,1)S(1)}, u32[]{:S(2)}, u32[]{:S(2)}) collective-permute-start(bf16[40,1152]{1,0:T(8,128)(2,1)S(1)} %get-tuple-element.22.refs_8_), channel_id=1, source_target_pairs={{0,224},{32,0},{64,32},{96,64},{128,96},{160,128},{192,160},{224,1... | collective-permute-start | bytes 276488 | tf_op jit(solution)/shard_map/ppermute | solution.py:26
  30.9 6.3 %collective-permute-start.13 = (bf16[40,1152]{1,0:T(8,128)(2,1)S(1)}, bf16[40,1152]{1,0:T(8,128)(2,1)S(1)}, u32[]{:S(2)}, u32[]{:S(2)}) collective-permute-start(bf16[40,1152]{1,0:T(8,128)(2,1)S(1)} %collective-permute-done.12.refs_15_), channel_id=1, source_target_pairs={{0,224},{32,0},{64,32},{96,64},{128,96},{160,128},{192,160},{224,1... | collective-permute-start | bytes 276488 | tf_op jit(solution)/shard_map/ppermute | solution.py:26
  36.7 7.1 %collective-permute-start.3 = (bf16[40,1152]{1,0:T(8,128)(2,1)S(1)}, bf16[40,1152]{1,0:T(8,128)(2,1)S(1)}, u32[]{:S(2)}, u32[]{:S(2)}) collective-permute-start(bf16[40,1152]{1,0:T(8,128)(2,1)S(1)} %get-tuple-element.22.refs_8_), channel_id=1, source_target_pairs={{0,1},{1,0},{2,3},{3,2},{4,5},{5,4},{6,7},{7,6},{8,9},{9,8},{10,11... | collective-permute-start | bytes 276488 | tf_op jit(solution)/shard_map/ppermute | solution.py:22
  36.7 7.4 %collective-permute-start.17 = (bf16[40,1152]{1,0:T(8,128)(2,1)S(1)}, bf16[40,1152]{1,0:T(8,128)(2,1)S(1)}, u32[]{:S(2)}, u32[]{:S(2)}) collective-permute-start(bf16[40,1152]{1,0:T(8,128)(2,1)S(1)} %collective-permute-done.12.refs_15_), channel_id=1, source_target_pairs={{0,1},{1,0},{2,3},{3,2},{4,5},{5,4},{6,7},{7,6},{8,9},{9,8},{10,11... | collective-permute-start | bytes 276488 | tf_op jit(solution)/shard_map/ppermute | solution.py:22
  37.2 8.0 %collective-permute-start.5 = (bf16[40,1152]{1,0:T(8,128)(2,1)S(1)}, bf16[40,1152]{1,0:T(8,128)(2,1)S(1)}, u32[]{:S(2)}, u32[]{:S(2)}) collective-permute-start(bf16[40,1152]{1,0:T(8,128)(2,1)S(1)} %collective-permute-done.4.refs_9_), channel_id=1, source_target_pairs={{0,1},{1,0},{2,3},{3,2},{4,5},{5,4},{6,7},{7,6},{8,9},{9,8},{10,11... | collective-permute-start | bytes 276488 | tf_op jit(solution)/shard_map/ppermute | solution.py:22
  37.2 8.7 %collective-permute-start.14 = (bf16[40,1152]{1,0:T(8,128)(2,1)S(1)}, bf16[40,1152]{1,0:T(8,128)(2,1)S(1)}, u32[]{:S(2)}, u32[]{:S(2)}) collective-permute-start(bf16[40,1152]{1,0:T(8,128)(2,1)S(1)} %collective-permute-done.13.refs_14_), channel_id=1, source_target_pairs={{0,224},{32,0},{64,32},{96,64},{128,96},{160,128},{192,160},{224,1... | collective-permute-start | bytes 276488 | tf_op jit(solution)/shard_map/ppermute | solution.py:26
  43.8 6.3 %collective-permute-start.16 = (bf16[40,1152]{1,0:T(8,128)(2,1)S(1)}, bf16[40,1152]{1,0:T(8,128)(2,1)S(1)}, u32[]{:S(2)}, u32[]{:S(2)}) collective-permute-start(bf16[40,1152]{1,0:T(8,128)(2,1)S(1)} %collective-permute-done.13.refs_14_), channel_id=1, source_target_pairs={{0,1},{1,0},{2,3},{3,2},{4,5},{5,4},{6,7},{7,6},{8,9},{9,8},{10,11... | collective-permute-start | bytes 276488 | tf_op jit(solution)/shard_map/ppermute | solution.py:22
  44.7 6.0 %collective-permute-start.7 = (bf16[40,1152]{1,0:T(8,128)(2,1)S(1)}, bf16[40,1152]{1,0:T(8,128)(2,1)S(1)}, u32[]{:S(2)}, u32[]{:S(2)}) collective-permute-start(bf16[40,1152]{1,0:T(8,128)(2,1)S(1)} %collective-permute-done.6.refs_10_), channel_id=1, source_target_pairs={{0,1},{1,0},{2,3},{3,2},{4,5},{5,4},{6,7},{7,6},{8,9},{9,8},{10,11... | collective-permute-start | bytes 276488 | tf_op jit(solution)/shard_map/ppermute | solution.py:22
  45.9 6.1 %collective-permute-start.9 = (bf16[40,1152]{1,0:T(8,128)(2,1)S(1)}, bf16[40,1152]{1,0:T(8,128)(2,1)S(1)}, u32[]{:S(2)}, u32[]{:S(2)}) collective-permute-start(bf16[40,1152]{1,0:T(8,128)(2,1)S(1)} %collective-permute-done.8.refs_11_), channel_id=1, source_target_pairs={{0,1},{1,0},{2,3},{3,2},{4,5},{5,4},{6,7},{7,6},{8,9},{9,8},{10,11... | collective-permute-start | bytes 276488 | tf_op jit(solution)/shard_map/ppermute | solution.py:22
  73.4 8.3 %collective-permute-start.18 = (bf16[320,1152]{1,0:T(8,128)(2,1)S(1)}, bf16[320,1152]{1,0:T(8,128)(2,1)}, u32[]{:S(2)}, u32[]{:S(2)}) collective-permute-start(bf16[320,1152]{1,0:T(8,128)(2,1)S(1)} %get-tuple-element.25), channel_id=1, source_target_pairs={{0,1},{1,0},{2,3},{3,2},{4,5},{5,4},{6,7},{7,6},{8,9},{9,8},{10,11... | collective-permute-start | bytes 2211848 | tf_op jit(solution)/shard_map/ppermute | solution.py:22
  74.1 49.5 %all-to-all-start.1 = ((bf16[16,40,1152]{2,1,0:T(8,128)(2,1)}), bf16[16,40,1152]{2,1,0:T(8,128)(2,1)}, u32[]{:S(2)}, u32[]{:S(2)}) async-start(bf16[16,40,1152]{2,1,0:T(8,128)(2,1)} %bitcast.12), calls=%async_computation.1 | async-start | bytes 2949120 | tf_op jit(solution)/shard_map/all_to_all | solution.py:18
  81.4 27.0 %collective-permute-start.29 = (bf16[320,576]{1,0:T(8,128)(2,1)S(1)}, bf16[320,576]{1,0:T(8,128)(2,1)S(1)}, u32[]{:S(2)}, u32[]{:S(2)}) collective-permute-start(bf16[320,576]{1,0:T(8,128)(2,1)S(1)} %copy-done.28), channel_id=1, source_target_pairs={{0,16},{16,0},{1,17},{17,1},{2,18},{18,2},{3,19},{19,3},{4,20},{20... | collective-permute-start | bytes 1105928 | tf_op jit(solution)/shard_map/ppermute | solution.py:155
  83.1 29.3 %collective-permute-start.19 = (bf16[40,1152]{1,0:T(8,128)(2,1)S(1)}, bf16[40,1152]{1,0:T(8,128)(2,1)S(1)}, u32[]{:S(2)}, u32[]{:S(2)}) collective-permute-start(bf16[40,1152]{1,0:T(8,128)(2,1)S(1)} %get-tuple-element.36), channel_id=1, source_target_pairs={{0,224},{32,0},{64,32},{96,64},{128,96},{160,128},{192,160},{224,1... | collective-permute-start | bytes 276488 | tf_op jit(solution)/shard_map/ppermute | solution.py:26
  85.2 27.2 %collective-permute-start.20 = (bf16[40,1152]{1,0:T(8,128)(2,1)S(1)}, bf16[40,1152]{1,0:T(8,128)(2,1)S(1)}, u32[]{:S(2)}, u32[]{:S(2)}) collective-permute-start(bf16[40,1152]{1,0:T(8,128)(2,1)S(1)} %get-tuple-element.42), channel_id=1, source_target_pairs={{0,192},{32,224},{64,0},{96,32},{128,64},{160,96},{192,128},{224,1... | collective-permute-start | bytes 276488 | tf_op jit(solution)/shard_map/ppermute | solution.py:26
  85.6 28.5 %collective-permute-start.21 = (bf16[40,1152]{1,0:T(8,128)(2,1)S(1)}, bf16[40,1152]{1,0:T(8,128)(2,1)S(1)}, u32[]{:S(2)}, u32[]{:S(2)}) collective-permute-start(bf16[40,1152]{1,0:T(8,128)(2,1)S(1)} %get-tuple-element.41), channel_id=1, source_target_pairs={{0,160},{32,192},{64,224},{96,0},{128,32},{160,64},{192,96},{224,1... | collective-permute-start | bytes 276488 | tf_op jit(solution)/shard_map/ppermute | solution.py:26
  89.8 24.2 %collective-permute-start.22 = (bf16[40,1152]{1,0:T(8,128)(2,1)S(1)}, bf16[40,1152]{1,0:T(8,128)(2,1)S(1)}, u32[]{:S(2)}, u32[]{:S(2)}) collective-permute-start(bf16[40,1152]{1,0:T(8,128)(2,1)S(1)} %get-tuple-element.40), channel_id=1, source_target_pairs={{0,128},{32,160},{64,192},{96,224},{128,0},{160,32},{192,64},{224,... | collective-permute-start | bytes 276488 | tf_op jit(solution)/shard_map/ppermute | solution.py:26
  108.4 12.0 %collective-permute-start.23 = (bf16[40,1152]{1,0:T(8,128)(2,1)S(1)}, bf16[40,1152]{1,0:T(8,128)(2,1)S(1)}, u32[]{:S(2)}, u32[]{:S(2)}) collective-permute-start(bf16[40,1152]{1,0:T(8,128)(2,1)S(1)} %get-tuple-element.39), channel_id=1, source_target_pairs={{0,96},{32,128},{64,160},{96,192},{128,224},{160,0},{192,32},{224,... | collective-permute-start | bytes 276488 | tf_op jit(solution)/shard_map/ppermute | solution.py:26
  112.4 9.6 %collective-permute-start.24 = (bf16[40,1152]{1,0:T(8,128)(2,1)S(1)}, bf16[40,1152]{1,0:T(8,128)(2,1)S(1)}, u32[]{:S(2)}, u32[]{:S(2)}) collective-permute-start(bf16[40,1152]{1,0:T(8,128)(2,1)S(1)} %get-tuple-element.38), channel_id=1, source_target_pairs={{0,64},{32,96},{64,128},{96,160},{128,192},{160,224},{192,0},{224,... | collective-permute-start | bytes 276488 | tf_op jit(solution)/shard_map/ppermute | solution.py:26
  112.4 11.1 %collective-permute-start.25 = (bf16[40,1152]{1,0:T(8,128)(2,1)S(1)}, bf16[40,1152]{1,0:T(8,128)(2,1)S(1)}, u32[]{:S(2)}, u32[]{:S(2)}) collective-permute-start(bf16[40,1152]{1,0:T(8,128)(2,1)S(1)} %get-tuple-element.37), channel_id=1, source_target_pairs={{0,32},{32,64},{64,96},{96,128},{128,160},{160,192},{192,224},{224... | collective-permute-start | bytes 276488 | tf_op jit(solution)/shard_map/ppermute | solution.py:26
  126.8 14.0 %all-to-all-start.2 = ((bf16[8,200,128]{2,1,0:T(8,128)(2,1)}), bf16[8,200,128]{2,1,0:T(8,128)(2,1)S(1)}, u32[]{:S(2)}, u32[]{:S(2)}) async-start(bf16[8,200,128]{2,1,0:T(8,128)(2,1)} %bitcast.20), calls=%async_computation.2 | async-start | bytes 819200 | tf_op jit(solution)/shard_map/all_to_all | solution.py:18
  142.4 7.3 %collective-permute-start.31 = (bf16[144,640]{1,0:T(8,128)(2,1)S(1)}, bf16[144,640]{1,0:T(8,128)(2,1)S(1)}, u32[]{:S(2)}, u32[]{:S(2)}) collective-permute-start(bf16[144,640]{1,0:T(8,128)(2,1)S(1)} %get-tuple-element.33), channel_id=1, source_target_pairs={{0,4},{4,8},{8,12},{12,0},{1,5},{5,9},{9,13},{13,1},{2,6},{6,10},{... | collective-permute-start | bytes 552968 | tf_op jit(solution)/shard_map/ppermute | solution.py:26
  142.5 10.6 %collective-permute-start.30 = (bf16[144,640]{1,0:T(8,128)(2,1)S(1)}, bf16[144,640]{1,0:T(8,128)(2,1)S(1)}, u32[]{:S(2)}, u32[]{:S(2)}) collective-permute-start(bf16[144,640]{1,0:T(8,128)(2,1)S(1)} %get-tuple-element.32), channel_id=1, source_target_pairs={{0,12},{4,0},{8,4},{12,8},{1,13},{5,1},{9,5},{13,9},{2,14},{6,2},{... | collective-permute-start | bytes 552968 | tf_op jit(solution)/shard_map/ppermute | solution.py:26
  146.6 16.0 %collective-permute-start.26 = (bf16[2,160,288]{2,1,0:T(8,128)(2,1)S(1)}, bf16[2,160,288]{2,1,0:T(8,128)(2,1)S(1)}, u32[]{:S(2)}, u32[]{:S(2)}) collective-permute-start(bf16[2,160,288]{2,1,0:T(8,128)(2,1)S(1)} %pad_maximum_fusion.9), channel_id=1, source_target_pairs={{0,1},{1,0},{2,3},{3,2},{4,5},{5,4},{6,7},{7,6},{8,9},{9,8},{10,11... | collective-permute-start | bytes 552968 | tf_op jit(solution)/shard_map/ppermute | solution.py:31
  149.8 6.8 %collective-permute-start.32 = (bf16[144,640]{1,0:T(8,128)(2,1)S(1)}, bf16[144,640]{1,0:T(8,128)(2,1)S(1)}, u32[]{:S(2)}, u32[]{:S(2)}) collective-permute-start(bf16[144,640]{1,0:T(8,128)(2,1)S(1)} %fusion.20), channel_id=1, source_target_pairs={{0,4},{4,8},{8,12},{12,0},{1,5},{5,9},{9,13},{13,1},{2,6},{6,10},{... | collective-permute-start | bytes 552968 | tf_op jit(solution)/shard_map/ppermute | solution.py:26
  149.9 12.7 %collective-permute-start.27 = (bf16[2,160,288]{2,1,0:T(8,128)(2,1)S(1)}, bf16[2,160,288]{2,1,0:T(8,128)(2,1)S(1)}, u32[]{:S(2)}, u32[]{:S(2)}) collective-permute-start(bf16[2,160,288]{2,1,0:T(8,128)(2,1)S(1)} %pad_maximum_fusion.10), channel_id=1, source_target_pairs={{0,2},{1,3},{2,0},{3,1},{4,6},{5,7},{6,4},{7,5},{8,10},{9,11},{10,... | collective-permute-start | bytes 552968 | tf_op jit(solution)/shard_map/ppermute | solution.py:31
  152.4 10.2 %collective-permute-start.28 = (bf16[2,160,288]{2,1,0:T(8,128)(2,1)S(1)}, bf16[2,160,288]{2,1,0:T(8,128)(2,1)S(1)}, u32[]{:S(2)}, u32[]{:S(2)}) collective-permute-start(bf16[2,160,288]{2,1,0:T(8,128)(2,1)S(1)} %pad_maximum_fusion.11), channel_id=1, source_target_pairs={{0,3},{1,2},{2,1},{3,0},{4,7},{5,6},{6,5},{7,4},{8,11},{9,10},{10,... | collective-permute-start | bytes 552968 | tf_op jit(solution)/shard_map/ppermute | solution.py:31
  157.4 15.5 %all-to-all-start.3 = ((bf16[8,18,640]{2,1,0:T(8,128)(2,1)}), bf16[8,18,640]{2,1,0:T(8,128)(2,1)S(1)}, u32[]{:S(2)}, u32[]{:S(2)}) async-start(bf16[8,18,640]{2,1,0:T(8,128)(2,1)} %reshape.151), calls=%async_computation.3 | async-start | bytes 491520 | tf_op jit(solution)/shard_map/all_to_all | solution.py:18
  (34 other events, 109.6 us)

commit v2 on v1

--- a/solution.py
+++ b/solution.py
@@ -49,56 +49,48 @@
 
 
 def block_kernel(scalars, place, img_in, *refs):
-    pieces, (t_oth, t_own, g_img, img, parts, texts, coef_t, img_sem, sems) = refs[:16], refs[16:]
-    scale, offset = scalars[0], scalars[1]
-    img_copy = pltpu.make_async_copy(img_in, img, img_sem)
+    pieces = refs[:16]
+    to_oth, to_own, to_img, img, parts, texts, coef, coef_t, t_oth, t_own, g_img, sems, out_sems = refs[16:]
     copies = [pltpu.make_async_copy(pieces[d], parts.at[d], sems.at[d]) for d in range(16)]
+    copies.append(pltpu.make_async_copy(img_in, img, sems.at[16]))
     for copy in copies:
         copy.start()
-    img_copy.start()
     for d in range(8):
         copies[2 * d].wait()
         copies[2 * d + 1].wait()
         texts[80 * d : 80 * d + 80, :] = jnp.concatenate([parts[2 * d], parts[2 * d + 1]])
-    img_copy.wait()
-    first = place[0] * 40
-
-    def images(i, _):
-        at = pl.multiple_of(i * 128, 128)
-        block = img[pl.ds(at, 128), :]
-        dots = lax.dot_general(block, texts[...], (((1,), (1,)), ((), ())), preferred_element_type=F32)
-        rows = lax.broadcasted_iota(jnp.int32, (128, 640), 0) + at - first
-        cols = lax.broadcasted_iota(jnp.int32, (128, 640), 1) - 320
-        sign = jnp.where((rows == cols) & (cols >= 0) & (cols < 40), F32(1.0), F32(-1.0))
-        value = -sign * scale * jax.nn.sigmoid(-sign * (scale * dots + offset))
-        coef_t[:, pl.ds(at, 128)] = value.T.astype(BF)
-        value = value.astype(BF)
-        g_img[pl.ds(at, 128), :] = jnp.dot(value, texts[...], preferred_element_type=F32).astype(BF)
-        return 0
-
-    lax.fori_loop(0, 5, images, 0)
-
-    def others(j, _):
-        at = pl.multiple_of(j * 160, 32)
-        t_oth[pl.ds(at, 160), :] = jnp.dot(
-            coef_t[pl.ds(at, 160), :], img[...], preferred_element_type=F32
+    copies[16].wait()
+    scale, offset = scalars[0], scalars[1]
+    dots = lax.dot_general(img[...], texts[...], (((1,), (1,)), ((), ())), preferred_element_type=F32)
+    rows = lax.broadcasted_iota(jnp.int32, (640, 640), 0) - place[0] * 40
+    cols = lax.broadcasted_iota(jnp.int32, (640, 640), 1) - 320
+    sign = jnp.where((rows == cols) & (cols >= 0) & (cols < 40), F32(1.0), F32(-1.0))
+    value = (-sign * scale * jax.nn.sigmoid(-sign * (scale * dots + offset))).astype(BF)
+    coef[...] = value
+    coef_t[...] = value.T
+    sends = [
+        pltpu.make_async_copy(t_oth, to_oth, out_sems.at[0]),
+        pltpu.make_async_copy(t_own, to_own, out_sems.at[1]),
+        pltpu.make_async_copy(g_img.at[pl.ds(0, 320)], to_img.at[pl.ds(0, 320)], out_sems.at[2]),
+        pltpu.make_async_copy(g_img.at[pl.ds(320, 320)], to_img.at[pl.ds(320, 320)], out_sems.at[3]),
+    ]
+    t_oth[...] = jnp.dot(coef_t[:320, :], img[...], preferred_element_type=F32).astype(BF)
+    sends[0].start()
+    t_own[...] = jnp.dot(coef_t[320:, :], img[...], preferred_element_type=F32)
+    sends[1].start()
+    for half in range(2):
+        at = 320 * half
+        g_img[at : at + 320, :] = jnp.dot(
+            coef[at : at + 320, :], texts[...], preferred_element_type=F32
         ).astype(BF)
-        return 0
-
-    lax.fori_loop(0, 2, others, 0)
-
-    def owns(j, _):
-        at = pl.multiple_of(j * 160, 32)
-        t_own[pl.ds(at, 160), :] = jnp.dot(coef_t[pl.ds(320 + at, 160), :], img[...], preferred_element_type=F32)
-        return 0
-
-    lax.fori_loop(0, 2, owns, 0)
+        sends[2 + half].start()
+    for send in sends:
+        send.wait()
 
 
 def block_grads(scalars, place, img, pieces):
     small = pl.BlockSpec(memory_space=pltpu.SMEM)
-    large = pl.BlockSpec(memory_space=pl.ANY)
-    vmem = pl.BlockSpec(memory_space=pltpu.VMEM)
+    large = pl.BlockSpec(memory_space=pltpu.HBM)
     return pl.pallas_call(
         block_kernel,
         out_shape=[
@@ -107,16 +99,20 @@
             jax.ShapeDtypeStruct((640, 1152), BF),
         ],
         in_specs=[small, small] + [large] * 17,
-        out_specs=[vmem] * 3,
+        out_specs=[large] * 3,
         scratch_shapes=[
             pltpu.VMEM((640, 1152), BF),
             pltpu.VMEM((16, 40, 1152), BF),
             pltpu.VMEM((640, 1152), BF),
             pltpu.VMEM((640, 640), BF),
-            pltpu.SemaphoreType.DMA,
-            pltpu.SemaphoreType.DMA((16,)),
+            pltpu.VMEM((640, 640), BF),
+            pltpu.VMEM((320, 1152), BF),
+            pltpu.VMEM((320, 1152), F32),
+            pltpu.VMEM((640, 1152), BF),
+            pltpu.SemaphoreType.DMA((17,)),
+            pltpu.SemaphoreType.DMA((4,)),
         ],
-        compiler_params=pltpu.CompilerParams(vmem_limit_bytes=24 * 2**20),
+        compiler_params=pltpu.CompilerParams(vmem_limit_bytes=60 * 2**20),
         cost_estimate=pl.CostEstimate(flops=2900000000, bytes_accessed=8000000, transcendentals=400000),
     )(scalars, place, img, *pieces)
 
@@ -144,15 +140,16 @@
     img = jnp.broadcast_to(z_img[None], (16, 40, 1152))
     img, z_near = lax.optimization_barrier((img, z_txt))
     img = a2a(img, PLANE).reshape(640, 1152)
+    come = lax.ppermute(give, "xl", [(0, 1), (1, 0)])
     up, down = [z_near], [z_near]
     for d in range(3):
         up.append(shift(up[-1], "z", 8, 1))
         down.append(shift(down[-1], "z", 8, -1))
+        if d == 1:
+            up[2], come = lax.optimization_barrier((up[2], come))
     up.append(shift(up[-1], "z", 8, 1))
     txt_own = up + down[:0:-1]
     txt_oth = [swap_core(piece) for piece in txt_own]
-    give, img = lax.optimization_barrier((give, img))
-    come = lax.ppermute(give, "xl", [(0, 1), (1, 0)])
     first, second = jnp.where(xl == 0, keep, come), jnp.where(xl == 0, come, keep)
     fi = jnp.concatenate([first[:160], second[:160]])
     ft = jnp.concatenate([first[160:], second[160:]])

time: 176 us -> 163 us (0.926)
  local copies, waits for them, and re-layouts: 22 us -> 8.88 us
  Pallas kernels: 10.8 us -> 7.66 us
    unnamed x59 -> x37, local copies, waits for them, and re-layouts: 17.3 us -> 3.53 us
    ppermute x17, waiting for transfers between devices: 23.4 us -> 27.9 us  [shift(): return lax.ppermute(x, axis, [(i, (i + step) % size) for i in range(size)])]
    ppermute x1, waiting for transfers between devices: 17.2 us -> 13 us  [shards(): come = lax.ppermute(give, 'xl', [(0, 1), (1, 0)])]
    ppermute x17, starting transfers between devices: 29.5 us -> 33.4 us  [shift(): return lax.ppermute(x, axis, [(i, (i + step) % size) for i in range(size)])]
    pallas_call x1, Pallas kernels: 10.8 us -> 7.66 us  [block_grads(): pl.pallas_call(block_kernel, out_shape=[jax.ShapeDtypeStruct((320, 1152),...]
    ppermute x6, waiting for transfers between devices: 2.67 us -> 4.92 us  [mp_shift(): return lax.ppermute(x, MP, pairs)]
    all_to_all x4, starting transfers between devices: 26.9 us -> 25 us  [a2a(): return lax.all_to_all(x, axes, 0, 0, tiled=True)]
  transfers between devices with their start and end apart: 37 -> 37, of which waited for: 14 -> 16; matrix products, arithmetic and copies ran while one was open for 6% -> 7% of each run, Pallas kernels for 0% -> 0%
where the time goes in v2:
time: 163 us; the launch traced here: 161 us
  starting transfers between devices  66 us (40%)
  waiting for transfers between devices  61.3 us (38%)
  local copies, waits for them, and re-layouts  8.88 us (5%)
  matrix products  8.37 us (5%)
  Pallas kernels  7.66 us (5%)
  other arithmetic  6.26 us (4%)
  between operations  2.6 us (2%)
    ppermute x17, starting transfers between devices, shift(): return lax.ppermute(x, axis, [(i, (i + step) % size) for i in range(size)])  33.4 us
    ppermute x17, waiting for transfers between devices, shift(): return lax.ppermute(x, axis, [(i, (i + step) % size) for i in range(size)])  27.9 us
    all_to_all x4, starting transfers between devices, a2a(): return lax.all_to_all(x, axes, 0, 0, tiled=True)  25 us
    all_to_all x4, waiting for transfers between devices, a2a(): return lax.all_to_all(x, axes, 0, 0, tiled=True)  15.4 us
    ppermute x1, waiting for transfers between devices, shards(): come = lax.ppermute(give, 'xl', [(0, 1), (1, 0)])  13 us
    pallas_call x1, Pallas kernels, block_grads(): pl.pallas_call(block_kernel, out_shape=[jax.ShapeDtypeStruct((320, 1152),...  7.66 us
    ppermute x6, starting transfers between devices, mp_shift(): return lax.ppermute(x, MP, pairs)  5.29 us
    ppermute x6, waiting for transfers between devices, mp_shift(): return lax.ppermute(x, MP, pairs)  4.92 us
  transfers between devices with their start and end apart: 37, of which 16 were waited for; matrix products, arithmetic and copies ran while one was open for 7% of the time, Pallas kernels for 0%

profile of v2, /device:TPU:2, one launch (start us, length us, event | category | flops | bytes accessed | tf_op | source)
XLA Modules:
  0.0 161.1 jit_solution(11574353535160238979)
XLA Ops:
  4.4 2.1 %collective-permute-start.1 = (f32[2,40,288]{2,1,0:T(8,128)}, f32[2,40,288]{2,1,0:T(8,128)S(1)}, u32[]{:S(2)}, u32[]{:S(2)}) collective-permute-start(f32[2,40,288]{2,1,0:T(8,128)} %get-tuple-element.50), channel_id=1, source_target_pairs={{0,2},{1,3},{2,0},{3,1},{4,6},{5,7},{6,4},{7,5},{8,10},{9,11},{10,... | collective-permute-start | bytes 276488 | tf_op jit(solution)/shard_map/ppermute | solution.py:31
  8.8 1.6 fusion.9
  10.4 1.9 %collective-permute-done.1 = f32[2,40,288]{2,1,0:T(8,128)S(1)} collective-permute-done((f32[2,40,288]{2,1,0:T(8,128)}, f32[2,40,288]{2,1,0:T(8,128)S(1)}, u32[]{:S(2)}, u32[]{:S(2)}) %collective-permute-start.1) | collective-permute-done | bytes 92192 | tf_op jit(solution)/shard_map/ppermute | solution.py:31
  12.2 1.9 %collective-permute-done.2 = f32[2,40,288]{2,1,0:T(8,128)S(1)} collective-permute-done((f32[2,40,288]{2,1,0:T(8,128)S(1)}, f32[2,40,288]{2,1,0:T(8,128)S(1)}, u32[]{:S(2)}, u32[]{:S(2)}) %collective-permute-start.2) | collective-permute-done | bytes 92192 | tf_op jit(solution)/shard_map/ppermute | solution.py:31
  15.9 7.5 %all-to-all-start = ((bf16[16,40,1152]{2,1,0:T(8,128)(2,1)}), bf16[16,40,1152]{2,1,0:T(8,128)(2,1)S(1)}, u32[]{:S(2)}, u32[]{:S(2)}) async-start(bf16[16,40,1152]{2,1,0:T(8,128)(2,1)} %broadcast_in_dim.37), calls=%async_computation | async-start | bytes 2949120 | tf_op jit(solution)/shard_map/all_to_all | solution.py:18
  23.6 1.9 %collective-permute-start.4 = (bf16[40,1152]{1,0:T(8,128)(2,1)S(1)}, bf16[40,1152]{1,0:T(8,128)(2,1)S(1)}, u32[]{:S(2)}, u32[]{:S(2)}) collective-permute-start(bf16[40,1152]{1,0:T(8,128)(2,1)S(1)} %get-tuple-element.20.refs_8_), channel_id=1, source_target_pairs={{0,32},{32,64},{64,96},{96,128},{128,160},{160,192},{192,224},{224... | collective-permute-start | bytes 276488 | tf_op jit(solution)/shard_map/ppermute | solution.py:26
  25.5 3.9 %collective-permute-start.13 = (bf16[40,1152]{1,0:T(8,128)(2,1)S(1)}, bf16[40,1152]{1,0:T(8,128)(2,1)S(1)}, u32[]{:S(2)}, u32[]{:S(2)}) collective-permute-start(bf16[40,1152]{1,0:T(8,128)(2,1)S(1)} %get-tuple-element.20.refs_8_), channel_id=1, source_target_pairs={{0,224},{32,0},{64,32},{96,64},{128,96},{160,128},{192,160},{224,1... | collective-permute-start | bytes 276488 | tf_op jit(solution)/shard_map/ppermute | solution.py:26
  29.4 2.5 %collective-permute-done.4.refs_9_ = bf16[40,1152]{1,0:T(8,128)(2,1)S(1)} collective-permute-done((bf16[40,1152]{1,0:T(8,128)(2,1)S(1)}, bf16[40,1152]{1,0:T(8,128)(2,1)S(1)}, u32[]{:S(2)}, u32[]{:S(2)}) %collective-permute-start.4) | collective-permute-done | bytes 92192 | tf_op jit(solution)/shard_map/ppermute | solution.py:26
  32.0 3.2 %collective-permute-start.14 = (bf16[40,1152]{1,0:T(8,128)(2,1)S(1)}, bf16[40,1152]{1,0:T(8,128)(2,1)}, u32[]{:S(2)}, u32[]{:S(2)}) collective-permute-start(bf16[40,1152]{1,0:T(8,128)(2,1)S(1)} %collective-permute-done.13.refs_15_), channel_id=1, source_target_pairs={{0,224},{32,0},{64,32},{96,64},{128,96},{160,128},{192,160},{224,1... | collective-permute-start | bytes 276488 | tf_op jit(solution)/shard_map/ppermute | solution.py:26
  35.2 2.5 %collective-permute-done.6.refs_10_ = bf16[40,1152]{1,0:T(8,128)(2,1)S(1)} collective-permute-done((bf16[40,1152]{1,0:T(8,128)(2,1)S(1)}, bf16[40,1152]{1,0:T(8,128)(2,1)S(1)}, u32[]{:S(2)}, u32[]{:S(2)}) %collective-permute-start.6) | collective-permute-done | bytes 92192 | tf_op jit(solution)/shard_map/ppermute | solution.py:26
  37.7 13.0 %collective-permute-done.7 = bf16[320,576]{1,0:T(8,128)(2,1)S(1)} collective-permute-done((bf16[320,576]{1,0:T(8,128)(2,1)}, bf16[320,576]{1,0:T(8,128)(2,1)S(1)}, u32[]{:S(2)}, u32[]{:S(2)}) %collective-permute-start.7) | collective-permute-done | bytes 368672 | tf_op jit(solution)/shard_map/ppermute | solution.py:143
  50.7 1.9 %collective-permute-start.9 = (bf16[40,1152]{1,0:T(8,128)(2,1)S(1)}, bf16[40,1152]{1,0:T(8,128)(2,1)}, u32[]{:S(2)}, u32[]{:S(2)}) collective-permute-start(bf16[40,1152]{1,0:T(8,128)(2,1)S(1)} %collective-permute-done.6.refs_10_), channel_id=1, source_target_pairs={{0,32},{32,64},{64,96},{96,128},{128,160},{160,192},{192,224},{224... | collective-permute-start | bytes 276488 | tf_op jit(solution)/shard_map/ppermute | solution.py:26
  52.7 4.1 %collective-permute-start.15 = (bf16[40,1152]{1,0:T(8,128)(2,1)}, bf16[40,1152]{1,0:T(8,128)(2,1)}, u32[]{:S(2)}, u32[]{:S(2)}) collective-permute-start(bf16[40,1152]{1,0:T(8,128)(2,1)} %collective-permute-done.14.refs_14_), channel_id=1, source_target_pairs={{0,224},{32,0},{64,32},{96,64},{128,96},{160,128},{192,160},{224,1... | collective-permute-start | bytes 276488 | tf_op jit(solution)/shard_map/ppermute | solution.py:26
  57.3 1.9 %collective-permute-done.9.refs_11_ = bf16[40,1152]{1,0:T(8,128)(2,1)} collective-permute-done((bf16[40,1152]{1,0:T(8,128)(2,1)S(1)}, bf16[40,1152]{1,0:T(8,128)(2,1)}, u32[]{:S(2)}, u32[]{:S(2)}) %collective-permute-start.9) | collective-permute-done | bytes 92192 | tf_op jit(solution)/shard_map/ppermute | solution.py:26
  61.7 3.6 %collective-permute-done.11.refs_12_ = bf16[40,1152]{1,0:T(8,128)(2,1)} collective-permute-done((bf16[40,1152]{1,0:T(8,128)(2,1)}, bf16[40,1152]{1,0:T(8,128)(2,1)}, u32[]{:S(2)}, u32[]{:S(2)}) %collective-permute-start.11) | collective-permute-done | bytes 92192 | tf_op jit(solution)/shard_map/ppermute | solution.py:26
  68.4 7.7 %shard_map.93 = (bf16[320,1152]{1,0:T(8,128)(2,1)}, f32[320,1152]{1,0:T(8,128)}, bf16[640,1152]{1,0:T(8,128)(2,1)}) custom-call(f32[2]{0:T(128)} %pad_maximum_fusion.16.scalars, s32[1]{0:T(128)} %bitcast.8.place, bf16[640,1152]{1,0:T(8,128)(2,1)} %bitcast.97, bf16[40,1152]{1,0:T(8,128)(2,1)} %collective-permute-done.3.refs_0_, ...), custom_call_target="tpu_custom_call" | custom-call | flops 2900000000 | bytes 8000000 | tf_op jit(solution)/shard_map/pallas_call | solution.py:94
  77.3 8.6 %all-to-all-start.1 = ((bf16[16,40,1152]{2,1,0:T(8,128)(2,1)}), bf16[16,40,1152]{2,1,0:T(8,128)(2,1)S(1)}, u32[]{:S(2)}, u32[]{:S(2)}) async-start(bf16[16,40,1152]{2,1,0:T(8,128)(2,1)} %bitcast.96), calls=%async_computation.1 | async-start | bytes 2949120 | tf_op jit(solution)/shard_map/all_to_all | solution.py:18
  88.5 1.6 %collective-permute-start.21 = (bf16[40,1152]{1,0:T(8,128)(2,1)S(1)}, bf16[40,1152]{1,0:T(8,128)(2,1)S(1)}, u32[]{:S(2)}, u32[]{:S(2)}) collective-permute-start(bf16[40,1152]{1,0:T(8,128)(2,1)S(1)} %get-tuple-element.42), channel_id=1, source_target_pairs={{0,192},{32,224},{64,0},{96,32},{128,64},{160,96},{192,128},{224,1... | collective-permute-start | bytes 276488 | tf_op jit(solution)/shard_map/ppermute | solution.py:26
  90.7 2.7 %collective-permute-start.22 = (bf16[40,1152]{1,0:T(8,128)(2,1)S(1)}, bf16[40,1152]{1,0:T(8,128)(2,1)S(1)}, u32[]{:S(2)}, u32[]{:S(2)}) collective-permute-start(bf16[40,1152]{1,0:T(8,128)(2,1)S(1)} %get-tuple-element.41), channel_id=1, source_target_pairs={{0,160},{32,192},{64,224},{96,0},{128,32},{160,64},{192,96},{224,1... | collective-permute-start | bytes 276488 | tf_op jit(solution)/shard_map/ppermute | solution.py:26
  93.3 2.6 %collective-permute-start.23 = (bf16[40,1152]{1,0:T(8,128)(2,1)S(1)}, bf16[40,1152]{1,0:T(8,128)(2,1)S(1)}, u32[]{:S(2)}, u32[]{:S(2)}) collective-permute-start(bf16[40,1152]{1,0:T(8,128)(2,1)S(1)} %get-tuple-element.40), channel_id=1, source_target_pairs={{0,128},{32,160},{64,192},{96,224},{128,0},{160,32},{192,64},{224,... | collective-permute-start | bytes 276488 | tf_op jit(solution)/shard_map/ppermute | solution.py:26
  97.2 3.7 %collective-permute-start.25 = (bf16[40,1152]{1,0:T(8,128)(2,1)S(1)}, bf16[40,1152]{1,0:T(8,128)(2,1)S(1)}, u32[]{:S(2)}, u32[]{:S(2)}) collective-permute-start(bf16[40,1152]{1,0:T(8,128)(2,1)S(1)} %get-tuple-element.38), channel_id=1, source_target_pairs={{0,64},{32,96},{64,128},{96,160},{128,192},{160,224},{192,0},{224,... | collective-permute-start | bytes 276488 | tf_op jit(solution)/shard_map/ppermute | solution.py:26
  100.8 1.9 %collective-permute-start.26 = (bf16[40,1152]{1,0:T(8,128)(2,1)S(1)}, bf16[40,1152]{1,0:T(8,128)(2,1)S(1)}, u32[]{:S(2)}, u32[]{:S(2)}) collective-permute-start(bf16[40,1152]{1,0:T(8,128)(2,1)S(1)} %get-tuple-element.37), channel_id=1, source_target_pairs={{0,32},{32,64},{64,96},{96,128},{128,160},{160,192},{192,224},{224... | collective-permute-start | bytes 276488 | tf_op jit(solution)/shard_map/ppermute | solution.py:26
  103.2 5.7 %collective-permute-done.24 = bf16[40,1152]{1,0:T(8,128)(2,1)S(1)} collective-permute-done((bf16[40,1152]{1,0:T(8,128)(2,1)S(1)}, bf16[40,1152]{1,0:T(8,128)(2,1)S(1)}, u32[]{:S(2)}, u32[]{:S(2)}) %collective-permute-start.24) | collective-permute-done | bytes 92192 | tf_op jit(solution)/shard_map/ppermute | solution.py:26
  108.9 4.6 %collective-permute-done.25 = bf16[40,1152]{1,0:T(8,128)(2,1)S(1)} collective-permute-done((bf16[40,1152]{1,0:T(8,128)(2,1)S(1)}, bf16[40,1152]{1,0:T(8,128)(2,1)S(1)}, u32[]{:S(2)}, u32[]{:S(2)}) %collective-permute-start.25) | collective-permute-done | bytes 92192 | tf_op jit(solution)/shard_map/ppermute | solution.py:26
  116.6 4.9 %all-to-all-start.2 = ((bf16[8,200,128]{2,1,0:T(8,128)(2,1)}), bf16[8,200,128]{2,1,0:T(8,128)(2,1)S(1)}, u32[]{:S(2)}, u32[]{:S(2)}) async-start(bf16[8,200,128]{2,1,0:T(8,128)(2,1)} %bitcast.20), calls=%async_computation.2 | async-start | bytes 819200 | tf_op jit(solution)/shard_map/all_to_all | solution.py:18
  121.6 7.0 %all-to-all-done.2 = bf16[8,200,128]{2,1,0:T(8,128)(2,1)S(1)} async-done(((bf16[8,200,128]{2,1,0:T(8,128)(2,1)}), bf16[8,200,128]{2,1,0:T(8,128)(2,1)S(1)}, u32[]{:S(2)}, u32[]{:S(2)}) %all-to-all-start.2) | async-done | bytes 409632 | tf_op jit(solution)/shard_map/all_to_all | solution.py:18
  131.8 1.8 %collective-permute-start.30 = (bf16[144,640]{1,0:T(8,128)(2,1)S(1)}, bf16[144,640]{1,0:T(8,128)(2,1)S(1)}, u32[]{:S(2)}, u32[]{:S(2)}) collective-permute-start(bf16[144,640]{1,0:T(8,128)(2,1)S(1)} %get-tuple-element.32), channel_id=1, source_target_pairs={{0,12},{4,0},{8,4},{12,8},{1,13},{5,1},{9,5},{13,9},{2,14},{6,2},{... | collective-permute-start | bytes 552968 | tf_op jit(solution)/shard_map/ppermute | solution.py:26
  135.2 2.4 %collective-permute-done.31 = bf16[144,640]{1,0:T(8,128)(2,1)S(1)} collective-permute-done((bf16[144,640]{1,0:T(8,128)(2,1)S(1)}, bf16[144,640]{1,0:T(8,128)(2,1)S(1)}, u32[]{:S(2)}, u32[]{:S(2)}) %collective-permute-start.31) | collective-permute-done | bytes 184352 | tf_op jit(solution)/shard_map/ppermute | solution.py:26
  138.0 1.7 %collective-permute-start.28 = (bf16[2,160,288]{2,1,0:T(8,128)(2,1)S(1)}, bf16[2,160,288]{2,1,0:T(8,128)(2,1)S(1)}, u32[]{:S(2)}, u32[]{:S(2)}) collective-permute-start(bf16[2,160,288]{2,1,0:T(8,128)(2,1)S(1)} %pad_maximum_fusion.10), channel_id=1, source_target_pairs={{0,2},{1,3},{2,0},{3,1},{4,6},{5,7},{6,4},{7,5},{8,10},{9,11},{10,... | collective-permute-start | bytes 552968 | tf_op jit(solution)/shard_map/ppermute | solution.py:31
  141.2 3.2 %collective-permute-done.32 = bf16[144,640]{1,0:T(8,128)(2,1)S(1)} collective-permute-done((bf16[144,640]{1,0:T(8,128)(2,1)S(1)}, bf16[144,640]{1,0:T(8,128)(2,1)S(1)}, u32[]{:S(2)}, u32[]{:S(2)}) %collective-permute-start.32) | collective-permute-done | bytes 184352 | tf_op jit(solution)/shard_map/ppermute | solution.py:26
  145.2 3.9 %all-to-all-start.3 = ((bf16[8,18,640]{2,1,0:T(8,128)(2,1)}), bf16[8,18,640]{2,1,0:T(8,128)(2,1)S(1)}, u32[]{:S(2)}, u32[]{:S(2)}) async-start(bf16[8,18,640]{2,1,0:T(8,128)(2,1)} %reshape.151), calls=%async_computation.3 | async-start | bytes 491520 | tf_op jit(solution)/shard_map/all_to_all | solution.py:18
  151.3 8.4 %all-to-all-done.3 = bf16[8,18,640]{2,1,0:T(8,128)(2,1)S(1)} async-done(((bf16[8,18,640]{2,1,0:T(8,128)(2,1)}), bf16[8,18,640]{2,1,0:T(8,128)(2,1)S(1)}, u32[]{:S(2)}, u32[]{:S(2)}) %all-to-all-start.3) | async-done | bytes 184352 | tf_op jit(solution)/shard_map/all_to_all | solution.py:18
  (144 shorter events, 32.3 us)
Async XLA Ops:
  4.4 6.0 %collective-permute-start = (f32[2,40,288]{2,1,0:T(8,128)}, f32[2,40,288]{2,1,0:T(8,128)S(1)}, u32[]{:S(2)}, u32[]{:S(2)}) collective-permute-start(f32[2,40,288]{2,1,0:T(8,128)} %get-tuple-element.49), channel_id=1, source_target_pairs={{0,1},{1,0},{2,3},{3,2},{4,5},{5,4},{6,7},{7,6},{8,9},{9,8},{10,11... | collective-permute-start | bytes 276488 | tf_op jit(solution)/shard_map/ppermute | solution.py:31
  4.4 7.8 %collective-permute-start.1 = (f32[2,40,288]{2,1,0:T(8,128)}, f32[2,40,288]{2,1,0:T(8,128)S(1)}, u32[]{:S(2)}, u32[]{:S(2)}) collective-permute-start(f32[2,40,288]{2,1,0:T(8,128)} %get-tuple-element.50), channel_id=1, source_target_pairs={{0,2},{1,3},{2,0},{3,1},{4,6},{5,7},{6,4},{7,5},{8,10},{9,11},{10,... | collective-permute-start | bytes 276488 | tf_op jit(solution)/shard_map/ppermute | solution.py:31
  6.5 7.6 %collective-permute-start.2 = (f32[2,40,288]{2,1,0:T(8,128)S(1)}, f32[2,40,288]{2,1,0:T(8,128)S(1)}, u32[]{:S(2)}, u32[]{:S(2)}) collective-permute-start(f32[2,40,288]{2,1,0:T(8,128)S(1)} %get-tuple-element.48), channel_id=1, source_target_pairs={{0,3},{1,2},{2,1},{3,0},{4,7},{5,6},{6,5},{7,4},{8,11},{9,10},{10,... | collective-permute-start | bytes 276488 | tf_op jit(solution)/shard_map/ppermute | solution.py:31
  15.9 51.3 %all-to-all-start = ((bf16[16,40,1152]{2,1,0:T(8,128)(2,1)}), bf16[16,40,1152]{2,1,0:T(8,128)(2,1)S(1)}, u32[]{:S(2)}, u32[]{:S(2)}) async-start(bf16[16,40,1152]{2,1,0:T(8,128)(2,1)} %broadcast_in_dim.37), calls=%async_computation | async-start | bytes 2949120 | tf_op jit(solution)/shard_map/all_to_all | solution.py:18
  23.4 27.3 %collective-permute-start.7 = (bf16[320,576]{1,0:T(8,128)(2,1)}, bf16[320,576]{1,0:T(8,128)(2,1)S(1)}, u32[]{:S(2)}, u32[]{:S(2)}) collective-permute-start(bf16[320,576]{1,0:T(8,128)(2,1)} %fusion.9), channel_id=1, source_target_pairs={{0,16},{16,0},{1,17},{17,1},{2,18},{18,2},{3,19},{19,3},{4,20},{20... | collective-permute-start | bytes 1105928 | tf_op jit(solution)/shard_map/ppermute | solution.py:143
  23.6 8.4 %collective-permute-start.4 = (bf16[40,1152]{1,0:T(8,128)(2,1)S(1)}, bf16[40,1152]{1,0:T(8,128)(2,1)S(1)}, u32[]{:S(2)}, u32[]{:S(2)}) collective-permute-start(bf16[40,1152]{1,0:T(8,128)(2,1)S(1)} %get-tuple-element.20.refs_8_), channel_id=1, source_target_pairs={{0,32},{32,64},{64,96},{96,128},{128,160},{160,192},{192,224},{224... | collective-permute-start | bytes 276488 | tf_op jit(solution)/shard_map/ppermute | solution.py:26
  25.5 6.5 %collective-permute-start.13 = (bf16[40,1152]{1,0:T(8,128)(2,1)S(1)}, bf16[40,1152]{1,0:T(8,128)(2,1)S(1)}, u32[]{:S(2)}, u32[]{:S(2)}) collective-permute-start(bf16[40,1152]{1,0:T(8,128)(2,1)S(1)} %get-tuple-element.20.refs_8_), channel_id=1, source_target_pairs={{0,224},{32,0},{64,32},{96,64},{128,96},{160,128},{192,160},{224,1... | collective-permute-start | bytes 276488 | tf_op jit(solution)/shard_map/ppermute | solution.py:26
  32.0 5.8 %collective-permute-start.6 = (bf16[40,1152]{1,0:T(8,128)(2,1)S(1)}, bf16[40,1152]{1,0:T(8,128)(2,1)S(1)}, u32[]{:S(2)}, u32[]{:S(2)}) collective-permute-start(bf16[40,1152]{1,0:T(8,128)(2,1)S(1)} %collective-permute-done.4.refs_9_), channel_id=1, source_target_pairs={{0,32},{32,64},{64,96},{96,128},{128,160},{160,192},{192,224},{224... | collective-permute-start | bytes 276488 | tf_op jit(solution)/shard_map/ppermute | solution.py:26
  32.0 20.7 %collective-permute-start.14 = (bf16[40,1152]{1,0:T(8,128)(2,1)S(1)}, bf16[40,1152]{1,0:T(8,128)(2,1)}, u32[]{:S(2)}, u32[]{:S(2)}) collective-permute-start(bf16[40,1152]{1,0:T(8,128)(2,1)S(1)} %collective-permute-done.13.refs_15_), channel_id=1, source_target_pairs={{0,224},{32,0},{64,32},{96,64},{128,96},{160,128},{192,160},{224,1... | collective-permute-start | bytes 276488 | tf_op jit(solution)/shard_map/ppermute | solution.py:26
  50.7 8.5 %collective-permute-start.9 = (bf16[40,1152]{1,0:T(8,128)(2,1)S(1)}, bf16[40,1152]{1,0:T(8,128)(2,1)}, u32[]{:S(2)}, u32[]{:S(2)}) collective-permute-start(bf16[40,1152]{1,0:T(8,128)(2,1)S(1)} %collective-permute-done.6.refs_10_), channel_id=1, source_target_pairs={{0,32},{32,64},{64,96},{96,128},{128,160},{160,192},{192,224},{224... | collective-permute-start | bytes 276488 | tf_op jit(solution)/shard_map/ppermute | solution.py:26
  52.7 7.9 %collective-permute-start.3 = (bf16[40,1152]{1,0:T(8,128)(2,1)S(1)}, bf16[40,1152]{1,0:T(8,128)(2,1)}, u32[]{:S(2)}, u32[]{:S(2)}) collective-permute-start(bf16[40,1152]{1,0:T(8,128)(2,1)S(1)} %get-tuple-element.20.refs_8_), channel_id=1, source_target_pairs={{0,1},{1,0},{2,3},{3,2},{4,5},{5,4},{6,7},{7,6},{8,9},{9,8},{10,11... | collective-permute-start | bytes 276488 | tf_op jit(solution)/shard_map/ppermute | solution.py:22
  52.7 8.0 %collective-permute-start.15 = (bf16[40,1152]{1,0:T(8,128)(2,1)}, bf16[40,1152]{1,0:T(8,128)(2,1)}, u32[]{:S(2)}, u32[]{:S(2)}) collective-permute-start(bf16[40,1152]{1,0:T(8,128)(2,1)} %collective-permute-done.14.refs_14_), channel_id=1, source_target_pairs={{0,224},{32,0},{64,32},{96,64},{128,96},{160,128},{192,160},{224,1... | collective-permute-start | bytes 276488 | tf_op jit(solution)/shard_map/ppermute | solution.py:26
  59.2 6.1 %collective-permute-start.11 = (bf16[40,1152]{1,0:T(8,128)(2,1)}, bf16[40,1152]{1,0:T(8,128)(2,1)}, u32[]{:S(2)}, u32[]{:S(2)}) collective-permute-start(bf16[40,1152]{1,0:T(8,128)(2,1)} %collective-permute-done.9.refs_11_), channel_id=1, source_target_pairs={{0,32},{32,64},{64,96},{96,128},{128,160},{160,192},{192,224},{224... | collective-permute-start | bytes 276488 | tf_op jit(solution)/shard_map/ppermute | solution.py:26
  60.6 5.3 %collective-permute-start.17 = (bf16[40,1152]{1,0:T(8,128)(2,1)}, bf16[40,1152]{1,0:T(8,128)(2,1)S(1)}, u32[]{:S(2)}, u32[]{:S(2)}) collective-permute-start(bf16[40,1152]{1,0:T(8,128)(2,1)} %collective-permute-done.14.refs_14_), channel_id=1, source_target_pairs={{0,1},{1,0},{2,3},{3,2},{4,5},{5,4},{6,7},{7,6},{8,9},{9,8},{10,11... | collective-permute-start | bytes 276488 | tf_op jit(solution)/shard_map/ppermute | solution.py:22
  60.7 5.2 %collective-permute-start.16 = (bf16[40,1152]{1,0:T(8,128)(2,1)}, bf16[40,1152]{1,0:T(8,128)(2,1)S(1)}, u32[]{:S(2)}, u32[]{:S(2)}) collective-permute-start(bf16[40,1152]{1,0:T(8,128)(2,1)} %collective-permute-done.15.refs_13_), channel_id=1, source_target_pairs={{0,1},{1,0},{2,3},{3,2},{4,5},{5,4},{6,7},{7,6},{8,9},{9,8},{10,11... | collective-permute-start | bytes 276488 | tf_op jit(solution)/shard_map/ppermute | solution.py:22
  76.0 9.9 %collective-permute-start.19 = (bf16[320,1152]{1,0:T(8,128)(2,1)}, bf16[320,1152]{1,0:T(8,128)(2,1)S(1)}, u32[]{:S(2)}, u32[]{:S(2)}) collective-permute-start(bf16[320,1152]{1,0:T(8,128)(2,1)} %get-tuple-element.25), channel_id=1, source_target_pairs={{0,1},{1,0},{2,3},{3,2},{4,5},{5,4},{6,7},{7,6},{8,9},{9,8},{10,11... | collective-permute-start | bytes 2211848 | tf_op jit(solution)/shard_map/ppermute | solution.py:22
  77.3 37.4 %all-to-all-start.1 = ((bf16[16,40,1152]{2,1,0:T(8,128)(2,1)}), bf16[16,40,1152]{2,1,0:T(8,128)(2,1)S(1)}, u32[]{:S(2)}, u32[]{:S(2)}) async-start(bf16[16,40,1152]{2,1,0:T(8,128)(2,1)} %bitcast.96), calls=%async_computation.1 | async-start | bytes 2949120 | tf_op jit(solution)/shard_map/all_to_all | solution.py:18
  87.6 9.5 %collective-permute-start.20 = (bf16[40,1152]{1,0:T(8,128)(2,1)S(1)}, bf16[40,1152]{1,0:T(8,128)(2,1)S(1)}, u32[]{:S(2)}, u32[]{:S(2)}) collective-permute-start(bf16[40,1152]{1,0:T(8,128)(2,1)S(1)} %get-tuple-element.36), channel_id=1, source_target_pairs={{0,224},{32,0},{64,32},{96,64},{128,96},{160,128},{192,160},{224,1... | collective-permute-start | bytes 276488 | tf_op jit(solution)/shard_map/ppermute | solution.py:26
  88.5 12.3 %collective-permute-start.21 = (bf16[40,1152]{1,0:T(8,128)(2,1)S(1)}, bf16[40,1152]{1,0:T(8,128)(2,1)S(1)}, u32[]{:S(2)}, u32[]{:S(2)}) collective-permute-start(bf16[40,1152]{1,0:T(8,128)(2,1)S(1)} %get-tuple-element.42), channel_id=1, source_target_pairs={{0,192},{32,224},{64,0},{96,32},{128,64},{160,96},{192,128},{224,1... | collective-permute-start | bytes 276488 | tf_op jit(solution)/shard_map/ppermute | solution.py:26
  90.7 12.2 %collective-permute-start.22 = (bf16[40,1152]{1,0:T(8,128)(2,1)S(1)}, bf16[40,1152]{1,0:T(8,128)(2,1)S(1)}, u32[]{:S(2)}, u32[]{:S(2)}) collective-permute-start(bf16[40,1152]{1,0:T(8,128)(2,1)S(1)} %get-tuple-element.41), channel_id=1, source_target_pairs={{0,160},{32,192},{64,224},{96,0},{128,32},{160,64},{192,96},{224,1... | collective-permute-start | bytes 276488 | tf_op jit(solution)/shard_map/ppermute | solution.py:26
  93.3 9.8 %collective-permute-start.23 = (bf16[40,1152]{1,0:T(8,128)(2,1)S(1)}, bf16[40,1152]{1,0:T(8,128)(2,1)S(1)}, u32[]{:S(2)}, u32[]{:S(2)}) collective-permute-start(bf16[40,1152]{1,0:T(8,128)(2,1)S(1)} %get-tuple-element.40), channel_id=1, source_target_pairs={{0,128},{32,160},{64,192},{96,224},{128,0},{160,32},{192,64},{224,... | collective-permute-start | bytes 276488 | tf_op jit(solution)/shard_map/ppermute | solution.py:26
  96.0 12.9 %collective-permute-start.24 = (bf16[40,1152]{1,0:T(8,128)(2,1)S(1)}, bf16[40,1152]{1,0:T(8,128)(2,1)S(1)}, u32[]{:S(2)}, u32[]{:S(2)}) collective-permute-start(bf16[40,1152]{1,0:T(8,128)(2,1)S(1)} %get-tuple-element.39), channel_id=1, source_target_pairs={{0,96},{32,128},{64,160},{96,192},{128,224},{160,0},{192,32},{224,... | collective-permute-start | bytes 276488 | tf_op jit(solution)/shard_map/ppermute | solution.py:26
  97.2 16.3 %collective-permute-start.25 = (bf16[40,1152]{1,0:T(8,128)(2,1)S(1)}, bf16[40,1152]{1,0:T(8,128)(2,1)S(1)}, u32[]{:S(2)}, u32[]{:S(2)}) collective-permute-start(bf16[40,1152]{1,0:T(8,128)(2,1)S(1)} %get-tuple-element.38), channel_id=1, source_target_pairs={{0,64},{32,96},{64,128},{96,160},{128,192},{160,224},{192,0},{224,... | collective-permute-start | bytes 276488 | tf_op jit(solution)/shard_map/ppermute | solution.py:26
  100.8 13.8 %collective-permute-start.26 = (bf16[40,1152]{1,0:T(8,128)(2,1)S(1)}, bf16[40,1152]{1,0:T(8,128)(2,1)S(1)}, u32[]{:S(2)}, u32[]{:S(2)}) collective-permute-start(bf16[40,1152]{1,0:T(8,128)(2,1)S(1)} %get-tuple-element.37), channel_id=1, source_target_pairs={{0,32},{32,64},{64,96},{96,128},{128,160},{160,192},{192,224},{224... | collective-permute-start | bytes 276488 | tf_op jit(solution)/shard_map/ppermute | solution.py:26
  116.6 12.0 %all-to-all-start.2 = ((bf16[8,200,128]{2,1,0:T(8,128)(2,1)}), bf16[8,200,128]{2,1,0:T(8,128)(2,1)S(1)}, u32[]{:S(2)}, u32[]{:S(2)}) async-start(bf16[8,200,128]{2,1,0:T(8,128)(2,1)} %bitcast.20), calls=%async_computation.2 | async-start | bytes 819200 | tf_op jit(solution)/shard_map/all_to_all | solution.py:18
  130.2 7.3 %collective-permute-start.31 = (bf16[144,640]{1,0:T(8,128)(2,1)S(1)}, bf16[144,640]{1,0:T(8,128)(2,1)S(1)}, u32[]{:S(2)}, u32[]{:S(2)}) collective-permute-start(bf16[144,640]{1,0:T(8,128)(2,1)S(1)} %get-tuple-element.33), channel_id=1, source_target_pairs={{0,4},{4,8},{8,12},{12,0},{1,5},{5,9},{9,13},{13,1},{2,6},{6,10},{... | collective-permute-start | bytes 552968 | tf_op jit(solution)/shard_map/ppermute | solution.py:26
  131.8 9.4 %collective-permute-start.30 = (bf16[144,640]{1,0:T(8,128)(2,1)S(1)}, bf16[144,640]{1,0:T(8,128)(2,1)S(1)}, u32[]{:S(2)}, u32[]{:S(2)}) collective-permute-start(bf16[144,640]{1,0:T(8,128)(2,1)S(1)} %get-tuple-element.32), channel_id=1, source_target_pairs={{0,12},{4,0},{8,4},{12,8},{1,13},{5,1},{9,5},{13,9},{2,14},{6,2},{... | collective-permute-start | bytes 552968 | tf_op jit(solution)/shard_map/ppermute | solution.py:26
  134.4 14.8 %collective-permute-start.27 = (bf16[2,160,288]{2,1,0:T(8,128)(2,1)S(1)}, bf16[2,160,288]{2,1,0:T(8,128)(2,1)S(1)}, u32[]{:S(2)}, u32[]{:S(2)}) collective-permute-start(bf16[2,160,288]{2,1,0:T(8,128)(2,1)S(1)} %pad_maximum_fusion.9), channel_id=1, source_target_pairs={{0,1},{1,0},{2,3},{3,2},{4,5},{5,4},{6,7},{7,6},{8,9},{9,8},{10,11... | collective-permute-start | bytes 552968 | tf_op jit(solution)/shard_map/ppermute | solution.py:31
  137.6 6.8 %collective-permute-start.32 = (bf16[144,640]{1,0:T(8,128)(2,1)S(1)}, bf16[144,640]{1,0:T(8,128)(2,1)S(1)}, u32[]{:S(2)}, u32[]{:S(2)}) collective-permute-start(bf16[144,640]{1,0:T(8,128)(2,1)S(1)} %fusion.20), channel_id=1, source_target_pairs={{0,4},{4,8},{8,12},{12,0},{1,5},{5,9},{9,13},{13,1},{2,6},{6,10},{... | collective-permute-start | bytes 552968 | tf_op jit(solution)/shard_map/ppermute | solution.py:26
  138.0 11.2 %collective-permute-start.28 = (bf16[2,160,288]{2,1,0:T(8,128)(2,1)S(1)}, bf16[2,160,288]{2,1,0:T(8,128)(2,1)S(1)}, u32[]{:S(2)}, u32[]{:S(2)}) collective-permute-start(bf16[2,160,288]{2,1,0:T(8,128)(2,1)S(1)} %pad_maximum_fusion.10), channel_id=1, source_target_pairs={{0,2},{1,3},{2,0},{3,1},{4,6},{5,7},{6,4},{7,5},{8,10},{9,11},{10,... | collective-permute-start | bytes 552968 | tf_op jit(solution)/shard_map/ppermute | solution.py:31
  140.4 9.9 %collective-permute-start.29 = (bf16[2,160,288]{2,1,0:T(8,128)(2,1)S(1)}, bf16[2,160,288]{2,1,0:T(8,128)(2,1)S(1)}, u32[]{:S(2)}, u32[]{:S(2)}) collective-permute-start(bf16[2,160,288]{2,1,0:T(8,128)(2,1)S(1)} %pad_maximum_fusion.11), channel_id=1, source_target_pairs={{0,3},{1,2},{2,1},{3,0},{4,7},{5,6},{6,5},{7,4},{8,11},{9,10},{10,... | collective-permute-start | bytes 552968 | tf_op jit(solution)/shard_map/ppermute | solution.py:31
  145.2 14.5 %all-to-all-start.3 = ((bf16[8,18,640]{2,1,0:T(8,128)(2,1)}), bf16[8,18,640]{2,1,0:T(8,128)(2,1)S(1)}, u32[]{:S(2)}, u32[]{:S(2)}) async-start(bf16[8,18,640]{2,1,0:T(8,128)(2,1)} %reshape.151), calls=%async_computation.3 | async-start | bytes 491520 | tf_op jit(solution)/shard_map/all_to_all | solution.py:18
  (23 other events, 232.2 us)

commit v3 on v2

--- a/solution.py
+++ b/solution.py
@@ -125,11 +125,12 @@
     col = jnp.arange(576, dtype=jnp.int32)
     source = (col % 144) // 18 * 144 + col // 144 * 18 + col % 18
 
-    def pick(half):
+    def pick(half, rows):
         chosen = jnp.arange(1152, dtype=jnp.int32)[:, None] == (source + 72 * half)[None, :]
-        return jnp.dot(stacked, chosen.astype(BF), preferred_element_type=F32).astype(BF)
-
-    keep, give = pick(xl), pick(1 - xl)
+        return jnp.dot(rows, chosen.astype(BF), preferred_element_type=F32).astype(BF)
+
+    keep = pick(xl, stacked)
+    give = pick(1 - xl, lax.dynamic_slice_in_dim(stacked, c * 160, 160, 0))
     own = rows_from_slices(jnp.stack([p_img, p_txt]), xh, c)
     r = lax.rsqrt(jnp.sum(own * own, axis=2, keepdims=True) + 1e-06)
     z = (own * r).astype(BF)
@@ -140,29 +141,36 @@
     img = jnp.broadcast_to(z_img[None], (16, 40, 1152))
     img, z_near = lax.optimization_barrier((img, z_txt))
     img = a2a(img, PLANE).reshape(640, 1152)
-    come = lax.ppermute(give, "xl", [(0, 1), (1, 0)])
     up, down = [z_near], [z_near]
     for d in range(3):
         up.append(shift(up[-1], "z", 8, 1))
         down.append(shift(down[-1], "z", 8, -1))
-        if d == 1:
-            up[2], come = lax.optimization_barrier((up[2], come))
     up.append(shift(up[-1], "z", 8, 1))
     txt_own = up + down[:0:-1]
     txt_oth = [swap_core(piece) for piece in txt_own]
+    give, img = lax.optimization_barrier((give, img))
+    come = lax.ppermute(give, "xl", [(0, 1), (1, 0)])
+    place = (xl * 4 + y) * 2 + xh
+    scalars = jnp.concatenate([jnp.exp(log_scale), bias])
+    t_oth, t_own, g_img = block_grads(scalars, place.astype(jnp.int32).reshape(1), img, txt_oth + txt_own)
+    t_oth, come = lax.optimization_barrier((t_oth, come))
+    t_got = swap_core(t_oth)
+    come_oth = swap_core(come)
+    come = jnp.concatenate([jnp.where(c == 0, come, come_oth), jnp.where(c == 0, come_oth, come)])
     first, second = jnp.where(xl == 0, keep, come), jnp.where(xl == 0, come, keep)
     fi = jnp.concatenate([first[:160], second[:160]])
     ft = jnp.concatenate([first[160:], second[160:]])
 
-    place = (xl * 4 + y) * 2 + xh
-    scalars = jnp.concatenate([jnp.exp(log_scale), bias])
-    t_oth, t_own, g_img = block_grads(scalars, place.astype(jnp.int32).reshape(1), img, txt_oth + txt_own)
-    t_got = swap_core(t_oth)
     t_sum = t_own + t_got.astype(F32)
-    t_out = t_sum[40:].astype(BF)
-    gz_txt = t_sum[:40]
-    for d in range(1, 8):
-        gz_txt = gz_txt + shift(t_out[40 * d - 40 : 40 * d], "z", 8, -d).astype(F32)
+    to = {k: t_sum[40 * (-k % 8) : 40 * (-k % 8) + 40] for k in range(-3, 5)}
+    far_up = shift(jnp.concatenate([to[4], to[3]]).astype(BF), "z", 8, 2).astype(F32)
+    far_down = shift(jnp.concatenate([to[-3], to[-2]]).astype(BF), "z", 8, -2).astype(F32)
+    near = [
+        shift((to[2] + far_up[:40]).astype(BF), "z", 8, 2),
+        shift((to[1] + far_up[40:]).astype(BF), "z", 8, 1),
+        shift((to[-1] + far_down[:40]).astype(BF), "z", 8, -1),
+    ]
+    gz_txt = to[0] + far_down[40:] + near[0].astype(F32) + near[1].astype(F32) + near[2].astype(F32)
     g_img = g_img.reshape(16, 40, 1152)
     gz_img = jnp.sum(a2a(g_img, PLANE).astype(F32), axis=0)
 
@@ -192,11 +200,12 @@
         ],
         axis=1,
     ).reshape(4, 144, 640)
-    up = lax.dynamic_index_in_dim(w, (y + 2) % 4, 0, keepdims=False).astype(BF)
-    down = lax.dynamic_index_in_dim(w, (y + 3) % 4, 0, keepdims=False).astype(BF)
-    up = shift(up, "y", 4, 1).astype(F32) + lax.dynamic_index_in_dim(w, (y + 1) % 4, 0, keepdims=False)
-    w = lax.dynamic_index_in_dim(w, y, 0, keepdims=False) + shift(down, "y", 4, -1).astype(F32)
-    w = w + shift(up.astype(BF), "y", 4, 1).astype(F32)
+    def block(k):
+        return lax.dynamic_index_in_dim(w, (y + k) % 4, 0, keepdims=False)
+
+    up, down = shift(block(2).astype(BF), "y", 4, 1), shift(block(3).astype(BF), "y", 4, -1)
+    up = shift((up.astype(F32) + block(1)).astype(BF), "y", 4, 1)
+    w = block(0) + down.astype(F32) + up.astype(F32)
     w = jnp.sum(a2a(w.astype(BF).reshape(8, 18, 640), ("z",)).astype(F32), axis=0)
     w_img = jnp.concatenate([w[:, :256], w[:, 512:544]], axis=1)
     w_txt = jnp.concatenate([w[:, 256:512], w[:, 544:576]], axis=1)

time: 163 us -> 142 us (0.87)
  waiting for transfers between devices: 61.3 us -> 51.3 us
  starting transfers between devices: 66 us -> 56.6 us
  local copies, waits for them, and re-layouts: 8.88 us -> 6.57 us
    ppermute x1, waiting for transfers between devices: 13 us -> 0.01 us  [shards(): come = lax.ppermute(give, 'xl', [(0, 1), (1, 0)])]
    ppermute x17 -> x15, starting transfers between devices: 33.4 us -> 23.3 us  [shift(): return lax.ppermute(x, axis, [(i, (i + step) % size) for i in range(size)])]
    unnamed x37 -> x33, local copies, waits for them, and re-layouts: 3.53 us -> 1.23 us
    ppermute x17 -> x15, waiting for transfers between devices: 27.9 us -> 30.2 us  [shift(): return lax.ppermute(x, axis, [(i, (i + step) % size) for i in range(size)])]
  transfers between devices with their start and end apart: 37 -> 36, of which waited for: 16 -> 14; matrix products, arithmetic and copies ran while one was open for 7% -> 8% of each run, Pallas kernels for 0% -> 5%
where the time goes in v3:
time: 142 us; the launch traced here: 140 us
  starting transfers between devices  56.6 us (40%)
  waiting for transfers between devices  51.3 us (36%)
  matrix products  8.16 us (6%)
  Pallas kernels  7.65 us (5%)
  other arithmetic  7.41 us (5%)
  local copies, waits for them, and re-layouts  6.57 us (5%)
  between operations  2.61 us (2%)
    ppermute x15, waiting for transfers between devices, shift(): return lax.ppermute(x, axis, [(i, (i + step) % size) for i in range(size)])  30.2 us
    all_to_all x4, starting transfers between devices, a2a(): return lax.all_to_all(x, axes, 0, 0, tiled=True)  25 us
    ppermute x15, starting transfers between devices, shift(): return lax.ppermute(x, axis, [(i, (i + step) % size) for i in range(size)])  23.3 us
    all_to_all x4, waiting for transfers between devices, a2a(): return lax.all_to_all(x, axes, 0, 0, tiled=True)  16.6 us
    pallas_call x1, Pallas kernels, block_grads(): pl.pallas_call(block_kernel, out_shape=[jax.ShapeDtypeStruct((320, 1152),...  7.65 us
    ppermute x6, starting transfers between devices, mp_shift(): return lax.ppermute(x, MP, pairs)  5.28 us
    ppermute x6, waiting for transfers between devices, mp_shift(): return lax.ppermute(x, MP, pairs)  3.97 us
  transfers between devices with their start and end apart: 36, of which 14 were waited for; matrix products, arithmetic and copies ran while one was open for 8% of the time, Pallas kernels for 5%

profile of v3, /device:TPU:2, one launch (start us, length us, event | category | flops | bytes accessed | tf_op | source)
XLA Modules:
  0.0 140.3 jit_solution(7480424504030816446)
XLA Ops:
  1.7 1.5 %fusion.104 = f32[160,288]{1,0:T(8,128)S(1)} fusion(bf16[160,1152]{1,0:T(8,128)(2,1)} %param.6, bf16[1152,288]{0,1:T(8,128)(2,1)S(1)} %copy-done), kind=kOutput, calls=%fused_computation.189 | convolution fusion | flops 106168320 | bytes 1216512 | tf_op jit(solution)/shard_map/dot_general | solution.py:122
  4.4 2.1 %collective-permute-start.1 = (f32[2,40,288]{2,1,0:T(8,128)}, f32[2,40,288]{2,1,0:T(8,128)S(1)}, u32[]{:S(2)}, u32[]{:S(2)}) collective-permute-start(f32[2,40,288]{2,1,0:T(8,128)} %get-tuple-element.52), channel_id=1, source_target_pairs={{0,2},{1,3},{2,0},{3,1},{4,6},{5,7},{6,4},{7,5},{8,10},{9,11},{10,... | collective-permute-start | bytes 276488 | tf_op jit(solution)/shard_map/ppermute | solution.py:31
  8.7 1.4 fusion.10
  10.1 2.1 %collective-permute-done.1 = f32[2,40,288]{2,1,0:T(8,128)S(1)} collective-permute-done((f32[2,40,288]{2,1,0:T(8,128)}, f32[2,40,288]{2,1,0:T(8,128)S(1)}, u32[]{:S(2)}, u32[]{:S(2)}) %collective-permute-start.1) | collective-permute-done | bytes 92192 | tf_op jit(solution)/shard_map/ppermute | solution.py:31
  12.2 1.9 %collective-permute-done.2 = f32[2,40,288]{2,1,0:T(8,128)S(1)} collective-permute-done((f32[2,40,288]{2,1,0:T(8,128)S(1)}, f32[2,40,288]{2,1,0:T(8,128)S(1)}, u32[]{:S(2)}, u32[]{:S(2)}) %collective-permute-start.2) | collective-permute-done | bytes 92192 | tf_op jit(solution)/shard_map/ppermute | solution.py:31
  14.7 1.2 broadcast_in_dim.37
  15.9 7.6 %all-to-all-start = ((bf16[16,40,1152]{2,1,0:T(8,128)(2,1)}), bf16[16,40,1152]{2,1,0:T(8,128)(2,1)S(1)}, u32[]{:S(2)}, u32[]{:S(2)}) async-start(bf16[16,40,1152]{2,1,0:T(8,128)(2,1)} %broadcast_in_dim.37), calls=%async_computation | async-start | bytes 2949120 | tf_op jit(solution)/shard_map/all_to_all | solution.py:18
  23.5 1.9 %collective-permute-start.4 = (bf16[40,1152]{1,0:T(8,128)(2,1)S(1)}, bf16[40,1152]{1,0:T(8,128)(2,1)S(1)}, u32[]{:S(2)}, u32[]{:S(2)}) collective-permute-start(bf16[40,1152]{1,0:T(8,128)(2,1)S(1)} %get-tuple-element.24.refs_8_), channel_id=1, source_target_pairs={{0,32},{32,64},{64,96},{96,128},{128,160},{160,192},{192,224},{224... | collective-permute-start | bytes 276488 | tf_op jit(solution)/shard_map/ppermute | solution.py:26
  25.4 4.0 %collective-permute-start.12 = (bf16[40,1152]{1,0:T(8,128)(2,1)S(1)}, bf16[40,1152]{1,0:T(8,128)(2,1)S(1)}, u32[]{:S(2)}, u32[]{:S(2)}) collective-permute-start(bf16[40,1152]{1,0:T(8,128)(2,1)S(1)} %get-tuple-element.24.refs_8_), channel_id=1, source_target_pairs={{0,224},{32,0},{64,32},{96,64},{128,96},{160,128},{192,160},{224,1... | collective-permute-start | bytes 276488 | tf_op jit(solution)/shard_map/ppermute | solution.py:26
  29.5 2.4 %collective-permute-done.4.refs_9_ = bf16[40,1152]{1,0:T(8,128)(2,1)S(1)} collective-permute-done((bf16[40,1152]{1,0:T(8,128)(2,1)S(1)}, bf16[40,1152]{1,0:T(8,128)(2,1)S(1)}, u32[]{:S(2)}, u32[]{:S(2)}) %collective-permute-start.4) | collective-permute-done | bytes 92192 | tf_op jit(solution)/shard_map/ppermute | solution.py:26
  31.9 3.3 %collective-permute-start.13 = (bf16[40,1152]{1,0:T(8,128)(2,1)S(1)}, bf16[40,1152]{1,0:T(8,128)(2,1)S(1)}, u32[]{:S(2)}, u32[]{:S(2)}) collective-permute-start(bf16[40,1152]{1,0:T(8,128)(2,1)S(1)} %collective-permute-done.12.refs_15_), channel_id=1, source_target_pairs={{0,224},{32,0},{64,32},{96,64},{128,96},{160,128},{192,160},{224,1... | collective-permute-start | bytes 276488 | tf_op jit(solution)/shard_map/ppermute | solution.py:26
  35.2 2.4 %collective-permute-done.6.refs_10_ = bf16[40,1152]{1,0:T(8,128)(2,1)S(1)} collective-permute-done((bf16[40,1152]{1,0:T(8,128)(2,1)S(1)}, bf16[40,1152]{1,0:T(8,128)(2,1)S(1)}, u32[]{:S(2)}, u32[]{:S(2)}) %collective-permute-start.6) | collective-permute-done | bytes 92192 | tf_op jit(solution)/shard_map/ppermute | solution.py:26
  38.4 3.1 %collective-permute-start.14 = (bf16[40,1152]{1,0:T(8,128)(2,1)S(1)}, bf16[40,1152]{1,0:T(8,128)(2,1)}, u32[]{:S(2)}, u32[]{:S(2)}) collective-permute-start(bf16[40,1152]{1,0:T(8,128)(2,1)S(1)} %collective-permute-done.13.refs_14_), channel_id=1, source_target_pairs={{0,224},{32,0},{64,32},{96,64},{128,96},{160,128},{192,160},{224,1... | collective-permute-start | bytes 276488 | tf_op jit(solution)/shard_map/ppermute | solution.py:26
  41.5 1.9 %collective-permute-done.8.refs_11_ = bf16[40,1152]{1,0:T(8,128)(2,1)S(1)} collective-permute-done((bf16[40,1152]{1,0:T(8,128)(2,1)S(1)}, bf16[40,1152]{1,0:T(8,128)(2,1)S(1)}, u32[]{:S(2)}, u32[]{:S(2)}) %collective-permute-start.8) | collective-permute-done | bytes 92192 | tf_op jit(solution)/shard_map/ppermute | solution.py:26
  46.1 3.2 %collective-permute-done.10.refs_12_ = bf16[40,1152]{1,0:T(8,128)(2,1)} collective-permute-done((bf16[40,1152]{1,0:T(8,128)(2,1)S(1)}, bf16[40,1152]{1,0:T(8,128)(2,1)}, u32[]{:S(2)}, u32[]{:S(2)}) %collective-permute-start.10) | collective-permute-done | bytes 92192 | tf_op jit(solution)/shard_map/ppermute | solution.py:26
  51.0 7.7 %shard_map.93 = (bf16[320,1152]{1,0:T(8,128)(2,1)}, f32[320,1152]{1,0:T(8,128)}, bf16[640,1152]{1,0:T(8,128)(2,1)}) custom-call(f32[2]{0:T(128)} %pad_maximum_fusion.18.scalars, s32[1]{0:T(128)} %bitcast.8.place, bf16[640,1152]{1,0:T(8,128)(2,1)} %bitcast.96, bf16[40,1152]{1,0:T(8,128)(2,1)} %collective-permute-done.3.refs_0_, ...), custom_call_target="tpu_custom_call" | custom-call | flops 2900000000 | bytes 8000000 | tf_op jit(solution)/shard_map/pallas_call | solution.py:94
  60.5 7.2 %all-to-all-start.1 = ((bf16[16,40,1152]{2,1,0:T(8,128)(2,1)}), bf16[16,40,1152]{2,1,0:T(8,128)(2,1)S(1)}, u32[]{:S(2)}, u32[]{:S(2)}) async-start(bf16[16,40,1152]{2,1,0:T(8,128)(2,1)} %bitcast.95), calls=%async_computation.1 | async-start | bytes 2949120 | tf_op jit(solution)/shard_map/all_to_all | solution.py:18
  67.8 1.6 %fusion.94 = (bf16[320,1152]{1,0:T(8,128)(2,1)S(1)}, f32[320,1152]{1,0:T(8,128)S(1)}) fusion(f32[320,1152]{1,0:T(8,128)} %get-tuple-element.26, bf16[320,1152]{1,0:T(8,128)(2,1)S(1)} %collective-permute-done.19), kind=kLoop, calls=%fused_computation.180 | loop fusion | flops 1105920 | bytes 4423680 | tf_op jit(solution)/shard_map/convert.16
  69.5 2.9 %collective-permute-start.21 = (bf16[80,1152]{1,0:T(8,128)(2,1)S(1)}, bf16[80,1152]{1,0:T(8,128)(2,1)S(1)}, u32[]{:S(2)}, u32[]{:S(2)}) collective-permute-start(bf16[80,1152]{1,0:T(8,128)(2,1)S(1)} %concatenate.70), channel_id=1, source_target_pairs={{0,64},{32,96},{64,128},{96,160},{128,192},{160,224},{192,0},{224,... | collective-permute-start | bytes 552968 | tf_op jit(solution)/shard_map/ppermute | solution.py:26
  73.4 7.3 %collective-permute-done.20 = bf16[80,1152]{1,0:T(8,128)(2,1)S(1)} collective-permute-done((bf16[80,1152]{1,0:T(8,128)(2,1)S(1)}, bf16[80,1152]{1,0:T(8,128)(2,1)S(1)}, u32[]{:S(2)}, u32[]{:S(2)}) %collective-permute-start.20) | collective-permute-done | bytes 184352 | tf_op jit(solution)/shard_map/ppermute | solution.py:26
  80.7 2.4 %collective-permute-done.21 = bf16[80,1152]{1,0:T(8,128)(2,1)S(1)} collective-permute-done((bf16[80,1152]{1,0:T(8,128)(2,1)S(1)}, bf16[80,1152]{1,0:T(8,128)(2,1)S(1)}, u32[]{:S(2)}, u32[]{:S(2)}) %collective-permute-start.21) | collective-permute-done | bytes 184352 | tf_op jit(solution)/shard_map/ppermute | solution.py:26
  84.6 2.9 %collective-permute-start.24 = (bf16[40,1152]{1,0:T(8,128)(2,1)S(1)}, bf16[40,1152]{1,0:T(8,128)(2,1)S(1)}, u32[]{:S(2)}, u32[]{:S(2)}) collective-permute-start(bf16[40,1152]{1,0:T(8,128)(2,1)S(1)} %get-tuple-element.40), channel_id=1, source_target_pairs={{0,224},{32,0},{64,32},{96,64},{128,96},{160,128},{192,160},{224,1... | collective-permute-start | bytes 276488 | tf_op jit(solution)/shard_map/ppermute | solution.py:26
  87.6 4.9 %collective-permute-done.22 = bf16[40,1152]{1,0:T(8,128)(2,1)S(1)} collective-permute-done((bf16[40,1152]{1,0:T(8,128)(2,1)S(1)}, bf16[40,1152]{1,0:T(8,128)(2,1)S(1)}, u32[]{:S(2)}, u32[]{:S(2)}) %collective-permute-start.22) | collective-permute-done | bytes 92192 | tf_op jit(solution)/shard_map/ppermute | solution.py:26
  94.5 4.9 %all-to-all-start.2 = ((bf16[8,200,128]{2,1,0:T(8,128)(2,1)}), bf16[8,200,128]{2,1,0:T(8,128)(2,1)S(1)}, u32[]{:S(2)}, u32[]{:S(2)}) async-start(bf16[8,200,128]{2,1,0:T(8,128)(2,1)} %bitcast.20), calls=%async_computation.2 | async-start | bytes 819200 | tf_op jit(solution)/shard_map/all_to_all | solution.py:18
  99.5 7.0 %all-to-all-done.2 = bf16[8,200,128]{2,1,0:T(8,128)(2,1)S(1)} async-done(((bf16[8,200,128]{2,1,0:T(8,128)(2,1)}), bf16[8,200,128]{2,1,0:T(8,128)(2,1)S(1)}, u32[]{:S(2)}, u32[]{:S(2)}) %all-to-all-start.2) | async-done | bytes 409632 | tf_op jit(solution)/shard_map/all_to_all | solution.py:18
  108.1 1.5 %collective-permute-start.30 = (bf16[144,640]{1,0:T(8,128)(2,1)S(1)}, bf16[144,640]{1,0:T(8,128)(2,1)S(1)}, u32[]{:S(2)}, u32[]{:S(2)}) collective-permute-start(bf16[144,640]{1,0:T(8,128)(2,1)S(1)} %get-tuple-element.39), channel_id=1, source_target_pairs={{0,4},{4,8},{8,12},{12,0},{1,5},{5,9},{9,13},{13,1},{2,6},{6,10},{... | collective-permute-start | bytes 552968 | tf_op jit(solution)/shard_map/ppermute | solution.py:26
  109.7 1.8 %collective-permute-start.29 = (bf16[144,640]{1,0:T(8,128)(2,1)S(1)}, bf16[144,640]{1,0:T(8,128)(2,1)S(1)}, u32[]{:S(2)}, u32[]{:S(2)}) collective-permute-start(bf16[144,640]{1,0:T(8,128)(2,1)S(1)} %get-tuple-element.38), channel_id=1, source_target_pairs={{0,12},{4,0},{8,4},{12,8},{1,13},{5,1},{9,5},{13,9},{2,14},{6,2},{... | collective-permute-start | bytes 552968 | tf_op jit(solution)/shard_map/ppermute | solution.py:26
  113.1 2.4 %collective-permute-done.30 = bf16[144,640]{1,0:T(8,128)(2,1)S(1)} collective-permute-done((bf16[144,640]{1,0:T(8,128)(2,1)S(1)}, bf16[144,640]{1,0:T(8,128)(2,1)S(1)}, u32[]{:S(2)}, u32[]{:S(2)}) %collective-permute-start.30) | collective-permute-done | bytes 184352 | tf_op jit(solution)/shard_map/ppermute | solution.py:26
  115.9 1.7 %collective-permute-start.26 = (bf16[2,160,288]{2,1,0:T(8,128)(2,1)S(1)}, bf16[2,160,288]{2,1,0:T(8,128)(2,1)S(1)}, u32[]{:S(2)}, u32[]{:S(2)}) collective-permute-start(bf16[2,160,288]{2,1,0:T(8,128)(2,1)S(1)} %pad_maximum_fusion.11), channel_id=1, source_target_pairs={{0,2},{1,3},{2,0},{3,1},{4,6},{5,7},{6,4},{7,5},{8,10},{9,11},{10,... | collective-permute-start | bytes 552968 | tf_op jit(solution)/shard_map/ppermute | solution.py:31
  119.1 3.2 %collective-permute-done.31 = bf16[144,640]{1,0:T(8,128)(2,1)S(1)} collective-permute-done((bf16[144,640]{1,0:T(8,128)(2,1)S(1)}, bf16[144,640]{1,0:T(8,128)(2,1)S(1)}, u32[]{:S(2)}, u32[]{:S(2)}) %collective-permute-start.31) | collective-permute-done | bytes 184352 | tf_op jit(solution)/shard_map/ppermute | solution.py:26
  123.2 5.2 %all-to-all-start.3 = ((bf16[8,18,640]{2,1,0:T(8,128)(2,1)}), bf16[8,18,640]{2,1,0:T(8,128)(2,1)S(1)}, u32[]{:S(2)}, u32[]{:S(2)}) async-start(bf16[8,18,640]{2,1,0:T(8,128)(2,1)} %reshape.151), calls=%async_computation.3 | async-start | bytes 491520 | tf_op jit(solution)/shard_map/all_to_all | solution.py:18
  129.3 9.6 %all-to-all-done.3 = bf16[8,18,640]{2,1,0:T(8,128)(2,1)S(1)} async-done(((bf16[8,18,640]{2,1,0:T(8,128)(2,1)}), bf16[8,18,640]{2,1,0:T(8,128)(2,1)S(1)}, u32[]{:S(2)}, u32[]{:S(2)}) %all-to-all-start.3) | async-done | bytes 184352 | tf_op jit(solution)/shard_map/all_to_all | solution.py:18
  (144 shorter events, 23.3 us)
Async XLA Ops:
  4.4 5.7 %collective-permute-start = (f32[2,40,288]{2,1,0:T(8,128)}, f32[2,40,288]{2,1,0:T(8,128)S(1)}, u32[]{:S(2)}, u32[]{:S(2)}) collective-permute-start(f32[2,40,288]{2,1,0:T(8,128)} %get-tuple-element.51), channel_id=1, source_target_pairs={{0,1},{1,0},{2,3},{3,2},{4,5},{5,4},{6,7},{7,6},{8,9},{9,8},{10,11... | collective-permute-start | bytes 276488 | tf_op jit(solution)/shard_map/ppermute | solution.py:31
  4.4 7.8 %collective-permute-start.1 = (f32[2,40,288]{2,1,0:T(8,128)}, f32[2,40,288]{2,1,0:T(8,128)S(1)}, u32[]{:S(2)}, u32[]{:S(2)}) collective-permute-start(f32[2,40,288]{2,1,0:T(8,128)} %get-tuple-element.52), channel_id=1, source_target_pairs={{0,2},{1,3},{2,0},{3,1},{4,6},{5,7},{6,4},{7,5},{8,10},{9,11},{10,... | collective-permute-start | bytes 276488 | tf_op jit(solution)/shard_map/ppermute | solution.py:31
  6.5 7.6 %collective-permute-start.2 = (f32[2,40,288]{2,1,0:T(8,128)S(1)}, f32[2,40,288]{2,1,0:T(8,128)S(1)}, u32[]{:S(2)}, u32[]{:S(2)}) collective-permute-start(f32[2,40,288]{2,1,0:T(8,128)S(1)} %get-tuple-element.50), channel_id=1, source_target_pairs={{0,3},{1,2},{2,1},{3,0},{4,7},{5,6},{6,5},{7,4},{8,11},{9,10},{10,... | collective-permute-start | bytes 276488 | tf_op jit(solution)/shard_map/ppermute | solution.py:31
  15.9 34.0 %all-to-all-start = ((bf16[16,40,1152]{2,1,0:T(8,128)(2,1)}), bf16[16,40,1152]{2,1,0:T(8,128)(2,1)S(1)}, u32[]{:S(2)}, u32[]{:S(2)}) async-start(bf16[16,40,1152]{2,1,0:T(8,128)(2,1)} %broadcast_in_dim.37), calls=%async_computation | async-start | bytes 2949120 | tf_op jit(solution)/shard_map/all_to_all | solution.py:18
  23.5 8.4 %collective-permute-start.4 = (bf16[40,1152]{1,0:T(8,128)(2,1)S(1)}, bf16[40,1152]{1,0:T(8,128)(2,1)S(1)}, u32[]{:S(2)}, u32[]{:S(2)}) collective-permute-start(bf16[40,1152]{1,0:T(8,128)(2,1)S(1)} %get-tuple-element.24.refs_8_), channel_id=1, source_target_pairs={{0,32},{32,64},{64,96},{96,128},{128,160},{160,192},{192,224},{224... | collective-permute-start | bytes 276488 | tf_op jit(solution)/shard_map/ppermute | solution.py:26
  25.4 6.5 %collective-permute-start.12 = (bf16[40,1152]{1,0:T(8,128)(2,1)S(1)}, bf16[40,1152]{1,0:T(8,128)(2,1)S(1)}, u32[]{:S(2)}, u32[]{:S(2)}) collective-permute-start(bf16[40,1152]{1,0:T(8,128)(2,1)S(1)} %get-tuple-element.24.refs_8_), channel_id=1, source_target_pairs={{0,224},{32,0},{64,32},{96,64},{128,96},{160,128},{192,160},{224,1... | collective-permute-start | bytes 276488 | tf_op jit(solution)/shard_map/ppermute | solution.py:26
  31.9 5.8 %collective-permute-start.6 = (bf16[40,1152]{1,0:T(8,128)(2,1)S(1)}, bf16[40,1152]{1,0:T(8,128)(2,1)S(1)}, u32[]{:S(2)}, u32[]{:S(2)}) collective-permute-start(bf16[40,1152]{1,0:T(8,128)(2,1)S(1)} %collective-permute-done.4.refs_9_), channel_id=1, source_target_pairs={{0,32},{32,64},{64,96},{96,128},{128,160},{160,192},{192,224},{224... | collective-permute-start | bytes 276488 | tf_op jit(solution)/shard_map/ppermute | solution.py:26
  31.9 6.5 %collective-permute-start.13 = (bf16[40,1152]{1,0:T(8,128)(2,1)S(1)}, bf16[40,1152]{1,0:T(8,128)(2,1)S(1)}, u32[]{:S(2)}, u32[]{:S(2)}) collective-permute-start(bf16[40,1152]{1,0:T(8,128)(2,1)S(1)} %collective-permute-done.12.refs_15_), channel_id=1, source_target_pairs={{0,224},{32,0},{64,32},{96,64},{128,96},{160,128},{192,160},{224,1... | collective-permute-start | bytes 276488 | tf_op jit(solution)/shard_map/ppermute | solution.py:26
  37.7 5.8 %collective-permute-start.8 = (bf16[40,1152]{1,0:T(8,128)(2,1)S(1)}, bf16[40,1152]{1,0:T(8,128)(2,1)S(1)}, u32[]{:S(2)}, u32[]{:S(2)}) collective-permute-start(bf16[40,1152]{1,0:T(8,128)(2,1)S(1)} %collective-permute-done.6.refs_10_), channel_id=1, source_target_pairs={{0,32},{32,64},{64,96},{96,128},{128,160},{160,192},{192,224},{224... | collective-permute-start | bytes 276488 | tf_op jit(solution)/shard_map/ppermute | solution.py:26
  37.7 7.1 %collective-permute-start.3 = (bf16[40,1152]{1,0:T(8,128)(2,1)S(1)}, bf16[40,1152]{1,0:T(8,128)(2,1)}, u32[]{:S(2)}, u32[]{:S(2)}) collective-permute-start(bf16[40,1152]{1,0:T(8,128)(2,1)S(1)} %get-tuple-element.24.refs_8_), channel_id=1, source_target_pairs={{0,1},{1,0},{2,3},{3,2},{4,5},{5,4},{6,7},{7,6},{8,9},{9,8},{10,11... | collective-permute-start | bytes 276488 | tf_op jit(solution)/shard_map/ppermute | solution.py:22
  37.8 7.3 %collective-permute-start.17 = (bf16[40,1152]{1,0:T(8,128)(2,1)S(1)}, bf16[40,1152]{1,0:T(8,128)(2,1)}, u32[]{:S(2)}, u32[]{:S(2)}) collective-permute-start(bf16[40,1152]{1,0:T(8,128)(2,1)S(1)} %collective-permute-done.12.refs_15_), channel_id=1, source_target_pairs={{0,1},{1,0},{2,3},{3,2},{4,5},{5,4},{6,7},{7,6},{8,9},{9,8},{10,11... | collective-permute-start | bytes 276488 | tf_op jit(solution)/shard_map/ppermute | solution.py:22
  38.3 7.3 %collective-permute-start.5 = (bf16[40,1152]{1,0:T(8,128)(2,1)S(1)}, bf16[40,1152]{1,0:T(8,128)(2,1)}, u32[]{:S(2)}, u32[]{:S(2)}) collective-permute-start(bf16[40,1152]{1,0:T(8,128)(2,1)S(1)} %collective-permute-done.4.refs_9_), channel_id=1, source_target_pairs={{0,1},{1,0},{2,3},{3,2},{4,5},{5,4},{6,7},{7,6},{8,9},{9,8},{10,11... | collective-permute-start | bytes 276488 | tf_op jit(solution)/shard_map/ppermute | solution.py:22
  38.4 7.3 %collective-permute-start.14 = (bf16[40,1152]{1,0:T(8,128)(2,1)S(1)}, bf16[40,1152]{1,0:T(8,128)(2,1)}, u32[]{:S(2)}, u32[]{:S(2)}) collective-permute-start(bf16[40,1152]{1,0:T(8,128)(2,1)S(1)} %collective-permute-done.13.refs_14_), channel_id=1, source_target_pairs={{0,224},{32,0},{64,32},{96,64},{128,96},{160,128},{192,160},{224,1... | collective-permute-start | bytes 276488 | tf_op jit(solution)/shard_map/ppermute | solution.py:26
  43.4 5.9 %collective-permute-start.10 = (bf16[40,1152]{1,0:T(8,128)(2,1)S(1)}, bf16[40,1152]{1,0:T(8,128)(2,1)}, u32[]{:S(2)}, u32[]{:S(2)}) collective-permute-start(bf16[40,1152]{1,0:T(8,128)(2,1)S(1)} %collective-permute-done.8.refs_11_), channel_id=1, source_target_pairs={{0,32},{32,64},{64,96},{96,128},{128,160},{160,192},{192,224},{224... | collective-permute-start | bytes 276488 | tf_op jit(solution)/shard_map/ppermute | solution.py:26
  44.8 5.1 %collective-permute-start.16 = (bf16[40,1152]{1,0:T(8,128)(2,1)S(1)}, bf16[40,1152]{1,0:T(8,128)(2,1)S(1)}, u32[]{:S(2)}, u32[]{:S(2)}) collective-permute-start(bf16[40,1152]{1,0:T(8,128)(2,1)S(1)} %collective-permute-done.13.refs_14_), channel_id=1, source_target_pairs={{0,1},{1,0},{2,3},{3,2},{4,5},{5,4},{6,7},{7,6},{8,9},{9,8},{10,11... | collective-permute-start | bytes 276488 | tf_op jit(solution)/shard_map/ppermute | solution.py:22
  45.1 5.3 %collective-permute-start.7 = (bf16[40,1152]{1,0:T(8,128)(2,1)S(1)}, bf16[40,1152]{1,0:T(8,128)(2,1)}, u32[]{:S(2)}, u32[]{:S(2)}) collective-permute-start(bf16[40,1152]{1,0:T(8,128)(2,1)S(1)} %collective-permute-done.6.refs_10_), channel_id=1, source_target_pairs={{0,1},{1,0},{2,3},{3,2},{4,5},{5,4},{6,7},{7,6},{8,9},{9,8},{10,11... | collective-permute-start | bytes 276488 | tf_op jit(solution)/shard_map/ppermute | solution.py:22
  49.9 8.8 %collective-permute-start.18 = (bf16[160,576]{1,0:T(8,128)(2,1)S(1)}, bf16[160,576]{1,0:T(8,128)(2,1)}, u32[]{:S(2)}, u32[]{:S(2)}) collective-permute-start(bf16[160,576]{1,0:T(8,128)(2,1)S(1)} %copy-done.9), channel_id=1, source_target_pairs={{0,16},{16,0},{1,17},{17,1},{2,18},{18,2},{3,19},{19,3},{4,20},{20... | collective-permute-start | bytes 552968 | tf_op jit(solution)/shard_map/ppermute | solution.py:152
  58.7 9.0 %collective-permute-start.19 = (bf16[320,1152]{1,0:T(8,128)(2,1)}, bf16[320,1152]{1,0:T(8,128)(2,1)S(1)}, u32[]{:S(2)}, u32[]{:S(2)}) collective-permute-start(bf16[320,1152]{1,0:T(8,128)(2,1)} %get-tuple-element.29), channel_id=1, source_target_pairs={{0,1},{1,0},{2,3},{3,2},{4,5},{5,4},{6,7},{7,6},{8,9},{9,8},{10,11... | collective-permute-start | bytes 2211848 | tf_op jit(solution)/shard_map/ppermute | solution.py:22
  60.5 32.1 %all-to-all-start.1 = ((bf16[16,40,1152]{2,1,0:T(8,128)(2,1)}), bf16[16,40,1152]{2,1,0:T(8,128)(2,1)S(1)}, u32[]{:S(2)}, u32[]{:S(2)}) async-start(bf16[16,40,1152]{2,1,0:T(8,128)(2,1)} %bitcast.95), calls=%async_computation.1 | async-start | bytes 2949120 | tf_op jit(solution)/shard_map/all_to_all | solution.py:18
  69.4 11.3 %collective-permute-start.20 = (bf16[80,1152]{1,0:T(8,128)(2,1)S(1)}, bf16[80,1152]{1,0:T(8,128)(2,1)S(1)}, u32[]{:S(2)}, u32[]{:S(2)}) collective-permute-start(bf16[80,1152]{1,0:T(8,128)(2,1)S(1)} %pad_maximum_fusion.13), channel_id=1, source_target_pairs={{0,192},{32,224},{64,0},{96,32},{128,64},{160,96},{192,128},{224,1... | collective-permute-start | bytes 552968 | tf_op jit(solution)/shard_map/ppermute | solution.py:26
  69.5 13.5 %collective-permute-start.21 = (bf16[80,1152]{1,0:T(8,128)(2,1)S(1)}, bf16[80,1152]{1,0:T(8,128)(2,1)S(1)}, u32[]{:S(2)}, u32[]{:S(2)}) collective-permute-start(bf16[80,1152]{1,0:T(8,128)(2,1)S(1)} %concatenate.70), channel_id=1, source_target_pairs={{0,64},{32,96},{64,128},{96,160},{128,192},{160,224},{192,0},{224,... | collective-permute-start | bytes 552968 | tf_op jit(solution)/shard_map/ppermute | solution.py:26
  83.2 9.4 %collective-permute-start.22 = (bf16[40,1152]{1,0:T(8,128)(2,1)S(1)}, bf16[40,1152]{1,0:T(8,128)(2,1)S(1)}, u32[]{:S(2)}, u32[]{:S(2)}) collective-permute-start(bf16[40,1152]{1,0:T(8,128)(2,1)S(1)} %get-tuple-element.36), channel_id=1, source_target_pairs={{0,64},{32,96},{64,128},{96,160},{128,192},{160,224},{192,0},{224,... | collective-permute-start | bytes 276488 | tf_op jit(solution)/shard_map/ppermute | solution.py:26
  84.2 8.3 %collective-permute-start.23 = (bf16[40,1152]{1,0:T(8,128)(2,1)S(1)}, bf16[40,1152]{1,0:T(8,128)(2,1)S(1)}, u32[]{:S(2)}, u32[]{:S(2)}) collective-permute-start(bf16[40,1152]{1,0:T(8,128)(2,1)S(1)} %get-tuple-element.37), channel_id=1, source_target_pairs={{0,32},{32,64},{64,96},{96,128},{128,160},{160,192},{192,224},{224... | collective-permute-start | bytes 276488 | tf_op jit(solution)/shard_map/ppermute | solution.py:26
  84.6 8.0 %collective-permute-start.24 = (bf16[40,1152]{1,0:T(8,128)(2,1)S(1)}, bf16[40,1152]{1,0:T(8,128)(2,1)S(1)}, u32[]{:S(2)}, u32[]{:S(2)}) collective-permute-start(bf16[40,1152]{1,0:T(8,128)(2,1)S(1)} %get-tuple-element.40), channel_id=1, source_target_pairs={{0,224},{32,0},{64,32},{96,64},{128,96},{160,128},{192,160},{224,1... | collective-permute-start | bytes 276488 | tf_op jit(solution)/shard_map/ppermute | solution.py:26
  94.5 12.0 %all-to-all-start.2 = ((bf16[8,200,128]{2,1,0:T(8,128)(2,1)}), bf16[8,200,128]{2,1,0:T(8,128)(2,1)S(1)}, u32[]{:S(2)}, u32[]{:S(2)}) async-start(bf16[8,200,128]{2,1,0:T(8,128)(2,1)} %bitcast.20), calls=%async_computation.2 | async-start | bytes 819200 | tf_op jit(solution)/shard_map/all_to_all | solution.py:18
  108.1 7.3 %collective-permute-start.30 = (bf16[144,640]{1,0:T(8,128)(2,1)S(1)}, bf16[144,640]{1,0:T(8,128)(2,1)S(1)}, u32[]{:S(2)}, u32[]{:S(2)}) collective-permute-start(bf16[144,640]{1,0:T(8,128)(2,1)S(1)} %get-tuple-element.39), channel_id=1, source_target_pairs={{0,4},{4,8},{8,12},{12,0},{1,5},{5,9},{9,13},{13,1},{2,6},{6,10},{... | collective-permute-start | bytes 552968 | tf_op jit(solution)/shard_map/ppermute | solution.py:26
  109.7 9.4 %collective-permute-start.29 = (bf16[144,640]{1,0:T(8,128)(2,1)S(1)}, bf16[144,640]{1,0:T(8,128)(2,1)S(1)}, u32[]{:S(2)}, u32[]{:S(2)}) collective-permute-start(bf16[144,640]{1,0:T(8,128)(2,1)S(1)} %get-tuple-element.38), channel_id=1, source_target_pairs={{0,12},{4,0},{8,4},{12,8},{1,13},{5,1},{9,5},{13,9},{2,14},{6,2},{... | collective-permute-start | bytes 552968 | tf_op jit(solution)/shard_map/ppermute | solution.py:26
  112.3 16.1 %collective-permute-start.25 = (bf16[2,160,288]{2,1,0:T(8,128)(2,1)S(1)}, bf16[2,160,288]{2,1,0:T(8,128)(2,1)S(1)}, u32[]{:S(2)}, u32[]{:S(2)}) collective-permute-start(bf16[2,160,288]{2,1,0:T(8,128)(2,1)S(1)} %pad_maximum_fusion.10), channel_id=1, source_target_pairs={{0,1},{1,0},{2,3},{3,2},{4,5},{5,4},{6,7},{7,6},{8,9},{9,8},{10,11... | collective-permute-start | bytes 552968 | tf_op jit(solution)/shard_map/ppermute | solution.py:31
  115.5 6.8 %collective-permute-start.31 = (bf16[144,640]{1,0:T(8,128)(2,1)S(1)}, bf16[144,640]{1,0:T(8,128)(2,1)S(1)}, u32[]{:S(2)}, u32[]{:S(2)}) collective-permute-start(bf16[144,640]{1,0:T(8,128)(2,1)S(1)} %fusion.20), channel_id=1, source_target_pairs={{0,4},{4,8},{8,12},{12,0},{1,5},{5,9},{9,13},{13,1},{2,6},{6,10},{... | collective-permute-start | bytes 552968 | tf_op jit(solution)/shard_map/ppermute | solution.py:26
  115.9 12.5 %collective-permute-start.26 = (bf16[2,160,288]{2,1,0:T(8,128)(2,1)S(1)}, bf16[2,160,288]{2,1,0:T(8,128)(2,1)S(1)}, u32[]{:S(2)}, u32[]{:S(2)}) collective-permute-start(bf16[2,160,288]{2,1,0:T(8,128)(2,1)S(1)} %pad_maximum_fusion.11), channel_id=1, source_target_pairs={{0,2},{1,3},{2,0},{3,1},{4,6},{5,7},{6,4},{7,5},{8,10},{9,11},{10,... | collective-permute-start | bytes 552968 | tf_op jit(solution)/shard_map/ppermute | solution.py:31
  118.3 10.1 %collective-permute-start.27 = (bf16[2,160,288]{2,1,0:T(8,128)(2,1)S(1)}, bf16[2,160,288]{2,1,0:T(8,128)(2,1)S(1)}, u32[]{:S(2)}, u32[]{:S(2)}) collective-permute-start(bf16[2,160,288]{2,1,0:T(8,128)(2,1)S(1)} %pad_maximum_fusion.12), channel_id=1, source_target_pairs={{0,3},{1,2},{2,1},{3,0},{4,7},{5,6},{6,5},{7,4},{8,11},{9,10},{10,... | collective-permute-start | bytes 552968 | tf_op jit(solution)/shard_map/ppermute | solution.py:31
  123.2 15.8 %all-to-all-start.3 = ((bf16[8,18,640]{2,1,0:T(8,128)(2,1)}), bf16[8,18,640]{2,1,0:T(8,128)(2,1)S(1)}, u32[]{:S(2)}, u32[]{:S(2)}) async-start(bf16[8,18,640]{2,1,0:T(8,128)(2,1)} %reshape.151), calls=%async_computation.3 | async-start | bytes 491520 | tf_op jit(solution)/shard_map/all_to_all | solution.py:18
  (20 other events, 175.6 us)

commit v4 on v3

--- a/solution.py
+++ b/solution.py
@@ -26,40 +26,58 @@
     return lax.ppermute(x, axis, [(i, (i + step) % size) for i in range(size)])
 
 
+def apart(x):
+    pairs = [(2 * i + k, (i + 1 - 2 * k) % 8 * 2 + k) for i in range(8) for k in range(2)]
+    return lax.ppermute(x, ("z", "c"), pairs)
+
+
 def mp_shift(x, dx, dc):
     pairs = [(a * 2 + b, (a ^ dx) * 2 + (b ^ dc)) for a in range(2) for b in range(2)]
     return lax.ppermute(x, MP, pairs)
 
 
-def rows_from_slices(pair, xh, c):
-    quarters = pair.reshape(2, 2, 2, 40, 288)
+def mp_exchange(part, xh, c):
+    quarters = part.reshape(2, 2, 40, 288)
     got = {}
-    for dx in range(2):
-        for dc in range(2):
-            to = lax.dynamic_index_in_dim(quarters, xh ^ dx, 1, keepdims=False)
-            to = lax.dynamic_index_in_dim(to, c ^ dc, 1, keepdims=False)
-            got[dx, dc] = mp_shift(to, dx, dc) if dx or dc else to
+    for dx, dc in ((0, 0), (0, 1), (1, 0), (1, 1)):
+        to = lax.dynamic_index_in_dim(quarters, xh ^ dx, 0, keepdims=False)
+        to = lax.dynamic_index_in_dim(to, c ^ dc, 0, keepdims=False)
+        got[dx, dc] = mp_shift(to, dx, dc) if dx or dc else to
+    return got
+
+
+def embed(got, xh, c):
     parts = []
     for a in range(2):
         for b in range(2):
             near = jnp.where(c == b, got[0, 0], got[0, 1])
             far = jnp.where(c == b, got[1, 0], got[1, 1])
             parts.append(jnp.where(xh == a, near, far))
-    return jnp.concatenate(parts, axis=2)
+    rows = jnp.concatenate(parts, axis=1)
+    r = lax.rsqrt(jnp.sum(rows * rows, axis=1, keepdims=True) + 1e-06)
+    return (rows * r).astype(BF), r
 
 
 def block_kernel(scalars, place, img_in, *refs):
-    pieces = refs[:16]
-    to_oth, to_own, to_img, img, parts, texts, coef, coef_t, t_oth, t_own, g_img, sems, out_sems = refs[16:]
-    copies = [pltpu.make_async_copy(pieces[d], parts.at[d], sems.at[d]) for d in range(16)]
-    copies.append(pltpu.make_async_copy(img_in, img, sems.at[16]))
+    pieces = refs[:11]
+    to_oth, to_own, to_img, img, parts, texts, coef, coef_t, t_oth, t_own, g_img, sems, out_sems = refs[11:]
+    core = place[1]
+    far = 1 - core
+    slots = [parts.at[0, core], parts.at[0, far]]
+    slots += [parts.at[k + core * (8 - 2 * k)] for k in (1, 2, 3)] + [parts.at[4, core]]
+    slots += [parts.at[k + far * (8 - 2 * k)] for k in (1, 2)]
+    slots += [parts.at[3 + far * 2, 0], parts.at[3 + far * 2, 1], parts.at[4, far]]
+    copies = [pltpu.make_async_copy(pieces[d], slots[d], sems.at[d]) for d in range(11)]
+    copies.append(pltpu.make_async_copy(img_in, img, sems.at[11]))
     for copy in copies:
         copy.start()
-    for d in range(8):
-        copies[2 * d].wait()
-        copies[2 * d + 1].wait()
-        texts[80 * d : 80 * d + 80, :] = jnp.concatenate([parts[2 * d], parts[2 * d + 1]])
-    copies[16].wait()
+    for copy in copies:
+        copy.wait()
+    for side in range(2):
+        who = core if side else 1 - core
+        for d in range(4):
+            at = 320 * side + 80 * d
+            texts[at : at + 80, :] = jnp.concatenate([parts[2 * d, who], parts[2 * d + 1, who]])
     scale, offset = scalars[0], scalars[1]
     dots = lax.dot_general(img[...], texts[...], (((1,), (1,)), ((), ())), preferred_element_type=F32)
     rows = lax.broadcasted_iota(jnp.int32, (640, 640), 0) - place[0] * 40
@@ -98,18 +116,18 @@
             jax.ShapeDtypeStruct((320, 1152), F32),
             jax.ShapeDtypeStruct((640, 1152), BF),
         ],
-        in_specs=[small, small] + [large] * 17,
+        in_specs=[small, small] + [large] * 12,
         out_specs=[large] * 3,
         scratch_shapes=[
             pltpu.VMEM((640, 1152), BF),
-            pltpu.VMEM((16, 40, 1152), BF),
+            pltpu.VMEM((8, 2, 40, 1152), BF),
             pltpu.VMEM((640, 1152), BF),
             pltpu.VMEM((640, 640), BF),
             pltpu.VMEM((640, 640), BF),
             pltpu.VMEM((320, 1152), BF),
             pltpu.VMEM((320, 1152), F32),
             pltpu.VMEM((640, 1152), BF),
-            pltpu.SemaphoreType.DMA((17,)),
+            pltpu.SemaphoreType.DMA((12,)),
             pltpu.SemaphoreType.DMA((4,)),
         ],
         compiler_params=pltpu.CompilerParams(vmem_limit_bytes=60 * 2**20),
@@ -131,28 +149,29 @@
 
     keep = pick(xl, stacked)
     give = pick(1 - xl, lax.dynamic_slice_in_dim(stacked, c * 160, 160, 0))
-    own = rows_from_slices(jnp.stack([p_img, p_txt]), xh, c)
-    r = lax.rsqrt(jnp.sum(own * own, axis=2, keepdims=True) + 1e-06)
-    z = (own * r).astype(BF)
-    z, keep, give = lax.optimization_barrier((z, keep, give))
-    z_img, z_txt = z[0], z[1]
-    r_img, r_txt = r[0], r[1]
+    got_img = mp_exchange(p_img, xh, c)
+    got_img[0, 1], p_txt = lax.optimization_barrier((got_img[0, 1], p_txt))
+    got_txt = mp_exchange(p_txt, xh, c)
+    z_img, r_img = embed(got_img, xh, c)
+    z_txt, r_txt = embed(got_txt, xh, c)
+    z_txt, keep, give = lax.optimization_barrier((z_txt, keep, give))
 
     img = jnp.broadcast_to(z_img[None], (16, 40, 1152))
-    img, z_near = lax.optimization_barrier((img, z_txt))
+    z_near = z_txt
     img = a2a(img, PLANE).reshape(640, 1152)
-    up, down = [z_near], [z_near]
-    for d in range(3):
-        up.append(shift(up[-1], "z", 8, 1))
-        down.append(shift(down[-1], "z", 8, -1))
-    up.append(shift(up[-1], "z", 8, 1))
-    txt_own = up + down[:0:-1]
-    txt_oth = [swap_core(piece) for piece in txt_own]
+    z_far = swap_core(z_near)
+    carried = [jnp.stack([jnp.where(c == 0, z_near, z_far), jnp.where(c == 0, z_far, z_near)])]
+    for _ in range(3):
+        carried.append(apart(carried[-1]))
+    last, img = lax.optimization_barrier((carried[3], img))
+    mine = carried[1:] + [shift(z_near, "z", 8, 4)]
+    lower, upper = lax.optimization_barrier((swap_core(last[0]), last[1]))
+    pieces = [z_near, z_far] + mine + [swap_core(mine[0]), swap_core(mine[1]), lower, swap_core(upper), swap_core(mine[3])]
     give, img = lax.optimization_barrier((give, img))
     come = lax.ppermute(give, "xl", [(0, 1), (1, 0)])
-    place = (xl * 4 + y) * 2 + xh
+    place = jnp.stack([(xl * 4 + y) * 2 + xh, c]).astype(jnp.int32)
     scalars = jnp.concatenate([jnp.exp(log_scale), bias])
-    t_oth, t_own, g_img = block_grads(scalars, place.astype(jnp.int32).reshape(1), img, txt_oth + txt_own)
+    t_oth, t_own, g_img = block_grads(scalars, place, img, pieces)
     t_oth, come = lax.optimization_barrier((t_oth, come))
     t_got = swap_core(t_oth)
     come_oth = swap_core(come)
@@ -165,6 +184,7 @@
     to = {k: t_sum[40 * (-k % 8) : 40 * (-k % 8) + 40] for k in range(-3, 5)}
     far_up = shift(jnp.concatenate([to[4], to[3]]).astype(BF), "z", 8, 2).astype(F32)
     far_down = shift(jnp.concatenate([to[-3], to[-2]]).astype(BF), "z", 8, -2).astype(F32)
+    far_up, z_img, z_txt, r_img, r_txt = lax.optimization_barrier((far_up, z_img, z_txt, r_img, r_txt))
     near = [
         shift((to[2] + far_up[:40]).astype(BF), "z", 8, 2),
         shift((to[1] + far_up[40:]).astype(BF), "z", 8, 1),
@@ -175,11 +195,13 @@
     gz_img = jnp.sum(a2a(g_img, PLANE).astype(F32), axis=0)
 
     gz = jnp.stack([gz_img, gz_txt])
-    values = z.astype(F32)
+    r = jnp.stack([r_img, r_txt])
+    values = jnp.stack([z_img, z_txt]).astype(F32)
     inner = jnp.sum(values * gz, axis=2, keepdims=True)
     gp_rows = (r * (gz - values * inner)).astype(BF)
     cut = gp_rows.reshape(2, 40, 4, 288).transpose(2, 0, 1, 3)
-    rest = jnp.concatenate([cut[:, 0, :, 256:], cut[:, 1, :, 256:], jnp.zeros((4, 40, 64), BF)], axis=2)
+    rest = jnp.concatenate([cut[:, 0, :, 256:], cut[:, 1, :, 256:]], axis=2)
+    rest = jnp.concatenate([rest, rest], axis=2)
     piece = jnp.concatenate(
         [cut[:, :, :, :128].reshape(4, 80, 128), cut[:, :, :, 128:256].reshape(4, 80, 128), rest], axis=1
     )
@@ -190,13 +212,11 @@
         return jnp.einsum("rd,re->de", x, g, preferred_element_type=F32)
 
     lane = jnp.arange(128, dtype=jnp.int32)[None, :]
-    rest_img = jnp.where(lane < 32, rest, jnp.zeros_like(rest))
-    rest_txt = jnp.where(lane < 32, jnp.zeros_like(rest), rest)
     w = jnp.concatenate(
         [
             rows_dot(fi, jnp.concatenate([a_img, b_img], axis=1)),
             rows_dot(ft, jnp.concatenate([a_txt, b_txt], axis=1)),
-            rows_dot(fi, rest_img) + rows_dot(ft, rest_txt),
+            jnp.where(lane < 32, rows_dot(fi, rest), rows_dot(ft, rest)),
         ],
         axis=1,
     ).reshape(4, 144, 640)

time: 142 us -> 153 us (1.077)
  waiting for transfers between devices: 51.3 us -> 55.7 us
  other arithmetic: 7.41 us -> 11.2 us
  local copies, waits for them, and re-layouts: 6.57 us -> 10.2 us
    ppermute x0 -> x3, waiting for transfers between devices: none -> 14.9 us  [apart(): return lax.ppermute(x, ('z', 'c'), pairs)]
    ppermute x15 -> x9, waiting for transfers between devices: 30.2 us -> 19.2 us  [shift(): return lax.ppermute(x, axis, [(i, (i + step) % size) for i in range(size)])]
    ppermute x15 -> x9, starting transfers between devices: 23.3 us -> 19 us  [shift(): return lax.ppermute(x, axis, [(i, (i + step) % size) for i in range(size)])]
    ppermute x6 -> x9, starting transfers between devices: 5.28 us -> 8.74 us  [mp_shift(): return lax.ppermute(x, MP, pairs)]
    another operation x0 -> x4, local copies, waits for them, and re-layouts: none -> 2.72 us  [the longest x2 1.63 us: shards(): values = jnp.stack([z_img, z_txt]).astype(F32)]
    ppermute x0 -> x3, starting transfers between devices: none -> 1.98 us  [apart(): return lax.ppermute(x, ('z', 'c'), pairs)]
    ppermute x6 -> x9, waiting for transfers between devices: 3.97 us -> 4.15 us  [mp_shift(): return lax.ppermute(x, MP, pairs)]
  transfers between devices with their start and end apart: 36 -> 34, of which waited for: 14 -> 17; matrix products, arithmetic and copies ran while one was open for 8% -> 11% of each run, Pallas kernels for 5% -> 5%
where the time goes in v4:
time: 153 us; the launch traced here: 151 us
  waiting for transfers between devices  55.7 us (36%)
  starting transfers between devices  55.2 us (36%)
  other arithmetic  11.2 us (7%)
  local copies, waits for them, and re-layouts  10.2 us (7%)
  matrix products  8.84 us (6%)
  Pallas kernels  7.69 us (5%)
  between operations  2.61 us (2%)
    all_to_all x4, starting transfers between devices, a2a(): return lax.all_to_all(x, axes, 0, 0, tiled=True)  23.6 us
    ppermute x9, waiting for transfers between devices, shift(): return lax.ppermute(x, axis, [(i, (i + step) % size) for i in range(size)])  19.2 us
    ppermute x9, starting transfers between devices, shift(): return lax.ppermute(x, axis, [(i, (i + step) % size) for i in range(size)])  19 us
    all_to_all x4, waiting for transfers between devices, a2a(): return lax.all_to_all(x, axes, 0, 0, tiled=True)  15.8 us
    ppermute x3, waiting for transfers between devices, apart(): return lax.ppermute(x, ('z', 'c'), pairs)  14.9 us
    ppermute x9, starting transfers between devices, mp_shift(): return lax.ppermute(x, MP, pairs)  8.74 us
    pallas_call x1, Pallas kernels, block_grads(): pl.pallas_call(block_kernel, out_shape=[jax.ShapeDtypeStruct((320, 1152),...  7.69 us
    ppermute x9, waiting for transfers between devices, mp_shift(): return lax.ppermute(x, MP, pairs)  4.15 us
  transfers between devices with their start and end apart: 34, of which 17 were waited for; matrix products, arithmetic and copies ran while one was open for 11% of the time, Pallas kernels for 5%

profile of v4, /device:TPU:2, one launch (start us, length us, event | category | flops | bytes accessed | tf_op | source)
XLA Modules:
  0.0 151.4 jit_solution(9514967658282440766)
XLA Ops:
  1.7 1.4 fusion.93
  3.8 2.1 %collective-permute-start.8 = (f32[40,288]{1,0:T(8,128)}, f32[40,288]{1,0:T(8,128)S(1)}, u32[]{:S(2)}, u32[]{:S(2)}) collective-permute-start(f32[40,288]{1,0:T(8,128)} %get-tuple-element.92), channel_id=1, source_target_pairs={{0,2},{1,3},{2,0},{3,1},{4,6},{5,7},{6,4},{7,5},{8,10},{9,11},{10,... | collective-permute-start | bytes 138248 | tf_op jit(solution)/shard_map/ppermute | solution.py:36
  7.7 1.6 %fusion.4 = bf16[320,576]{1,0:T(8,128)(2,1)} fusion(bf16[320,1152]{1,0:T(8,128)(2,1)S(1)} %constant_dynamic-update-slice_fusion, s32[576]{0:T(1024)S(1)} %get-tuple-element.112), kind=kOutput, calls=%fused_computation.9 | convolution fusion | flops 425521152 | bytes 1108224 | tf_op jit(solution)/shard_map/dot_general | solution.py:148
  9.8 2.1 %collective-permute-start.2 = (f32[40,288]{1,0:T(8,128)S(1)}, f32[40,288]{1,0:T(8,128)S(1)}, u32[]{:S(2)}, u32[]{:S(2)}) collective-permute-start(f32[40,288]{1,0:T(8,128)S(1)} %get-tuple-element.96), channel_id=1, source_target_pairs={{0,2},{1,3},{2,0},{3,1},{4,6},{5,7},{6,4},{7,5},{8,10},{9,11},{10,... | collective-permute-start | bytes 138248 | tf_op jit(solution)/shard_map/ppermute | solution.py:36
  12.8 1.4 fusion.5
  15.5 2.1 %collective-permute-done.3 = f32[40,288]{1,0:T(8,128)S(1)} collective-permute-done((f32[40,288]{1,0:T(8,128)S(1)}, f32[40,288]{1,0:T(8,128)S(1)}, u32[]{:S(2)}, u32[]{:S(2)}) %collective-permute-start.3) | collective-permute-done | bytes 46112 | tf_op jit(solution)/shard_map/ppermute | solution.py:36
  19.2 6.5 %all-to-all-start = ((bf16[16,40,1152]{2,1,0:T(8,128)(2,1)}), bf16[16,40,1152]{2,1,0:T(8,128)(2,1)S(1)}, u32[]{:S(2)}, u32[]{:S(2)}) async-start(bf16[16,40,1152]{2,1,0:T(8,128)(2,1)} %broadcast_in_dim.9), calls=%async_computation | async-start | bytes 2949120 | tf_op jit(solution)/shard_map/all_to_all | solution.py:18
  27.6 2.0 %collective-permute-start.5 = (bf16[2,40,1152]{2,1,0:T(8,128)(2,1)S(1)}, bf16[2,40,1152]{2,1,0:T(8,128)(2,1)S(1)}, u32[]{:S(2)}, u32[]{:S(2)}) collective-permute-start(bf16[2,40,1152]{2,1,0:T(8,128)(2,1)S(1)} %pad_maximum_fusion.11), channel_id=1, source_target_pairs={{0,32},{1,225},{32,64},{33,1},{64,96},{65,33},{96,128},{97,65},{12... | collective-permute-start | bytes 552968 | tf_op jit(solution)/shard_map/ppermute | solution.py:31
  29.6 7.5 %collective-permute-done.5.refs_2_ = bf16[2,40,1152]{2,1,0:T(8,128)(2,1)S(1)} collective-permute-done((bf16[2,40,1152]{2,1,0:T(8,128)(2,1)S(1)}, bf16[2,40,1152]{2,1,0:T(8,128)(2,1)S(1)}, u32[]{:S(2)}, u32[]{:S(2)}) %collective-permute-start.5) | collective-permute-done | bytes 184352 | tf_op jit(solution)/shard_map/ppermute | solution.py:31
  37.0 6.7 %collective-permute-done.6.refs_3_ = bf16[2,40,1152]{2,1,0:T(8,128)(2,1)S(1)} collective-permute-done((bf16[2,40,1152]{2,1,0:T(8,128)(2,1)S(1)}, bf16[2,40,1152]{2,1,0:T(8,128)(2,1)S(1)}, u32[]{:S(2)}, u32[]{:S(2)}) %collective-permute-start.6) | collective-permute-done | bytes 184352 | tf_op jit(solution)/shard_map/ppermute | solution.py:31
  45.1 4.7 %collective-permute-start.10 = (bf16[40,1152]{1,0:T(8,128)(2,1)S(1)}, bf16[40,1152]{1,0:T(8,128)(2,1)}, u32[]{:S(2)}, u32[]{:S(2)}) collective-permute-start(bf16[40,1152]{1,0:T(8,128)(2,1)S(1)} %multiply_convert_fusion.1.refs_0_), channel_id=1, source_target_pairs={{0,128},{32,160},{64,192},{96,224},{128,0},{160,32},{192,64},{224,... | collective-permute-start | bytes 276488 | tf_op jit(solution)/shard_map/ppermute | solution.py:26
  51.9 3.1 %collective-permute-done.10.refs_5_ = bf16[40,1152]{1,0:T(8,128)(2,1)} collective-permute-done((bf16[40,1152]{1,0:T(8,128)(2,1)S(1)}, bf16[40,1152]{1,0:T(8,128)(2,1)}, u32[]{:S(2)}, u32[]{:S(2)}) %collective-permute-start.10) | collective-permute-done | bytes 92192 | tf_op jit(solution)/shard_map/ppermute | solution.py:26
  57.8 7.7 %shard_map.93 = (bf16[320,1152]{1,0:T(8,128)(2,1)}, f32[320,1152]{1,0:T(8,128)}, bf16[640,1152]{1,0:T(8,128)(2,1)}) custom-call(f32[2]{0:T(128)} %pad_maximum_fusion.18.scalars, s32[2]{0:T(128)} %pad_add_fusion.place, bf16[640,1152]{1,0:T(8,128)(2,1)} %bitcast.126, bf16[40,1152]{1,0:T(8,128)(2,1)} %copy-done.6, bf16[40,1152]{1,0:T(8,128)(2,1)} %copy-done.14, ...), custom_call_target="tpu_custom_call" | custom-call | flops 2900000000 | bytes 8000000 | tf_op jit(solution)/shard_map/pallas_call | solution.py:112
  66.2 8.0 %all-to-all-start.1 = ((bf16[16,40,1152]{2,1,0:T(8,128)(2,1)}), bf16[16,40,1152]{2,1,0:T(8,128)(2,1)S(1)}, u32[]{:S(2)}, u32[]{:S(2)}) async-start(bf16[16,40,1152]{2,1,0:T(8,128)(2,1)} %bitcast.125), calls=%async_computation.1 | async-start | bytes 2949120 | tf_op jit(solution)/shard_map/all_to_all | solution.py:18
  75.3 1.6 %fusion.84 = (bf16[320,1152]{1,0:T(8,128)(2,1)S(1)}, f32[320,1152]{1,0:T(8,128)S(1)}) fusion(f32[320,1152]{1,0:T(8,128)} %get-tuple-element.38, bf16[320,1152]{1,0:T(8,128)(2,1)S(1)} %collective-permute-done.17), kind=kLoop, calls=%fused_computation.182 | loop fusion | flops 1105920 | bytes 4423680 | tf_op jit(solution)/shard_map/convert.16
  77.0 2.8 %collective-permute-start.18 = (bf16[80,1152]{1,0:T(8,128)(2,1)S(1)}, bf16[80,1152]{1,0:T(8,128)(2,1)S(1)}, u32[]{:S(2)}, u32[]{:S(2)}) collective-permute-start(bf16[80,1152]{1,0:T(8,128)(2,1)S(1)} %concatenate.81), channel_id=1, source_target_pairs={{0,64},{32,96},{64,128},{96,160},{128,192},{160,224},{192,0},{224,... | collective-permute-start | bytes 552968 | tf_op jit(solution)/shard_map/ppermute | solution.py:26
  79.8 1.5 collective-permute-start.19
  81.5 6.1 %collective-permute-done.18 = bf16[80,1152]{1,0:T(8,128)(2,1)S(1)} collective-permute-done((bf16[80,1152]{1,0:T(8,128)(2,1)S(1)}, bf16[80,1152]{1,0:T(8,128)(2,1)S(1)}, u32[]{:S(2)}, u32[]{:S(2)}) %collective-permute-start.18) | collective-permute-done | bytes 184352 | tf_op jit(solution)/shard_map/ppermute | solution.py:26
  87.6 2.9 %collective-permute-done.19 = bf16[80,1152]{1,0:T(8,128)(2,1)S(1)} collective-permute-done((bf16[80,1152]{1,0:T(8,128)(2,1)S(1)}, bf16[80,1152]{1,0:T(8,128)(2,1)S(1)}, u32[]{:S(2)}, u32[]{:S(2)}) %collective-permute-start.19) | collective-permute-done | bytes 184352 | tf_op jit(solution)/shard_map/ppermute | solution.py:26
  91.3 3.1 %collective-permute-start.20 = (bf16[40,1152]{1,0:T(8,128)(2,1)}, bf16[40,1152]{1,0:T(8,128)(2,1)}, u32[]{:S(2)}, u32[]{:S(2)}) collective-permute-start(bf16[40,1152]{1,0:T(8,128)(2,1)} %get-tuple-element.52), channel_id=1, source_target_pairs={{0,64},{32,96},{64,128},{96,160},{128,192},{160,224},{192,0},{224,... | collective-permute-start | bytes 276488 | tf_op jit(solution)/shard_map/ppermute | solution.py:26
  94.4 3.2 %collective-permute-start.22 = (bf16[40,1152]{1,0:T(8,128)(2,1)}, bf16[40,1152]{1,0:T(8,128)(2,1)}, u32[]{:S(2)}, u32[]{:S(2)}) collective-permute-start(bf16[40,1152]{1,0:T(8,128)(2,1)} %get-tuple-element.56), channel_id=1, source_target_pairs={{0,224},{32,0},{64,32},{96,64},{128,96},{160,128},{192,160},{224,1... | collective-permute-start | bytes 276488 | tf_op jit(solution)/shard_map/ppermute | solution.py:26
  99.3 1.4 collective-permute-done.21
  104.3 1.3 fusion.24
  106.8 4.8 %all-to-all-start.2 = ((bf16[8,200,128]{2,1,0:T(8,128)(2,1)}), bf16[8,200,128]{2,1,0:T(8,128)(2,1)S(1)}, u32[]{:S(2)}, u32[]{:S(2)}) async-start(bf16[8,200,128]{2,1,0:T(8,128)(2,1)} %bitcast.32), calls=%async_computation.2 | async-start | bytes 819200 | tf_op jit(solution)/shard_map/all_to_all | solution.py:18
  111.6 7.0 %all-to-all-done.2 = bf16[8,200,128]{2,1,0:T(8,128)(2,1)S(1)} async-done(((bf16[8,200,128]{2,1,0:T(8,128)(2,1)}), bf16[8,200,128]{2,1,0:T(8,128)(2,1)S(1)}, u32[]{:S(2)}, u32[]{:S(2)}) %all-to-all-start.2) | async-done | bytes 409632 | tf_op jit(solution)/shard_map/all_to_all | solution.py:18
  120.2 1.5 %collective-permute-start.28 = (bf16[144,640]{1,0:T(8,128)(2,1)S(1)}, bf16[144,640]{1,0:T(8,128)(2,1)S(1)}, u32[]{:S(2)}, u32[]{:S(2)}) collective-permute-start(bf16[144,640]{1,0:T(8,128)(2,1)S(1)} %get-tuple-element.55), channel_id=1, source_target_pairs={{0,4},{4,8},{8,12},{12,0},{1,5},{5,9},{9,13},{13,1},{2,6},{6,10},{... | collective-permute-start | bytes 552968 | tf_op jit(solution)/shard_map/ppermute | solution.py:26
  121.8 1.8 %collective-permute-start.27 = (bf16[144,640]{1,0:T(8,128)(2,1)S(1)}, bf16[144,640]{1,0:T(8,128)(2,1)S(1)}, u32[]{:S(2)}, u32[]{:S(2)}) collective-permute-start(bf16[144,640]{1,0:T(8,128)(2,1)S(1)} %get-tuple-element.54), channel_id=1, source_target_pairs={{0,12},{4,0},{8,4},{12,8},{1,13},{5,1},{9,5},{13,9},{2,14},{6,2},{... | collective-permute-start | bytes 552968 | tf_op jit(solution)/shard_map/ppermute | solution.py:26
  125.2 2.4 %collective-permute-done.28 = bf16[144,640]{1,0:T(8,128)(2,1)S(1)} collective-permute-done((bf16[144,640]{1,0:T(8,128)(2,1)S(1)}, bf16[144,640]{1,0:T(8,128)(2,1)S(1)}, u32[]{:S(2)}, u32[]{:S(2)}) %collective-permute-start.28) | collective-permute-done | bytes 184352 | tf_op jit(solution)/shard_map/ppermute | solution.py:26
  128.0 1.7 %collective-permute-start.24 = (bf16[2,160,288]{2,1,0:T(8,128)(2,1)S(1)}, bf16[2,160,288]{2,1,0:T(8,128)(2,1)S(1)}, u32[]{:S(2)}, u32[]{:S(2)}) collective-permute-start(bf16[2,160,288]{2,1,0:T(8,128)(2,1)S(1)} %pad_maximum_fusion.9), channel_id=1, source_target_pairs={{0,2},{1,3},{2,0},{3,1},{4,6},{5,7},{6,4},{7,5},{8,10},{9,11},{10,... | collective-permute-start | bytes 552968 | tf_op jit(solution)/shard_map/ppermute | solution.py:36
  131.2 3.2 %collective-permute-done.29 = bf16[144,640]{1,0:T(8,128)(2,1)S(1)} collective-permute-done((bf16[144,640]{1,0:T(8,128)(2,1)S(1)}, bf16[144,640]{1,0:T(8,128)(2,1)S(1)}, u32[]{:S(2)}, u32[]{:S(2)}) %collective-permute-start.29) | collective-permute-done | bytes 184352 | tf_op jit(solution)/shard_map/ppermute | solution.py:26
  135.2 4.3 %all-to-all-start.3 = ((bf16[8,18,640]{2,1,0:T(8,128)(2,1)}), bf16[8,18,640]{2,1,0:T(8,128)(2,1)S(1)}, u32[]{:S(2)}, u32[]{:S(2)}) async-start(bf16[8,18,640]{2,1,0:T(8,128)(2,1)} %reshape.229), calls=%async_computation.3 | async-start | bytes 491520 | tf_op jit(solution)/shard_map/all_to_all | solution.py:18
  141.3 8.8 %all-to-all-done.3 = bf16[8,18,640]{2,1,0:T(8,128)(2,1)S(1)} async-done(((bf16[8,18,640]{2,1,0:T(8,128)(2,1)}), bf16[8,18,640]{2,1,0:T(8,128)(2,1)S(1)}, u32[]{:S(2)}, u32[]{:S(2)}) %all-to-all-start.3) | async-done | bytes 184352 | tf_op jit(solution)/shard_map/all_to_all | solution.py:18
  (157 shorter events, 32.4 us)
Async XLA Ops:
  3.8 5.6 %collective-permute-start = (f32[40,288]{1,0:T(8,128)}, f32[40,288]{1,0:T(8,128)S(1)}, u32[]{:S(2)}, u32[]{:S(2)}) collective-permute-start(f32[40,288]{1,0:T(8,128)} %get-tuple-element.93), channel_id=1, source_target_pairs={{0,1},{1,0},{2,3},{3,2},{4,5},{5,4},{6,7},{7,6},{8,9},{9,8},{10,11... | collective-permute-start | bytes 138248 | tf_op jit(solution)/shard_map/ppermute | solution.py:36
  3.8 10.4 %collective-permute-start.8 = (f32[40,288]{1,0:T(8,128)}, f32[40,288]{1,0:T(8,128)S(1)}, u32[]{:S(2)}, u32[]{:S(2)}) collective-permute-start(f32[40,288]{1,0:T(8,128)} %get-tuple-element.92), channel_id=1, source_target_pairs={{0,2},{1,3},{2,0},{3,1},{4,6},{5,7},{6,4},{7,5},{8,10},{9,11},{10,... | collective-permute-start | bytes 138248 | tf_op jit(solution)/shard_map/ppermute | solution.py:36
  5.9 8.3 %collective-permute-start.9 = (f32[40,288]{1,0:T(8,128)S(1)}, f32[40,288]{1,0:T(8,128)S(1)}, u32[]{:S(2)}, u32[]{:S(2)}) collective-permute-start(f32[40,288]{1,0:T(8,128)S(1)} %get-tuple-element.91), channel_id=1, source_target_pairs={{0,3},{1,2},{2,1},{3,0},{4,7},{5,6},{6,5},{7,4},{8,11},{9,10},{10,... | collective-permute-start | bytes 138248 | tf_op jit(solution)/shard_map/ppermute | solution.py:36
  9.4 4.9 %collective-permute-start.1 = (f32[40,288]{1,0:T(8,128)S(1)}, f32[40,288]{1,0:T(8,128)S(1)}, u32[]{:S(2)}, u32[]{:S(2)}) collective-permute-start(f32[40,288]{1,0:T(8,128)S(1)} %get-tuple-element.94), channel_id=1, source_target_pairs={{0,1},{1,0},{2,3},{3,2},{4,5},{5,4},{6,7},{7,6},{8,9},{9,8},{10,11... | collective-permute-start | bytes 138248 | tf_op jit(solution)/shard_map/ppermute | solution.py:36
  9.8 5.7 %collective-permute-start.2 = (f32[40,288]{1,0:T(8,128)S(1)}, f32[40,288]{1,0:T(8,128)S(1)}, u32[]{:S(2)}, u32[]{:S(2)}) collective-permute-start(f32[40,288]{1,0:T(8,128)S(1)} %get-tuple-element.96), channel_id=1, source_target_pairs={{0,2},{1,3},{2,0},{3,1},{4,6},{5,7},{6,4},{7,5},{8,10},{9,11},{10,... | collective-permute-start | bytes 138248 | tf_op jit(solution)/shard_map/ppermute | solution.py:36
  11.9 5.7 %collective-permute-start.3 = (f32[40,288]{1,0:T(8,128)S(1)}, f32[40,288]{1,0:T(8,128)S(1)}, u32[]{:S(2)}, u32[]{:S(2)}) collective-permute-start(f32[40,288]{1,0:T(8,128)S(1)} %get-tuple-element.95), channel_id=1, source_target_pairs={{0,3},{1,2},{2,1},{3,0},{4,7},{5,6},{6,5},{7,4},{8,11},{9,10},{10,... | collective-permute-start | bytes 138248 | tf_op jit(solution)/shard_map/ppermute | solution.py:36
  19.2 31.8 %all-to-all-start = ((bf16[16,40,1152]{2,1,0:T(8,128)(2,1)}), bf16[16,40,1152]{2,1,0:T(8,128)(2,1)S(1)}, u32[]{:S(2)}, u32[]{:S(2)}) async-start(bf16[16,40,1152]{2,1,0:T(8,128)(2,1)} %broadcast_in_dim.9), calls=%async_computation | async-start | bytes 2949120 | tf_op jit(solution)/shard_map/all_to_all | solution.py:18
  27.6 9.4 %collective-permute-start.5 = (bf16[2,40,1152]{2,1,0:T(8,128)(2,1)S(1)}, bf16[2,40,1152]{2,1,0:T(8,128)(2,1)S(1)}, u32[]{:S(2)}, u32[]{:S(2)}) collective-permute-start(bf16[2,40,1152]{2,1,0:T(8,128)(2,1)S(1)} %pad_maximum_fusion.11), channel_id=1, source_target_pairs={{0,32},{1,225},{32,64},{33,1},{64,96},{65,33},{96,128},{97,65},{12... | collective-permute-start | bytes 552968 | tf_op jit(solution)/shard_map/ppermute | solution.py:31
  37.0 6.7 %collective-permute-start.6 = (bf16[2,40,1152]{2,1,0:T(8,128)(2,1)S(1)}, bf16[2,40,1152]{2,1,0:T(8,128)(2,1)S(1)}, u32[]{:S(2)}, u32[]{:S(2)}) collective-permute-start(bf16[2,40,1152]{2,1,0:T(8,128)(2,1)S(1)} %collective-permute-done.5.refs_2_), channel_id=1, source_target_pairs={{0,32},{1,225},{32,64},{33,1},{64,96},{65,33},{96,128},{97,65},{12... | collective-permute-start | bytes 552968 | tf_op jit(solution)/shard_map/ppermute | solution.py:31
  43.8 7.2 %collective-permute-start.7 = (bf16[2,40,1152]{2,1,0:T(8,128)(2,1)S(1)}, bf16[2,40,1152]{2,1,0:T(8,128)(2,1)S(1)}, u32[]{:S(2)}, u32[]{:S(2)}) collective-permute-start(bf16[2,40,1152]{2,1,0:T(8,128)(2,1)S(1)} %collective-permute-done.6.refs_3_), channel_id=1, source_target_pairs={{0,32},{1,225},{32,64},{33,1},{64,96},{65,33},{96,128},{97,65},{12... | collective-permute-start | bytes 552968 | tf_op jit(solution)/shard_map/ppermute | solution.py:31
  45.1 9.9 %collective-permute-start.10 = (bf16[40,1152]{1,0:T(8,128)(2,1)S(1)}, bf16[40,1152]{1,0:T(8,128)(2,1)}, u32[]{:S(2)}, u32[]{:S(2)}) collective-permute-start(bf16[40,1152]{1,0:T(8,128)(2,1)S(1)} %multiply_convert_fusion.1.refs_0_), channel_id=1, source_target_pairs={{0,128},{32,160},{64,192},{96,224},{128,0},{160,32},{192,64},{224,... | collective-permute-start | bytes 276488 | tf_op jit(solution)/shard_map/ppermute | solution.py:26
  49.8 6.8 %collective-permute-start.11 = (bf16[2,40,1152]{2,1,0:T(8,128)(2,1)S(1)}, bf16[2,40,1152]{2,1,0:T(8,128)(2,1)}, u32[]{:S(2)}, u32[]{:S(2)}) collective-permute-start(bf16[2,40,1152]{2,1,0:T(8,128)(2,1)S(1)} %collective-permute-done.5.refs_2_), channel_id=1, source_target_pairs={{0,1},{1,0},{2,3},{3,2},{4,5},{5,4},{6,7},{7,6},{8,9},{9,8},{10,11... | collective-permute-start | bytes 552968 | tf_op jit(solution)/shard_map/ppermute | solution.py:22
  49.8 6.8 %collective-permute-start.12 = (bf16[2,40,1152]{2,1,0:T(8,128)(2,1)S(1)}, bf16[2,40,1152]{2,1,0:T(8,128)(2,1)}, u32[]{:S(2)}, u32[]{:S(2)}) collective-permute-start(bf16[2,40,1152]{2,1,0:T(8,128)(2,1)S(1)} %collective-permute-done.6.refs_3_), channel_id=1, source_target_pairs={{0,1},{1,0},{2,3},{3,2},{4,5},{5,4},{6,7},{7,6},{8,9},{9,8},{10,11... | collective-permute-start | bytes 552968 | tf_op jit(solution)/shard_map/ppermute | solution.py:22
  51.0 4.1 %collective-permute-start.13 = (bf16[40,1152]{1,0:T(8,128)(2,1)S(1)}, bf16[40,1152]{1,0:T(8,128)(2,1)S(1)}, u32[]{:S(2)}, u32[]{:S(2)}) collective-permute-start(bf16[40,1152]{1,0:T(8,128)(2,1)S(1)} %get-tuple-element.98), channel_id=1, source_target_pairs={{0,1},{1,0},{2,3},{3,2},{4,5},{5,4},{6,7},{7,6},{8,9},{9,8},{10,11... | collective-permute-start | bytes 276488 | tf_op jit(solution)/shard_map/ppermute | solution.py:22
  55.0 1.5 collective-permute-start.15
  56.1 9.4 %collective-permute-start.16 = (bf16[160,576]{1,0:T(8,128)(2,1)}, bf16[160,576]{1,0:T(8,128)(2,1)S(1)}, u32[]{:S(2)}, u32[]{:S(2)}) collective-permute-start(bf16[160,576]{1,0:T(8,128)(2,1)} %fusion.5), channel_id=1, source_target_pairs={{0,16},{16,0},{1,17},{17,1},{2,18},{18,2},{3,19},{19,3},{4,20},{20... | collective-permute-start | bytes 552968 | tf_op jit(solution)/shard_map/ppermute | solution.py:171
  65.5 9.8 %collective-permute-start.17 = (bf16[320,1152]{1,0:T(8,128)(2,1)}, bf16[320,1152]{1,0:T(8,128)(2,1)S(1)}, u32[]{:S(2)}, u32[]{:S(2)}) collective-permute-start(bf16[320,1152]{1,0:T(8,128)(2,1)} %get-tuple-element.41), channel_id=1, source_target_pairs={{0,1},{1,0},{2,3},{3,2},{4,5},{5,4},{6,7},{7,6},{8,9},{9,8},{10,11... | collective-permute-start | bytes 2211848 | tf_op jit(solution)/shard_map/ppermute | solution.py:22
  65.7 8.4 %collective-permute-start.26 = (bf16[160,576]{1,0:T(8,128)(2,1)S(1)}, bf16[160,576]{1,0:T(8,128)(2,1)}, u32[]{:S(2)}, u32[]{:S(2)}) collective-permute-start(bf16[160,576]{1,0:T(8,128)(2,1)S(1)} %collective-permute-done.16), channel_id=1, source_target_pairs={{0,1},{1,0},{2,3},{3,2},{4,5},{5,4},{6,7},{7,6},{8,9},{9,8},{10,11... | collective-permute-start | bytes 552968 | tf_op jit(solution)/shard_map/ppermute | solution.py:22
  66.2 36.6 %all-to-all-start.1 = ((bf16[16,40,1152]{2,1,0:T(8,128)(2,1)}), bf16[16,40,1152]{2,1,0:T(8,128)(2,1)S(1)}, u32[]{:S(2)}, u32[]{:S(2)}) async-start(bf16[16,40,1152]{2,1,0:T(8,128)(2,1)} %bitcast.125), calls=%async_computation.1 | async-start | bytes 2949120 | tf_op jit(solution)/shard_map/all_to_all | solution.py:18
  77.0 10.6 %collective-permute-start.18 = (bf16[80,1152]{1,0:T(8,128)(2,1)S(1)}, bf16[80,1152]{1,0:T(8,128)(2,1)S(1)}, u32[]{:S(2)}, u32[]{:S(2)}) collective-permute-start(bf16[80,1152]{1,0:T(8,128)(2,1)S(1)} %concatenate.81), channel_id=1, source_target_pairs={{0,64},{32,96},{64,128},{96,160},{128,192},{160,224},{192,0},{224,... | collective-permute-start | bytes 552968 | tf_op jit(solution)/shard_map/ppermute | solution.py:26
  79.8 10.7 %collective-permute-start.19 = (bf16[80,1152]{1,0:T(8,128)(2,1)S(1)}, bf16[80,1152]{1,0:T(8,128)(2,1)S(1)}, u32[]{:S(2)}, u32[]{:S(2)}) collective-permute-start(bf16[80,1152]{1,0:T(8,128)(2,1)S(1)} %pad_maximum_fusion.12), channel_id=1, source_target_pairs={{0,192},{32,224},{64,0},{96,32},{128,64},{160,96},{192,128},{224,1... | collective-permute-start | bytes 552968 | tf_op jit(solution)/shard_map/ppermute | solution.py:26
  91.3 8.0 %collective-permute-start.20 = (bf16[40,1152]{1,0:T(8,128)(2,1)}, bf16[40,1152]{1,0:T(8,128)(2,1)}, u32[]{:S(2)}, u32[]{:S(2)}) collective-permute-start(bf16[40,1152]{1,0:T(8,128)(2,1)} %get-tuple-element.52), channel_id=1, source_target_pairs={{0,64},{32,96},{64,128},{96,160},{128,192},{160,224},{192,0},{224,... | collective-permute-start | bytes 276488 | tf_op jit(solution)/shard_map/ppermute | solution.py:26
  94.4 6.3 %collective-permute-start.21 = (bf16[40,1152]{1,0:T(8,128)(2,1)}, bf16[40,1152]{1,0:T(8,128)(2,1)}, u32[]{:S(2)}, u32[]{:S(2)}) collective-permute-start(bf16[40,1152]{1,0:T(8,128)(2,1)} %get-tuple-element.53), channel_id=1, source_target_pairs={{0,32},{32,64},{64,96},{96,128},{128,160},{160,192},{192,224},{224... | collective-permute-start | bytes 276488 | tf_op jit(solution)/shard_map/ppermute | solution.py:26
  94.4 6.3 %collective-permute-start.22 = (bf16[40,1152]{1,0:T(8,128)(2,1)}, bf16[40,1152]{1,0:T(8,128)(2,1)}, u32[]{:S(2)}, u32[]{:S(2)}) collective-permute-start(bf16[40,1152]{1,0:T(8,128)(2,1)} %get-tuple-element.56), channel_id=1, source_target_pairs={{0,224},{32,0},{64,32},{96,64},{128,96},{160,128},{192,160},{224,1... | collective-permute-start | bytes 276488 | tf_op jit(solution)/shard_map/ppermute | solution.py:26
  106.8 11.9 %all-to-all-start.2 = ((bf16[8,200,128]{2,1,0:T(8,128)(2,1)}), bf16[8,200,128]{2,1,0:T(8,128)(2,1)S(1)}, u32[]{:S(2)}, u32[]{:S(2)}) async-start(bf16[8,200,128]{2,1,0:T(8,128)(2,1)} %bitcast.32), calls=%async_computation.2 | async-start | bytes 819200 | tf_op jit(solution)/shard_map/all_to_all | solution.py:18
  120.2 7.3 %collective-permute-start.28 = (bf16[144,640]{1,0:T(8,128)(2,1)S(1)}, bf16[144,640]{1,0:T(8,128)(2,1)S(1)}, u32[]{:S(2)}, u32[]{:S(2)}) collective-permute-start(bf16[144,640]{1,0:T(8,128)(2,1)S(1)} %get-tuple-element.55), channel_id=1, source_target_pairs={{0,4},{4,8},{8,12},{12,0},{1,5},{5,9},{9,13},{13,1},{2,6},{6,10},{... | collective-permute-start | bytes 552968 | tf_op jit(solution)/shard_map/ppermute | solution.py:26
  121.8 9.4 %collective-permute-start.27 = (bf16[144,640]{1,0:T(8,128)(2,1)S(1)}, bf16[144,640]{1,0:T(8,128)(2,1)S(1)}, u32[]{:S(2)}, u32[]{:S(2)}) collective-permute-start(bf16[144,640]{1,0:T(8,128)(2,1)S(1)} %get-tuple-element.54), channel_id=1, source_target_pairs={{0,12},{4,0},{8,4},{12,8},{1,13},{5,1},{9,5},{13,9},{2,14},{6,2},{... | collective-permute-start | bytes 552968 | tf_op jit(solution)/shard_map/ppermute | solution.py:26
  124.4 15.1 %collective-permute-start.23 = (bf16[2,160,288]{2,1,0:T(8,128)(2,1)S(1)}, bf16[2,160,288]{2,1,0:T(8,128)(2,1)S(1)}, u32[]{:S(2)}, u32[]{:S(2)}) collective-permute-start(bf16[2,160,288]{2,1,0:T(8,128)(2,1)S(1)} %pad_maximum_fusion.8), channel_id=1, source_target_pairs={{0,1},{1,0},{2,3},{3,2},{4,5},{5,4},{6,7},{7,6},{8,9},{9,8},{10,11... | collective-permute-start | bytes 552968 | tf_op jit(solution)/shard_map/ppermute | solution.py:36
  127.6 6.8 %collective-permute-start.29 = (bf16[144,640]{1,0:T(8,128)(2,1)S(1)}, bf16[144,640]{1,0:T(8,128)(2,1)S(1)}, u32[]{:S(2)}, u32[]{:S(2)}) collective-permute-start(bf16[144,640]{1,0:T(8,128)(2,1)S(1)} %fusion.17), channel_id=1, source_target_pairs={{0,4},{4,8},{8,12},{12,0},{1,5},{5,9},{9,13},{13,1},{2,6},{6,10},{... | collective-permute-start | bytes 552968 | tf_op jit(solution)/shard_map/ppermute | solution.py:26
  128.0 11.5 %collective-permute-start.24 = (bf16[2,160,288]{2,1,0:T(8,128)(2,1)S(1)}, bf16[2,160,288]{2,1,0:T(8,128)(2,1)S(1)}, u32[]{:S(2)}, u32[]{:S(2)}) collective-permute-start(bf16[2,160,288]{2,1,0:T(8,128)(2,1)S(1)} %pad_maximum_fusion.9), channel_id=1, source_target_pairs={{0,2},{1,3},{2,0},{3,1},{4,6},{5,7},{6,4},{7,5},{8,10},{9,11},{10,... | collective-permute-start | bytes 552968 | tf_op jit(solution)/shard_map/ppermute | solution.py:36
  130.4 9.9 %collective-permute-start.25 = (bf16[2,160,288]{2,1,0:T(8,128)(2,1)S(1)}, bf16[2,160,288]{2,1,0:T(8,128)(2,1)S(1)}, u32[]{:S(2)}, u32[]{:S(2)}) collective-permute-start(bf16[2,160,288]{2,1,0:T(8,128)(2,1)S(1)} %pad_maximum_fusion.10), channel_id=1, source_target_pairs={{0,3},{1,2},{2,1},{3,0},{4,7},{5,6},{6,5},{7,4},{8,11},{9,10},{10,... | collective-permute-start | bytes 552968 | tf_op jit(solution)/shard_map/ppermute | solution.py:36
  135.2 14.8 %all-to-all-start.3 = ((bf16[8,18,640]{2,1,0:T(8,128)(2,1)}), bf16[8,18,640]{2,1,0:T(8,128)(2,1)S(1)}, u32[]{:S(2)}, u32[]{:S(2)}) async-start(bf16[8,18,640]{2,1,0:T(8,128)(2,1)} %reshape.229), calls=%async_computation.3 | async-start | bytes 491520 | tf_op jit(solution)/shard_map/all_to_all | solution.py:18
  (22 other events, 253.1 us)
